TPU v7x, 32 devices: a whole 2x2x4 slice. The times are simulated.
32 devices in a mesh: seg: 8 (over y, x, core), tensor: 4 (over z).
Axes of the slice: x: 2, y: 2, z: 4, core: 2. Of those that a mesh axis runs over, the one named last changes fastest.
Arguments:
- tokens: bfloat16 [8704, 8192], P(('seg', 'tensor')), may hold values from -6 to 6
- memory_embed: bfloat16 [64, 8192], P('tensor'), may hold values from -6 to 6
- norm_gain: bfloat16 [8192], replicated, may hold values from 0.5 to 1.5
- w_query: bfloat16 [8192, 4096], P(None, 'tensor'), as said below
- w_key: bfloat16 [8192, 1024], P(None, 'tensor'), as said below
- value_weight: bfloat16 [8192, 1024], P(None, 'tensor'), may hold values from -0.0625 to 0.0625
- w_out: bfloat16 [4096, 8192], P('tensor'), may hold values from -0.09375 to 0.09375
- retain: float32 [8, 32], P('seg', 'tensor'), may hold values from 0.05 to 1
Outputs:
- output: bfloat16 [8704, 8192], P(('seg', 'tensor'))
Inputs may be any that keep to these rules, and one draw needn't show every extreme that they name: `w_query`: entries lie within 6 / sqrt(8192) of zero. `w_key`: entries lie within 6 / sqrt(8192) of zero.
All inputs are finite; a program needn't handle non-finite values.
Results may differ from a plain program's by a relative error of at most 0.007.
Values may be sent and summed in bfloat16 or wider, within the bound.
No kernel may reach another device: no remote copies, remote signals or barrier semaphores. Data moves between devices by JAX's collectives and lax.ppermute only.
A program may use at most 192 MiB of HBM per device.

v0:
```python
import jax
import jax.numpy as jnp
from jax import lax
from jax.sharding import PartitionSpec as P

HEAD_SIZE = 128


epsilon = 1e-05


def shifted(block, axis, distance):
    devices = range(lax.axis_size(axis))
    route = [(i - distance, i) for i in devices if i - distance in devices]
    return lax.ppermute(block, axis, route)


def rms_rows(rows, norm_gain):
    widened = rows.astype(jnp.float32)
    scale_rows = lax.rsqrt(jnp.mean(widened * widened, axis=-1, keepdims=True) + epsilon)
    return (widened * scale_rows * norm_gain.astype(jnp.float32)).astype(jnp.bfloat16)


def feature_map(inputs):
    return jax.nn.elu(inputs) + 1.0


def project_rows(rows, w_query, w_key, value_weight):
    return jnp.concatenate(
        [
            jnp.dot(rows, w_query, preferred_element_type=jnp.float32),
            jnp.dot(rows, w_key, preferred_element_type=jnp.float32),
            jnp.dot(rows, value_weight, preferred_element_type=jnp.float32),
        ],
        axis=1,
    )


def soft_part(queries, keys_all, values_all):
    count_rows = queries.shape[0]
    kv_heads = keys_all.shape[1] // HEAD_SIZE
    heads_query = queries.reshape(count_rows, kv_heads, -1, HEAD_SIZE)
    heads_key = keys_all.reshape(count_rows, kv_heads, HEAD_SIZE)
    heads_value = values_all.reshape(count_rows, kv_heads, HEAD_SIZE)
    block_count = 1
    for divisor in range(1, count_rows // 512 + 1):
        block_count = divisor
    block_rows = count_rows // block_count
    col_ids = lax.broadcasted_iota(jnp.int32, (block_rows, count_rows), 1)
    soft_blocks = []
    for block_index in range(block_count):
        first_row = block_index * block_rows
        block_query = heads_query[first_row : first_row + block_rows]
        scores = jnp.einsum(
            "rkgd,ckd->kgrc", block_query, heads_key, preferred_element_type=jnp.float32
        ) * HEAD_SIZE ** (-0.5)
        row_ids = lax.broadcasted_iota(jnp.int32, (block_rows, count_rows), 0) + first_row
        scores = jnp.where(row_ids >= col_ids, scores, -1e30)
        top_score = jnp.max(scores, axis=-1, keepdims=True)
        weights = jnp.exp(scores - top_score)
        attn_probs = (weights / jnp.sum(weights, axis=-1, keepdims=True)).astype(jnp.bfloat16)
        soft_blocks.append(
            jnp.einsum(
                "kgrc,ckd->rkgd", attn_probs, heads_value, preferred_element_type=jnp.float32
            )
        )
    soft = jnp.concatenate(soft_blocks, axis=0)
    return (
        soft,
        feature_map(heads_query.astype(jnp.float32)),
        feature_map(heads_key.astype(jnp.float32)),
    )


def write_terms(soft, feat_key, tok_rows):
    mem_soft = soft[tok_rows:]
    mem_key = feat_key[tok_rows:]
    kv_heads = mem_soft.shape[1]
    groups = mem_soft.shape[2]
    write_mat = jnp.einsum("mkd,mkge->kgde", mem_key, mem_soft, precision=lax.Precision.HIGHEST)
    write_sum = jnp.broadcast_to(
        jnp.sum(mem_key, axis=0)[:, None, :], (kv_heads, groups, HEAD_SIZE)
    )
    return (
        write_mat.reshape(kv_heads * groups, HEAD_SIZE, HEAD_SIZE),
        write_sum.reshape(kv_heads * groups, HEAD_SIZE),
    )


def read_terms(soft, feat_query, state_mat, state_sum, tok_rows):
    kv_heads = soft.shape[1]
    groups = soft.shape[2]
    state_four = state_mat.reshape(kv_heads, groups, HEAD_SIZE, HEAD_SIZE)
    sum_four = state_sum.reshape(kv_heads, groups, HEAD_SIZE)
    token_query = feat_query[:tok_rows]
    numerator = jnp.einsum(
        "tkgd,kgde->tkge", token_query, state_four, precision=lax.Precision.HIGHEST
    )
    denominator = (
        jnp.einsum("tkgd,kgd->tkg", token_query, sum_four, precision=lax.Precision.HIGHEST) + 1.0
    )
    mixed = soft[:tok_rows] + numerator / denominator[..., None]
    return mixed.reshape(tok_rows, -1).astype(jnp.bfloat16)


def per_device(tokens, memory_embed, norm_gain, w_query, w_key, value_weight, w_out, retain):
    tok_local = rms_rows(tokens, norm_gain)
    mem_local = rms_rows(memory_embed, norm_gain)
    local_tok = tok_local.shape[0]
    tensor_count = lax.axis_size("tensor")
    tok_all, mem_all = (
        lax.all_gather(tok_local, "tensor", axis=0, tiled=True),
        lax.all_gather(mem_local, "tensor", axis=0, tiled=True),
    )
    projected = jnp.concatenate(
        [
            project_rows(tok_all, w_query, w_key, value_weight),
            project_rows(mem_all, w_query, w_key, value_weight),
        ],
        axis=0,
    )
    query_cols = w_query.shape[1]
    key_cols = w_key.shape[1]
    queries = projected[:, :query_cols].astype(jnp.bfloat16)
    keys_all = projected[:, query_cols : query_cols + key_cols].astype(jnp.bfloat16)
    values_all = projected[:, query_cols + key_cols :].astype(jnp.bfloat16)
    tok_rows = tensor_count * local_tok
    soft, feat_query, feat_key = soft_part(queries, keys_all, values_all)
    write_mat, write_sum = write_terms(soft, feat_key, tok_rows)
    keep_rates = retain[0]
    empty_state = (jnp.zeros_like(write_mat), jnp.zeros_like(write_sum))

    def relay_turn(index_turn, state_pair):
        prior_mat, prior_sum = state_pair
        moved = (
            keep_rates[:, None, None] * prior_mat + write_mat,
            keep_rates[:, None] * prior_sum + write_sum,
        )
        return (
            shifted(moved[0].astype(jnp.bfloat16), "seg", 1).astype(jnp.float32),
            shifted(moved[1].astype(jnp.bfloat16), "seg", 1).astype(jnp.float32),
        )

    prefix_mat, prefix_sum = lax.fori_loop(0, lax.axis_size("seg") - 1, relay_turn, empty_state)
    mixed = read_terms(soft, feat_query, prefix_mat, prefix_sum, tok_rows)
    partial_rows = jnp.dot(mixed, w_out, preferred_element_type=jnp.float32)
    summed = lax.psum_scatter(
        partial_rows.astype(jnp.bfloat16), "tensor", scatter_dimension=0, tiled=True
    ).astype(jnp.float32)
    return (tokens.astype(jnp.float32) + summed).astype(jnp.bfloat16)


def solution(mesh):
    return jax.shard_map(
        per_device,
        mesh=mesh,
        in_specs=(
            P(("seg", "tensor"), None),
            P("tensor", None),
            P(),
            P(None, "tensor"),
            P(None, "tensor"),
            P(None, "tensor"),
            P("tensor", None),
            P("seg", "tensor"),
        ),
        out_specs=P(("seg", "tensor"), None),
        check_vma=False,
    )
```

profile of v0, /device:TPU:9, one launch (start us, length us, event | category | flops | bytes accessed | tf_op | source)
XLA Modules:
  0.0 893.3 jit_solution(5897235783449736478)
XLA Ops:
  7.3 1.1 fusion.47
  8.4 1.8 fusion.49
  10.3 3.4 fusion.18
  13.9 3.4 fusion.20
  18.4 1.3 iota_compare_fusion
  19.7 19.5 %all-gather.5.cloned.1.call-done = bf16[64,8192]{1,0:T(8,128)(2,1)} async-done(((bf16[16,8192]{1,0:T(8,128)(2,1)}), bf16[64,8192]{1,0:T(8,128)(2,1)}) %all-gather.5.cloned.1.call-update) | async-done | bytes 1048592 | tf_op jit(solution)/shard_map/all_gather | solution.py:113
  39.2 3.4 fusion.103
  44.1 10.1 %fusion.101 = bf16[64,1024]{1,0:T(8,128)(2,1)S(1)} fusion(bf16[64,8192]{1,0:T(8,128)(2,1)S(1)} %copy-done.1, bf16[8192,1024]{1,0:T(8,128)(2,1)} %param.13), kind=kOutput, calls=%fused_computation.101 | convolution fusion | flops 1073741824 | bytes 17956864 | tf_op jit(solution)/shard_map/dot_general | solution.py:31
  54.2 289.8 %all-gather.3.cloned.1.call-done = bf16[1088,8192]{1,0:T(8,128)(2,1)} async-done(((bf16[272,8192]{1,0:T(8,128)(2,1)}), bf16[1088,8192]{1,0:T(8,128)(2,1)}) %all-gather.3.cloned.1.call-update) | async-done | bytes 17825808 | tf_op jit(solution)/shard_map/all_gather | solution.py:112
  344.0 12.2 %fusion.100 = bf16[1088,256]{1,0:T(8,128)(2,1)S(1)} fusion(bf16[1088,8192]{1,0:T(8,128)(2,1)} %all-gather.3.cloned.1.call-done, bf16[8192,256]{1,0:T(8,128)(2,1)} %param.15), kind=kOutput, calls=%fused_computation.100 | convolution fusion | flops 4563402752 | bytes 22577152 | tf_op jit(solution)/shard_map/dot_general | solution.py:33
  356.2 9.3 %fusion.99 = bf16[1088,256]{1,0:T(8,128)(2,1)S(1)} fusion(bf16[1088,8192]{1,0:T(8,128)(2,1)} %all-gather.3.cloned.1.call-done, bf16[8192,256]{1,0:T(8,128)(2,1)S(1)} %copy-done.3), kind=kOutput, calls=%fused_computation.99 | convolution fusion | flops 4563402752 | bytes 22577152 | tf_op jit(solution)/shard_map/dot_general | solution.py:32
  365.6 21.3 %fusion.98 = bf16[1088,1024]{1,0:T(8,128)(2,1)S(1)} fusion(bf16[1088,8192]{1,0:T(8,128)(2,1)} %all-gather.3.cloned.1.call-done, bf16[8192,1024]{1,0:T(8,128)(2,1)S(1)} %bitcast.72), kind=kOutput, calls=%fused_computation.98 | convolution fusion | flops 18253611008 | bytes 36831232 | tf_op jit(solution)/shard_map/dot_general | solution.py:31
  387.0 17.6 %maximum_convert_fusion = bf16[1152,1536]{1,0:T(8,128)(2,1)S(1)} fusion(bf16[64,256]{1,0:T(8,128)(2,1)S(1)} %fusion.103, bf16[64,256]{1,0:T(8,128)(2,1)S(1)} %fusion.102, bf16[64,1024]{1,0:T(8,128)(2,1)S(1)} %fusion.101, bf16[1088,256]{1,0:T(8,128)(2,1)S(1)} %fusion.100, bf16[1088,256]{1,0:T(8,128)(2,1)S(1)} %fusion.99, bf16[1088,1024]{1,0:T(8,128)(2,1)S(1)} %fusion.98), kind=kLoop, calls=%fused_computation.35 | loop fusion | flops 21233664 | bytes 7077888 | tf_op jit(solution)/shard_map/convert.3
  404.5 1.1 maximum_convert_fusion.2
  406.0 2.8 slice_convert_fusion
  408.8 1.6 slice.43
  410.4 2.5 reshape.51
  412.9 2.6 reshape.50
  417.2 14.1 %fusion.88 = (f32[2,4,576]{2,1,0:T(4,128)S(1)}, f32[2,4,576,1152]{3,2,1,0:T(8,128)}) fusion(pred[576,1152]{1,0:T(8,128)(4,1)} %iota_compare_fusion, bf16[576,2,4,128]{3,2,1,0:T(4,128)(2,1)} %slice.43, bf16[1152,2,128,1]{2,1,0,3:T(2,128)(2,1)} %bitcast.78), kind=kOutput, calls=%fused_computation.96 | convolution fusion | flops 1380189312 | bytes 23685120 | tf_op jit(solution)/shard_map/sub | solution.py:60
  431.3 8.8 fusion.33
  441.7 6.7 reshape.56
  448.4 4.1 slice.54
  452.5 58.2 %while.13 = (s32[]{:T(128)}, f32[8,128,128]{2,1,0:T(8,128)S(1)}, f32[8,128]{1,0:T(8,128)S(1)}, f32[1,8]{1,0:T(1,128)S(1)}, f32[8,128,128]{2,1,0:T(8,128)S(1)}, /*index=5*/f32[2,128]{1,0:T(2,128)S(1)}, s32[]{:T(128)}, s32[]{:T(128)}) while((s32[]{:T(128)}, f32[8,128,128]{2,1,0:T(8,128)S(1)}, f32[8,128]{1,0:T(8,128)S(1)}, ...), condition=%wide.region_8.9_spmd.clone, body=%wide.region_7.8_spmd.clone.sunk | while | flops 660483 | bytes 3175664 | solution.py:144
  452.6 3.7 collective-permute-start
  456.4 1.9 collective-permute-start.1
  458.4 1.3 collective-permute-done.1
  459.9 4.4 collective-permute-start
  464.3 1.9 collective-permute-start.1
  466.3 1.3 collective-permute-done.1
  467.8 4.4 collective-permute-start
  472.3 1.9 collective-permute-start.1
  474.2 1.3 collective-permute-done.1
  475.7 4.8 collective-permute-start
  480.5 2.4 collective-permute-start.1
  484.0 5.3 collective-permute-start
  489.4 2.4 collective-permute-start.1
  492.8 5.3 collective-permute-start
  498.2 2.4 collective-permute-start.1
  501.6 5.3 collective-permute-start
  507.0 2.4 collective-permute-start.1
  510.7 7.7 fusion.27
  518.5 13.4 %fusion.93 = (f32[2,4,576]{2,1,0:T(4,128)S(1)}, f32[2,4,576,1152]{3,2,1,0:T(8,128)}) fusion(pred[576,1152]{1,0:T(8,128)(4,1)S(1)} %copy-done.4, bf16[576,2,4,128]{3,2,1,0:T(4,128)(2,1)S(1)} %slice.41, bf16[1152,2,128,1]{2,1,0,3:T(2,128)(2,1)} %bitcast.79), kind=kOutput, calls=%fused_computation.97 | convolution fusion | flops 1380189312 | bytes 23685120 | tf_op jit(solution)/shard_map/sub | solution.py:60
  531.8 9.1 %fusion.34 = f32[576,2,4,128]{3,0,2,1:T(8,128)S(1)} fusion(f32[2,4,576,1152]{3,2,1,0:T(8,128)} %get-tuple-element.95, f32[2,4,576]{2,1,0:T(4,128)S(1)} %get-tuple-element.94, bf16[1152,2,128,1]{2,1,0,3:T(2,128)(2,1)} %bitcast.80), kind=kOutput, calls=%fused_computation.51 | convolution fusion | flops 1369571328 | bytes 24201216 | tf_op jit(solution)/shard_map/kgrc,ckd->rkgd/dot_general | solution.py:63
  541.0 8.5 fusion.25
  549.6 3.0 copy.31
  552.5 28.5 %convolution_convert_fusion = bf16[1088,8192]{1,0:T(8,128)(2,1)} fusion(bf16[1088,1024]{0,1:T(8,128)(2,1)S(1)} %bitcast.76, bf16[1024,8192]{1,0:T(8,128)(2,1)} %param.16), kind=kOutput, calls=%fused_computation.9 | convolution fusion | flops 18262523904 | bytes 36831232 | tf_op jit(solution)/shard_map/dot_general | solution.py:146
  581.0 298.1 %reduce-scatter.2.cloned.1.call-done = bf16[272,8192]{1,0:T(8,128)(2,1)} async-done(((bf16[1088,8192]{1,0:T(8,128)(2,1)}), bf16[272,8192]{1,0:T(8,128)(2,1)}) %reduce-scatter.2.cloned.1.call-update) | async-done | bytes 4456464 | tf_op jit(solution)/shard_map/reduce_scatter | solution.py:147
  879.2 7.4 fusion.21
  (99 shorter events, 12.1 us)
Async XLA Ops:
  6.5 32.7 %all-gather.5.cloned.1.call-start = ((), (), s32[]{:S(2)}) async-start(), calls=%async_computation.2 | async-start | bytes 1310720 | tf_op jit(solution)/shard_map/all_gather | solution.py:113
  10.2 333.8 %all-gather.3.cloned.1.call-start = ((), (), s32[]{:S(2)}) async-start(), calls=%async_computation.1 | async-start | bytes 22282240 | tf_op jit(solution)/shard_map/all_gather | solution.py:112
  10.3 3.6 copy-start
  17.3 861.9 %reduce-scatter.2.cloned.1.call-start = ((), (), s32[]{:S(2)}) async-start(), calls=%async_computation.3 | async-start | bytes 22282240 | tf_op jit(solution)/shard_map/reduce_scatter | solution.py:147
  39.2 3.5 copy-start.1
  39.2 4.1 copy-start.2
  344.0 12.2 %copy-start.3 = (bf16[8192,256]{1,0:T(8,128)(2,1)S(1)}, bf16[8192,256]{1,0:T(8,128)(2,1)}, u32[]{:S(2)}) copy-start(bf16[8192,256]{1,0:T(8,128)(2,1)} %param.14) | copy-start | bytes 12582916
  344.0 21.6 %slice-start = ((s8[16777216]{0:T(1024)(128)(4,1)}), s8[4194304]{0:T(1024)(128)(4,1)S(1)}, s32[]{:S(2)}) async-start(s8[16777216]{0:T(1024)(128)(4,1)} %bitcast.71), calls=%async_computation.4 | async-start | bytes 8388608
  344.0 21.6 %slice-start.1 = ((s8[16777216]{0:T(1024)(128)(4,1)}), s8[4194304]{0:T(1024)(128)(4,1)S(1)}, s32[]{:S(2)}) async-start(s8[16777216]{0:T(1024)(128)(4,1)} %bitcast.71), calls=%async_computation.5 | async-start | bytes 8388608
  344.0 21.6 %slice-start.2 = ((s8[16777216]{0:T(1024)(128)(4,1)}), s8[4194304]{0:T(1024)(128)(4,1)S(1)}, s32[]{:S(2)}) async-start(s8[16777216]{0:T(1024)(128)(4,1)} %bitcast.71), calls=%async_computation.6 | async-start | bytes 8388608
  356.2 9.4 %slice-start.3 = ((s8[16777216]{0:T(1024)(128)(4,1)}), s8[4194304]{0:T(1024)(128)(4,1)S(1)}, s32[]{:S(2)}) async-start(s8[16777216]{0:T(1024)(128)(4,1)} %bitcast.71), calls=%async_computation.7 | async-start | bytes 8388608
  417.2 14.1 %copy-start.5 = (bf16[1152,2,128]{2,1,0:T(2,128)(2,1)S(1)}, bf16[1152,2,128]{2,1,0:T(2,128)(2,1)}, u32[]{:S(2)}) copy-start(bf16[1152,2,128]{2,1,0:T(2,128)(2,1)} %reshape.50) | copy-start | bytes 1769476
  440.1 1.4 copy-start.7
  448.3 4.1 copy-start.6
  452.6 7.1 collective-permute-start
  456.4 3.2 collective-permute-start.1
  459.9 7.7 collective-permute-start
  464.3 3.2 collective-permute-start.1
  467.8 7.7 collective-permute-start
  472.3 3.2 collective-permute-start.1
  475.7 8.1 collective-permute-start
  480.5 3.2 collective-permute-start.1
  484.0 8.6 collective-permute-start
  489.4 3.2 collective-permute-start.1
  492.8 8.6 collective-permute-start
  498.2 3.2 collective-permute-start.1
  501.6 8.6 collective-permute-start
  507.0 3.2 collective-permute-start.1
  510.7 7.8 copy-start.4
  518.4 22.5 %slice-start.4 = ((s8[4456448]{0:T(1024)(128)(4,1)}), s8[262144]{0:T(1024)(128)(4,1)S(1)}, s32[]{:S(2)}) async-start(s8[4456448]{0:T(1024)(128)(4,1)} %bitcast.74), calls=%async_computation.8 | async-start | bytes 524288
  531.8 9.2 %slice-start.5 = ((s8[4456448]{0:T(1024)(128)(4,1)}), s8[4194304]{0:T(1024)(128)(4,1)S(1)}, s32[]{:S(2)}) async-start(s8[4456448]{0:T(1024)(128)(4,1)} %bitcast.74), calls=%async_computation.9 | async-start | bytes 8388608
  531.8 9.2 %copy-start.8 = (f32[576,2,4,128]{3,0,2,1:T(8,128)S(1)}, f32[576,2,4,128]{3,0,2,1:T(8,128)}, u32[]{:S(2)}) copy-start(f32[576,2,4,128]{3,0,2,1:T(8,128)} %copy-done.7) | copy-start | bytes 7077892
Sparse Core Ops, SparseCore 0:
  10.3 28.8 all-gather.4
  40.8 303.1 all-gather.2
  581.2 297.9 reduce-scatter.1
where the time goes:
time: 906 us; the launch traced here: 893 us
  waiting for transfers between devices  615 us (68%)
  matrix products  148 us (16%)
  starting transfers between devices  48.7 us (5%)
  other arithmetic  43.4 us (5%)
  local copies, waits for them, and re-layouts  23.9 us (3%)
  between operations  13.6 us (2%)
    reduce_scatter x1, waiting for transfers between devices, per_device(): lax.psum_scatter(partial_rows.astype(jnp.bfloat16), 'tensor', scatter_dim...  298 us
    all_gather x1, waiting for transfers between devices, per_device(): lax.all_gather(tok_local, 'tensor', axis=0, tiled=True)  290 us
    ppermute x14, starting transfers between devices, shifted(): return lax.ppermute(block, axis, route)  48.6 us
    dot_general x2, matrix products, project_rows(): jnp.dot(rows, w_query, preferred_element_type=jnp.float32)  31.4 us
    dot_general x1, matrix products, per_device(): partial_rows = jnp.dot(mixed, w_out, preferred_element_type=jnp.float32)  28.5 us
    sub x2, matrix products, soft_part(): weights = jnp.exp(scores - top_score)  27.5 us
    all_gather x1, waiting for transfers between devices, per_device(): lax.all_gather(mem_local, 'tensor', axis=0, tiled=True)  19.5 us
  transfers between devices with their start and end apart: 17, of which 10 were waited for; matrix products, arithmetic and copies ran while one was open for 3% of the time, Pallas kernels for 0%

commit v1 on v0

v1 whole, which is shorter than its diff:
```python
import functools

import jax
import jax.numpy as jnp
from jax import lax
from jax.experimental import pallas as pl
from jax.experimental.pallas import tpu as pltpu
from jax.sharding import PartitionSpec as P

HEAD = 128
EPSILON = 1e-05
SCALE = HEAD ** (-0.5)
LOG2E = 1.4426950408889634
STATE_ROWS = HEAD + 16
VMEM_LIMIT = 48 * 1024 * 1024


def rms_rows(rows, norm_gain):
    widened = rows.astype(jnp.float32)
    scale_rows = lax.rsqrt(jnp.mean(widened * widened, axis=-1, keepdims=True) + EPSILON)
    return (widened * scale_rows * norm_gain.astype(jnp.float32)).astype(jnp.bfloat16)


def feature_map(inputs):
    return jnp.exp(jnp.minimum(inputs, 0.0)) + jnp.maximum(inputs, 0.0)


def after(value, *others):
    return lax.optimization_barrier((value,) + others)[0]


class Planes:
    def __init__(self, count):
        self.count = count
        self.quarter = count // 4
        self.workers = range(self.quarter, 3 * self.quarter)
        self.ends = [i for i in range(count) if i not in self.workers]
        self.turns = range(1, count // 2)

    def partner(self, index):
        return index ^ self.quarter

    def peer(self, index, turn):
        return self.quarter + ((index - self.quarter) ^ turn)

    def lend(self):
        return [(e, self.partner(e)) for e in self.ends]

    def give_back(self):
        return [(w, self.partner(w)) for w in self.workers]

    def pairs(self):
        return [(i, self.partner(i)) for i in range(self.count)]

    def exchange(self, turn):
        return [(w, self.peer(w, turn)) for w in self.workers]

    def far_back(self, turn):
        return [(w, self.partner(self.peer(w, turn))) for w in self.workers]


def hop(block, pairs):
    return lax.ppermute(block, "tensor", pairs)


def seg_cycle(chips):
    half = chips // 2
    return list(range(half)) + list(range(chips - 1, half - 1, -1))


def seg_gather(block):
    size = lax.axis_size("seg")
    chips = size // 2
    cycle = seg_cycle(chips)
    place_of = [cycle.index(c) for c in range(chips)]

    def step(part, distance):
        route = [
            (cycle[i] * 2 + c, cycle[(i + distance) % chips] * 2 + c)
            for i in range(chips)
            for c in range(2)
        ]
        return lax.ppermute(part, "seg", route)

    me = lax.axis_index("seg")
    chip, core = me // 2, me % 2
    place = jnp.array(place_of, jnp.int32)[chip]
    cycle_table = jnp.array(cycle, jnp.int32)

    found = [((block,), 0)]
    right = left = block
    for turn in range(1, chips // 2):
        right, left = step(right, 1), step(left, -1)
        found += [((right,), -turn), ((left,), turn)]
    half = block.shape[0] // 2
    found.append(((step(right[:half], 1), step(left[half:], -1)), chips // 2))
    swap = [(i, i ^ 1) for i in range(size)]
    result = []
    for parts, distance in found:
        owner = cycle_table[(place + distance + chips) % chips] * 2
        result.append((parts, owner + core))
        other = tuple(lax.ppermute(p, "seg", swap) for p in parts)
        result.append((other, owner + 1 - core))
    return result


def seg_slice(array, axis):
    width = array.shape[axis] // lax.axis_size("seg")
    return lax.dynamic_slice_in_dim(array, lax.axis_index("seg") * width, width, axis)


def pad_to(value, unit):
    return -(-value // unit) * unit


def fill(place_ref, slot_refs, all_ref, stride, rows):
    for i, ref in enumerate(slot_refs):
        start = pl.multiple_of(place_ref[i] * stride, 16)
        all_ref[pl.ds(start, rows), :] = ref[...]


def nt_dot(a, b):
    return lax.dot_general(a, b, (((1,), (1,)), ((), ())), preferred_element_type=jnp.float32)


def memory_kernel(slots, stride, rows, groups, place_ref, *refs):
    keys, values = refs[:slots], refs[slots : 2 * slots]
    mem_q, mem_k, mem_v, out_ref, key_all, value_all = refs[2 * slots :]
    mem = mem_k.shape[0]
    base = slots * stride
    if stride != rows:
        key_all[...] = jnp.zeros_like(key_all)
        value_all[...] = jnp.zeros_like(value_all)
    fill(place_ref, keys, key_all, stride, rows)
    fill(place_ref, values, value_all, stride, rows)
    k_tok, v_tok = key_all[...], value_all[...]
    k_mem, v_mem = mem_k[...], mem_v[...]
    row_ids = lax.broadcasted_iota(jnp.int32, (mem, mem), 0)
    col_ids = lax.broadcasted_iota(jnp.int32, (mem, mem), 1)
    feat = feature_map(k_mem.astype(jnp.float32))
    feat_sum = jnp.sum(feat, axis=0, keepdims=True)
    feat_cast = feat.astype(jnp.bfloat16)
    for g in range(groups):
        q = mem_q[:, g * HEAD : (g + 1) * HEAD]
        s_tok = nt_dot(q, k_tok)
        if stride != rows:
            ids = lax.broadcasted_iota(jnp.int32, (mem, base), 1)
            s_tok = jnp.where(lax.rem(ids, stride) < rows, s_tok, -1e30)
        s_mem = jnp.where(row_ids >= col_ids, nt_dot(q, k_mem), -1e30)
        top = jnp.maximum(
            jnp.max(s_tok, axis=1, keepdims=True), jnp.max(s_mem, axis=1, keepdims=True)
        )
        p_tok = jnp.exp2((s_tok - top) * (SCALE * LOG2E))
        p_mem = jnp.exp2((s_mem - top) * (SCALE * LOG2E))
        total = jnp.sum(p_tok, axis=1, keepdims=True) + jnp.sum(p_mem, axis=1, keepdims=True)
        soft = jnp.dot(
            p_tok.astype(jnp.bfloat16), v_tok, preferred_element_type=jnp.float32
        ) + jnp.dot(p_mem.astype(jnp.bfloat16), v_mem, preferred_element_type=jnp.float32)
        soft = soft / total
        out_ref[g, :HEAD, :] = lax.dot_general(
            feat_cast,
            soft.astype(jnp.bfloat16),
            (((0,), (0,)), ((), ())),
            preferred_element_type=jnp.float32,
        )
        out_ref[g, HEAD:, :] = jnp.broadcast_to(feat_sum, (STATE_ROWS - HEAD, HEAD))


def token_kernel(slots, stride, rows, groups, place_ref, *refs):
    queries, keys, values = refs[:slots], refs[slots : 2 * slots], refs[2 * slots : 3 * slots]
    outs = refs[3 * slots : 4 * slots]
    query_all, key_all, value_all, out_all = refs[4 * slots :]
    full = key_all.shape[0]
    if stride != rows:
        query_all[...] = jnp.zeros_like(query_all)
        key_all[...] = jnp.zeros_like(key_all)
        value_all[...] = jnp.zeros_like(value_all)
    elif full > slots * stride:
        tail = (full - slots * stride, HEAD)
        key_all[slots * stride :, :] = jnp.zeros(tail, key_all.dtype)
        value_all[slots * stride :, :] = jnp.zeros(tail, value_all.dtype)
    fill(place_ref, queries, query_all, stride, rows)
    fill(place_ref, keys, key_all, stride, rows)
    fill(place_ref, values, value_all, stride, rows)

    for block in range(slots):
        first = block * stride
        low = first // 128 * 128
        high = min(pad_to(first + stride, 128), full)
        k_diag, v_diag = key_all[low:high, :], value_all[low:high, :]
        row_ids = lax.broadcasted_iota(jnp.int32, (stride, high - low), 0) + first
        col_ids = lax.broadcasted_iota(jnp.int32, (stride, high - low), 1) + low
        keep = row_ids >= col_ids
        if stride != rows:
            keep = keep & (lax.rem(col_ids, stride) < rows)

        def one_head(g, carry, first=first, low=low, k_diag=k_diag, v_diag=v_diag, keep=keep):
            lanes = pl.ds(pl.multiple_of(g * HEAD, HEAD), HEAD)
            q = query_all[first : first + stride, lanes]
            s_diag = jnp.where(keep, nt_dot(q, k_diag), -1e30)
            top = jnp.max(s_diag, axis=1, keepdims=True)
            if low > 0:
                s_prev = nt_dot(q, key_all[:low, :])
                if stride != rows:
                    ids = lax.broadcasted_iota(jnp.int32, (stride, low), 1)
                    s_prev = jnp.where(lax.rem(ids, stride) < rows, s_prev, -1e30)
                top = jnp.maximum(top, jnp.max(s_prev, axis=1, keepdims=True))
            p_diag = jnp.exp2((s_diag - top) * (SCALE * LOG2E))
            total = jnp.sum(p_diag, axis=1, keepdims=True)
            soft = jnp.dot(
                p_diag.astype(jnp.bfloat16), v_diag, preferred_element_type=jnp.float32
            )
            if low > 0:
                p_prev = jnp.exp2((s_prev - top) * (SCALE * LOG2E))
                total = total + jnp.sum(p_prev, axis=1, keepdims=True)
                soft = soft + jnp.dot(
                    p_prev.astype(jnp.bfloat16),
                    value_all[:low, :],
                    preferred_element_type=jnp.float32,
                )
            out_all[first : first + stride, lanes] = soft / total
            return carry

        lax.fori_loop(0, groups, one_head, 0)

    for i, ref in enumerate(outs):
        start = pl.multiple_of(place_ref[i] * stride, 16)
        ref[...] = out_all[pl.ds(start, rows), :]


def read_kernel(slots, *refs):
    softs, queries = refs[:slots], refs[slots : 2 * slots]
    state_ref = refs[2 * slots]
    outs = refs[2 * slots + 1 :]
    state = state_ref[0, :HEAD, :].astype(jnp.bfloat16)
    sums = jnp.broadcast_to(state_ref[0, HEAD : HEAD + 1, :], (HEAD, HEAD)).astype(jnp.bfloat16)
    for soft, query, out in zip(softs, queries, outs):
        feat = feature_map(query[...].astype(jnp.float32)).astype(jnp.bfloat16)
        numerator = jnp.dot(feat, state, preferred_element_type=jnp.float32)
        denominator = nt_dot(feat, sums) + 1.0
        out[...] = (soft[...] + numerator / denominator).astype(jnp.bfloat16)


class Group:
    def __init__(self, queries, keys, values, key_block, value_block, mem, heads, kv_heads):
        self.queries, self.keys, self.values = queries, keys, values
        self.key_block, self.value_block = key_block, value_block
        self.mem = mem
        self.heads, self.kv_heads = heads, kv_heads
        self.groups = heads // kv_heads
        self.rows = queries[0].shape[0]
        self.stride = pad_to(self.rows, 16)

    def specs(self, rows):
        wide = self.groups * HEAD
        kb, vb = self.key_block, self.value_block
        return (
            pl.BlockSpec((rows, wide), lambda h, *_: (0, h)),
            pl.BlockSpec((rows, HEAD), lambda h, *_: (0, h + kb)),
            pl.BlockSpec((rows, HEAD), lambda h, *_: (0, h + vb)),
        )

    def write(self, places):
        slots = len(self.keys)
        _, k_spec, v_spec = self.specs(self.rows)
        mem_rows = self.mem[0].shape[0]
        spread = slots * self.stride
        return pl.pallas_call(
            functools.partial(memory_kernel, slots, self.stride, self.rows, self.groups),
            grid_spec=pltpu.PrefetchScalarGridSpec(
                num_scalar_prefetch=1,
                grid=(self.kv_heads,),
                in_specs=[k_spec] * slots + [v_spec] * slots + list(self.specs(mem_rows)),
                out_specs=pl.BlockSpec((self.groups, STATE_ROWS, HEAD), lambda h, *_: (h, 0, 0)),
                scratch_shapes=[
                    pltpu.VMEM((spread, HEAD), jnp.bfloat16),
                    pltpu.VMEM((spread, HEAD), jnp.bfloat16),
                ],
            ),
            out_shape=jax.ShapeDtypeStruct((self.heads, STATE_ROWS, HEAD), jnp.float32),
            compiler_params=pltpu.CompilerParams(vmem_limit_bytes=VMEM_LIMIT),
            name="memory_write",
        )(places, *self.keys, *self.values, *self.mem)

    def attend(self, places):
        slots = len(self.keys)
        wide = self.groups * HEAD
        q_spec, k_spec, v_spec = self.specs(self.rows)
        spread = slots * self.stride
        full = pad_to(spread, 128)
        work = 2 * self.heads * spread * spread * HEAD
        return pl.pallas_call(
            functools.partial(token_kernel, slots, self.stride, self.rows, self.groups),
            grid_spec=pltpu.PrefetchScalarGridSpec(
                num_scalar_prefetch=1,
                grid=(self.kv_heads,),
                in_specs=[q_spec] * slots + [k_spec] * slots + [v_spec] * slots,
                out_specs=[pl.BlockSpec((self.rows, wide), lambda h, *_: (0, h))] * slots,
                scratch_shapes=[
                    pltpu.VMEM((spread, wide), jnp.bfloat16),
                    pltpu.VMEM((full, HEAD), jnp.bfloat16),
                    pltpu.VMEM((full, HEAD), jnp.bfloat16),
                    pltpu.VMEM((spread, wide), jnp.float32),
                ],
            ),
            out_shape=[jax.ShapeDtypeStruct((self.rows, self.heads * HEAD), jnp.float32)] * slots,
            compiler_params=pltpu.CompilerParams(vmem_limit_bytes=VMEM_LIMIT),
            cost_estimate=pl.CostEstimate(
                flops=2 * work, bytes_accessed=16 * spread * wide, transcendentals=work // 256
            ),
            name="token_attention",
        )(places, *self.queries, *self.keys, *self.values)

    def read(self, softs, state):
        slots = len(softs)
        block = pl.BlockSpec((self.rows, HEAD), lambda h: (0, h))
        return pl.pallas_call(
            functools.partial(read_kernel, slots),
            grid=(self.heads,),
            in_specs=[block] * (2 * slots)
            + [pl.BlockSpec((1, STATE_ROWS, HEAD), lambda h: (h, 0, 0))],
            out_specs=[block] * slots,
            out_shape=[jax.ShapeDtypeStruct((self.rows, self.heads * HEAD), jnp.bfloat16)] * slots,
            compiler_params=pltpu.CompilerParams(vmem_limit_bytes=VMEM_LIMIT),
            name="memory_read",
        )(*softs, *self.queries, state)


def relay(writes, rates):
    size = lax.axis_size("seg")
    me = lax.axis_index("seg")
    ids = lax.broadcasted_iota(jnp.int32, (size, 1), 0)

    def product(mask):
        return jnp.prod(jnp.where(mask, rates, 1.0), axis=0)[:, None, None]

    total = writes
    prefix = jnp.zeros_like(writes)
    bit = 1
    while bit < size:
        route = [(i, i ^ bit) for i in range(size)]
        got = lax.ppermute(total.astype(jnp.bfloat16), "seg", route).astype(jnp.float32)
        mine = ids // bit == me // bit
        theirs = ids // bit == (me // bit) ^ 1
        upper = (me // bit) % 2 == 1
        prefix = jnp.where(upper, product(mine & (ids < me)) * got + prefix, prefix)
        total = jnp.where(upper, product(mine) * got + total, product(theirs) * total + got)
        bit *= 2
    return prefix


def output_kernel(plan, bufs, ids_ref, mixed_ref, tokens_ref, own_ref, *refs):
    count = sum(len(p) for row in plan for p in row if p is not None)
    piece_refs, (out_ref, weights, total, sems) = refs[:count], refs[count:]
    blocks, groups = len(plan), len(plan[0])
    width = weights.shape[2]
    c, g = pl.program_id(0), pl.program_id(1)
    step = c * groups + g
    steps = blocks * groups

    def start(at):
        slot = lax.rem(at, bufs)
        for b in range(blocks):
            for j in range(groups):

                @pl.when(at == b * groups + j)
                def _():
                    if plan[b][j] is None:
                        columns = pl.ds(pl.multiple_of(ids_ref[b] * width, 128), width)
                        pltpu.make_async_copy(
                            own_ref.at[:, columns], weights.at[slot], sems.at[slot]
                        ).start()
                        return
                    row = 0
                    for index in plan[b][j]:
                        part = piece_refs[index]
                        high = part.shape[0]
                        pltpu.make_async_copy(
                            part, weights.at[slot, pl.ds(row, high), :], sems.at[slot]
                        ).start()
                        row += high

    @pl.when(step == 0)
    def _():
        for at in range(min(bufs - 1, steps)):
            start(jnp.int32(at))

    @pl.when(step + bufs - 1 < steps)
    def _():
        start(step + bufs - 1)

    slot = lax.rem(step, bufs)
    pltpu.make_async_copy(weights.at[slot], weights.at[slot], sems.at[slot]).wait()
    term = jnp.dot(mixed_ref[g], weights[slot], preferred_element_type=jnp.float32)

    @pl.when(g == 0)
    def _():
        total[...] = tokens_ref[...].astype(jnp.float32) + term

    @pl.when(g > 0)
    def _():
        total[...] = total[...] + term

    @pl.when(g == groups - 1)
    def _():
        out_ref[...] = total[...].astype(out_ref.dtype)


def output_product(mixed, tokens, w_out, gathered):
    groups, rows, depth = mixed.shape
    blocks = len(gathered[0])
    width = w_out.shape[1] // blocks
    ids = jnp.stack([gathered[0][b][1] for b in range(blocks)]).astype(jnp.int32)
    plan, pieces = [], []
    for b in range(blocks):
        row = [None]
        for pieces_of in gathered:
            parts = pieces_of[b][0]
            row.append(tuple(range(len(pieces), len(pieces) + len(parts))))
            pieces += parts
        plan.append(row)
    bufs = 4
    return pl.pallas_call(
        functools.partial(output_kernel, plan, bufs),
        grid_spec=pltpu.PrefetchScalarGridSpec(
            num_scalar_prefetch=1,
            grid=(blocks, groups),
            in_specs=[
                pl.BlockSpec((groups, rows, depth), lambda c, g, ids: (0, 0, 0)),
                pl.BlockSpec((rows, width), lambda c, g, ids: (0, ids[c])),
                pl.BlockSpec(memory_space=pl.ANY),
            ]
            + [pl.BlockSpec(memory_space=pl.ANY)] * len(pieces),
            out_specs=pl.BlockSpec((rows, width), lambda c, g, ids: (0, ids[c])),
            scratch_shapes=[
                pltpu.VMEM((bufs, depth, width), jnp.bfloat16),
                pltpu.VMEM((rows, width), jnp.float32),
                pltpu.SemaphoreType.DMA((bufs,)),
            ],
        ),
        out_shape=jax.ShapeDtypeStruct(tokens.shape, tokens.dtype),
        compiler_params=pltpu.CompilerParams(vmem_limit_bytes=VMEM_LIMIT),
        name="output_product",
    )(ids, mixed, tokens, w_out, *pieces)


def dot_cast(a, b):
    return jnp.dot(a, b, preferred_element_type=jnp.float32).astype(jnp.bfloat16)


def per_device(tokens, memory_embed, norm_gain, w_query, w_key, value_weight, w_out, retain):
    planes = Planes(lax.axis_size("tensor"))
    me = lax.axis_index("tensor")
    is_worker = (me >= planes.quarter) & (me < 3 * planes.quarter)
    is_end = jnp.logical_not(is_worker)
    worker = jnp.where(is_end, planes.partner(me), me)
    rows = tokens.shape[0]
    width = tokens.shape[1]
    seg_count = lax.axis_size("seg")
    heads, kv_heads = w_query.shape[1] // HEAD, w_key.shape[1] // HEAD

    normed = rms_rows(tokens, norm_gain)
    mem_local = rms_rows(memory_embed, norm_gain)

    lent = jnp.concatenate(
        [seg_slice(w_query, 0), seg_slice(w_key, 0), seg_slice(value_weight, 0)], axis=1
    )
    lent = hop(lent, planes.lend())
    lent_pieces = seg_gather(lent)

    slots = [normed]
    places = [me, planes.partner(me)]
    slots.append(hop(normed, planes.lend()))
    for turn in planes.turns:
        peer = planes.peer(worker, turn)
        slots.append(hop(normed, planes.exchange(turn)))
        slots.append(hop(slots[1], planes.exchange(turn)))
        places += [peer, planes.partner(peer)]
    places = jnp.stack(places).astype(jnp.int32)

    mem_slice = seg_slice(mem_local, 1)
    mem_all = lax.all_gather(mem_slice, "tensor", axis=0, tiled=True)
    mem_all = lax.all_gather(mem_all, "seg", axis=1, tiled=True)
    mem_rows = mem_all.shape[0]

    share = seg_slice(w_out, 1)
    near = hop(share, planes.pairs())
    shares = [near]
    for turn in planes.turns:
        for piece in (share, near):
            piece = hop(piece, planes.exchange(turn))
            shares.append(jnp.where(is_end, hop(piece, planes.give_back()), piece))
    gathered = [seg_gather(piece) for piece in shares]

    rates = lax.all_gather(retain[0], "seg", axis=0)
    rates = jnp.concatenate([rates, hop(rates, planes.lend())], axis=1)

    lent_all = jnp.zeros((width, lent.shape[1]), jnp.bfloat16)
    piece_rows = width // seg_count
    for parts, owner in lent_pieces:
        start = owner * piece_rows
        for part in parts:
            lent_all = lax.dynamic_update_slice(lent_all, part, (start, 0))
            start = start + part.shape[0]

    first = jnp.concatenate([normed, mem_all], axis=0)
    inputs = [first] + slots[1:]
    own_q = [dot_cast(x, w_query) for x in inputs]
    own_k = [dot_cast(x, w_key) for x in inputs]
    own_v = [dot_cast(x, value_weight) for x in inputs]
    lent_qkv = [dot_cast(x, lent_all) for x in inputs]

    def split(arrays):
        return [arrays[0][:rows]] + arrays[1:], arrays[0][rows:]

    (own_q, mem_q), (own_k, mem_k), (own_v, mem_v) = split(own_q), split(own_k), split(own_v)
    lent_qkv, mem_qkv = split(lent_qkv)
    own = Group(own_q, own_k, own_v, 0, 0, (mem_q, mem_k, mem_v), heads, kv_heads)
    lent = Group(
        lent_qkv,
        lent_qkv,
        lent_qkv,
        heads,
        heads + kv_heads,
        (mem_qkv, mem_qkv, mem_qkv),
        heads,
        kv_heads,
    )

    writes = jnp.concatenate([own.write(places), lent.write(places)], axis=0)
    state = relay(writes, rates)
    mixed_own = own.read(own.attend(places), state[:heads])
    mixed_lent = lent.read(lent.attend(places), state[heads:])

    back = planes.give_back()
    mixed = [
        jnp.where(is_end, hop(mixed_lent[1], back), mixed_own[0]),
        jnp.where(is_end, hop(mixed_own[1], back), mixed_lent[0]),
    ]
    for number, turn in enumerate(planes.turns):
        near_slot, far_slot = 2 + 2 * number, 3 + 2 * number
        for arrays in (mixed_own, mixed_lent):
            mixed.append(
                jnp.where(
                    is_end,
                    hop(arrays[far_slot], planes.far_back(turn)),
                    hop(arrays[near_slot], planes.exchange(turn)),
                )
            )
    return output_product(jnp.stack(mixed), tokens, w_out, gathered)


def solution(mesh):
    return jax.shard_map(
        per_device,
        mesh=mesh,
        in_specs=(
            P(("seg", "tensor"), None),
            P("tensor", None),
            P(),
            P(None, "tensor"),
            P(None, "tensor"),
            P(None, "tensor"),
            P("tensor", None),
            P("seg", "tensor"),
        ),
        out_specs=P(("seg", "tensor"), None),
        check_vma=False,
    )
```

time: 906 us -> 851 us (0.939)
  waiting for transfers between devices: 615 us -> 233 us
  blocking collectives: 0 us -> 175 us
  Pallas kernels: 0 us -> 120 us
  starting transfers between devices: 48.7 us -> 78.2 us
  local copies, waits for them, and re-layouts: 23.9 us -> 53.3 us
  other arithmetic: 43.4 us -> 24.2 us
  matrix products: 148 us -> 135 us
    all_gather x2 -> x1, waiting for transfers between devices: 309 us -> 3.64 us  [per_device(): mem_all = lax.all_gather(mem_all, 'seg', axis=1, tiled=True)]
    reduce_scatter x1 -> x0, waiting for transfers between devices: 298 us -> none  [per_device(): lax.psum_scatter(partial_rows.astype(jnp.bfloat16), 'tensor', scatter_dim...]
    ppermute x14 -> x55, waiting for transfers between devices: 7.16 us -> 230 us  [the longest x16 117 us: hop(): return lax.ppermute(block, 'tensor', pairs)]
    all_gather x0 -> x2, blocking collectives: none -> 175 us  [the longest x1 162 us: per_device(): mem_all = lax.all_gather(mem_slice, 'tensor', axis=0, tiled=True)]
    pallas_call x0 -> x7, Pallas kernels: none -> 120 us  [the longest x2 58.2 us: attend(): pl.pallas_call(functools.partial(token_kernel, slots, self.stride, self.r...]
    ppermute x14 -> x55, starting transfers between devices: 48.6 us -> 78.2 us  [the longest x16 40.4 us: hop(): return lax.ppermute(block, 'tensor', pairs)]
    sub x2 -> x0, matrix products: 27.5 us -> none  [soft_part(): weights = jnp.exp(scores - top_score)]
    dynamic_update_slice x0 -> x10, local copies, waits for them, and re-layouts: none -> 22.1 us  [per_device(): lent_all = lax.dynamic_update_slice(lent_all, part, (start, 0))]
  transfers between devices with their start and end apart: 17 -> 56, of which waited for: 10 -> 13; matrix products, arithmetic and copies ran while one was open for 3% -> 24% of each run, Pallas kernels for 0% -> 10%
where the time goes in v1:
time: 851 us; the launch traced here: 839 us
  waiting for transfers between devices  233 us (27%)
  blocking collectives  175 us (21%)
  matrix products  135 us (16%)
  Pallas kernels  120 us (14%)
  starting transfers between devices  78.2 us (9%)
  local copies, waits for them, and re-layouts  53.3 us (6%)
  other arithmetic  24.2 us (3%)
  between operations  20.3 us (2%)
    all_gather x1, blocking collectives, per_device(): mem_all = lax.all_gather(mem_slice, 'tensor', axis=0, tiled=True)  162 us
    dot_general x16, matrix products, dot_cast(): jnp.dot(a, b, preferred_element_type=jnp.float32).astype(jnp.bfloat16)  135 us
    ppermute x16, waiting for transfers between devices, hop(): return lax.ppermute(block, 'tensor', pairs)  117 us
    ppermute x16, waiting for transfers between devices, step(): return lax.ppermute(part, 'seg', route)  102 us
    pallas_call x2, Pallas kernels, attend(): pl.pallas_call(functools.partial(token_kernel, slots, self.stride, self.r...  58.2 us
    ppermute x16, starting transfers between devices, hop(): return lax.ppermute(block, 'tensor', pairs)  40.4 us
    pallas_call x1, Pallas kernels, output_product(): pl.pallas_call(functools.partial(output_kernel, plan, bufs), grid_spec=pl...  36.7 us
    ppermute x20, starting transfers between devices, seg_gather(): other = tuple((lax.ppermute(p, 'seg', swap) for p in parts))  22.2 us
  transfers between devices with their start and end apart: 56, of which 13 were waited for; matrix products, arithmetic and copies ran while one was open for 24% of the time, Pallas kernels for 10%

profile of v1, /device:TPU:9, one launch (start us, length us, event | category | flops | bytes accessed | tf_op | source)
XLA Modules:
  0.0 839.5 jit_solution(15746608034066661080)
XLA Ops:
  8.5 4.5 collective-permute-start.24
  18.8 3.4 fusion.2
  23.7 34.4 %collective-permute-done.24 = bf16[1024,1024]{1,0:T(8,128)(2,1)} collective-permute-done((bf16[1024,1024]{1,0:T(8,128)(2,1)S(1)}, bf16[1024,1024]{1,0:T(8,128)(2,1)}, u32[]{:S(2)}, u32[]{:S(2)}) %collective-permute-start.24) | collective-permute-done | bytes 2097184 | tf_op jit(solution)/shard_map/ppermute | solution.py:63
  62.0 162.4 %all_gather.9 = bf16[64,1024]{1,0:T(8,128)(2,1)} all-gather(bf16[16,1024]{1,0:T(8,128)(2,1)S(1)} %fusion.11), channel_id=1, replica_groups=mesh['seg'=8,'tensor'=4] {'tensor'}, dimensions={0}, use_global_device_ids=true | all-gather | bytes 163840 | tf_op jit(solution)/shard_map/all_gather | solution.py:482
  234.1 12.7 %all-gather = f32[8,1,8]{2,1,0:T(1,128)S(1)} all-gather(f32[1,1,8]{2,1,0:T(1,128)S(1)} %bitcast.62), channel_id=1, replica_groups=mesh['seg'=8,'tensor'=4] {'seg'}, dimensions={0}, use_global_device_ids=true | all-gather | bytes 288 | tf_op jit(solution)/shard_map/all_gather | solution.py:495
  249.5 3.6 all-gather.3.cloned.1.call-done
  253.2 11.3 %convolution_convert_fusion.4 = bf16[336,1024]{1,0:T(8,128)(2,1)S(1)} fusion(bf16[8192,1024]{1,0:T(8,128)(2,1)} %param.15, bf16[64,8192]{1,0:T(8,128)(2,1)} %all-gather.3.cloned.1.call-done, bf16[272,8192]{1,0:T(8,128)(2,1)} %fusion.2), kind=kOutput, calls=%fused_computation.22 | convolution fusion | flops 5648498688 | bytes 22970368 | tf_op jit(solution)/shard_map/dot_general | solution.py:448
  264.5 5.3 collective-permute-start.12
  269.8 3.9 convolution_convert_fusion.9
  273.7 21.7 %collective-permute-done.37.refs_12_ = bf16[1024,1024]{1,0:T(8,128)(2,1)S(1)} collective-permute-done((bf16[1024,1024]{1,0:T(8,128)(2,1)}, bf16[1024,1024]{1,0:T(8,128)(2,1)S(1)}, u32[]{:S(2)}, u32[]{:S(2)}) %collective-permute-start.37) | collective-permute-done | bytes 2097184 | tf_op jit(solution)/shard_map/ppermute | solution.py:83
  296.2 3.9 convolution_convert_fusion.8
  304.3 3.7 slice.84
  309.9 4.7 broadcast_select_fusion.1.refs_1_
  314.6 5.4 convolution_convert_fusion.15.refs_1_.refs_5_
  320.8 5.3 convolution_convert_fusion.12.refs_5_.refs_9_
  328.9 33.9 %collective-permute-done.4 = bf16[1024,1536]{1,0:T(8,128)(2,1)} collective-permute-done((bf16[1024,1536]{1,0:T(8,128)(2,1)}, bf16[1024,1536]{1,0:T(8,128)(2,1)}, u32[]{:S(2)}, u32[]{:S(2)}) %collective-permute-start.4) | collective-permute-done | bytes 3145760 | tf_op jit(solution)/shard_map/ppermute | solution.py:83
  363.5 3.7 convolution_convert_fusion.14.refs_2_.refs_6_
  367.2 3.6 convolution_convert_fusion.11.refs_6_.refs_10_
  374.6 3.9 constant_dynamic-update-slice_fusion.7
  380.2 36.1 %collective-permute-done.12 = bf16[272,8192]{1,0:T(8,128)(2,1)} collective-permute-done((bf16[272,8192]{1,0:T(8,128)(2,1)}, bf16[272,8192]{1,0:T(8,128)(2,1)}, u32[]{:S(2)}, u32[]{:S(2)}) %collective-permute-start.12) | collective-permute-done | bytes 4456480 | tf_op jit(solution)/shard_map/ppermute | solution.py:63
  416.3 4.4 collective-permute-start.8
  420.7 3.6 convolution_convert_fusion.13.refs_3_.refs_7_
  424.3 3.6 convolution_convert_fusion.10.refs_7_.refs_11_
  428.0 5.1 memory_write.2
  438.5 3.8 constant_dynamic-update-slice_fusion.3
  452.5 15.1 %convolution_convert_fusion = bf16[336,1536]{1,0:T(8,128)(2,1)S(1)} fusion(bf16[8192,1536]{1,0:T(8,128)(2,1)} %constant_dynamic-update-slice_fusion.5, bf16[64,8192]{1,0:T(8,128)(2,1)} %all-gather.3.cloned.1.call-done, bf16[272,8192]{1,0:T(8,128)(2,1)} %fusion.2), kind=kOutput, calls=%fused_computation.7 | convolution fusion | flops 8467243008 | bytes 31703040 | tf_op jit(solution)/shard_map/dot_general | solution.py:448
  467.6 13.1 %convolution_convert_fusion.3.refs_1_.refs_5_.refs_9_ = bf16[272,1536]{1,0:T(8,128)(2,1)S(1)} fusion(bf16[272,8192]{1,0:T(8,128)(2,1)} %collective-permute-done.10, bf16[8192,1536]{1,0:T(8,128)(2,1)} %constant_dynamic-update-slice_fusion.5), kind=kOutput, calls=%fused_computation.10 | convolution fusion | flops 6845521920 | bytes 30457856 | tf_op jit(solution)/shard_map/dot_general | solution.py:448
  480.7 13.3 %convolution_convert_fusion.2.refs_2_.refs_6_.refs_10_ = bf16[272,1536]{1,0:T(8,128)(2,1)S(1)} fusion(bf16[272,8192]{1,0:T(8,128)(2,1)} %collective-permute-done.11, bf16[8192,1536]{1,0:T(8,128)(2,1)} %constant_dynamic-update-slice_fusion.5), kind=kOutput, calls=%fused_computation.9 | convolution fusion | flops 6845521920 | bytes 30457856 | tf_op jit(solution)/shard_map/dot_general | solution.py:448
  497.5 13.3 %convolution_convert_fusion.1.refs_3_.refs_7_.refs_11_ = bf16[272,1536]{1,0:T(8,128)(2,1)S(1)} fusion(bf16[272,8192]{1,0:T(8,128)(2,1)} %collective-permute-done.12, bf16[8192,1536]{1,0:T(8,128)(2,1)} %constant_dynamic-update-slice_fusion.5), kind=kOutput, calls=%fused_computation.8 | convolution fusion | flops 6845521920 | bytes 30457856 | tf_op jit(solution)/shard_map/dot_general | solution.py:448
  510.9 5.2 memory_write.3
  517.0 23.9 %collective-permute-done.27 = bf16[1024,1024]{1,0:T(8,128)(2,1)S(1)} collective-permute-done((bf16[1024,1024]{1,0:T(8,128)(2,1)S(1)}, bf16[1024,1024]{1,0:T(8,128)(2,1)S(1)}, u32[]{:S(2)}, u32[]{:S(2)}) %collective-permute-start.27) | collective-permute-done | bytes 2097184 | tf_op jit(solution)/shard_map/ppermute | solution.py:63
  544.3 3.2 broadcast_select_fusion.refs_2_
  547.5 16.9 %collective-permute-done.44.refs_19_ = bf16[512,1024]{1,0:T(8,128)(2,1)} collective-permute-done((bf16[512,1024]{1,0:T(8,128)(2,1)}, bf16[512,1024]{1,0:T(8,128)(2,1)}, u32[]{:S(2)}, u32[]{:S(2)}) %collective-permute-start.44) | collective-permute-done | bytes 1048608 | tf_op jit(solution)/shard_map/ppermute | solution.py:83
  571.3 11.9 %convolution_convert_fusion.7.refs_1_.refs_5_ = bf16[272,1024]{1,0:T(8,128)(2,1)S(1)} fusion(bf16[272,8192]{1,0:T(8,128)(2,1)} %collective-permute-done.10, bf16[8192,1024]{1,0:T(8,128)(2,1)} %param.15), kind=kOutput, calls=%fused_computation.25 | convolution fusion | flops 4563681280 | bytes 21790720 | tf_op jit(solution)/shard_map/dot_general | solution.py:448
  586.3 27.4 %collective-permute-done.33.refs_8_ = bf16[1024,1024]{1,0:T(8,128)(2,1)} collective-permute-done((bf16[1024,1024]{1,0:T(8,128)(2,1)}, bf16[1024,1024]{1,0:T(8,128)(2,1)}, u32[]{:S(2)}, u32[]{:S(2)}) %collective-permute-start.33) | collective-permute-done | bytes 2097184 | tf_op jit(solution)/shard_map/ppermute | solution.py:83
  615.2 11.0 %collective-permute-done.15 = bf16[16,144,128]{2,1,0:T(8,128)(2,1)S(1)} collective-permute-done((bf16[16,144,128]{2,1,0:T(8,128)(2,1)S(1)}, bf16[16,144,128]{2,1,0:T(8,128)(2,1)S(1)}, u32[]{:S(2)}, u32[]{:S(2)}) %collective-permute-start.15) | collective-permute-done | bytes 589856 | tf_op jit(solution)/shard_map/ppermute | solution.py:342
  626.7 11.9 %convolution_convert_fusion.6.refs_2_.refs_6_ = bf16[272,1024]{1,0:T(8,128)(2,1)S(1)} fusion(bf16[272,8192]{1,0:T(8,128)(2,1)} %collective-permute-done.11, bf16[8192,1024]{1,0:T(8,128)(2,1)} %param.15), kind=kOutput, calls=%fused_computation.24 | convolution fusion | flops 4563681280 | bytes 21790720 | tf_op jit(solution)/shard_map/dot_general | solution.py:448
  652.3 12.0 %convolution_convert_fusion.5.refs_3_.refs_7_ = bf16[272,1024]{1,0:T(8,128)(2,1)S(1)} fusion(bf16[272,8192]{1,0:T(8,128)(2,1)} %collective-permute-done.12, bf16[8192,1024]{1,0:T(8,128)(2,1)} %param.15), kind=kOutput, calls=%fused_computation.23 | convolution fusion | flops 4563681280 | bytes 21790720 | tf_op jit(solution)/shard_map/dot_general | solution.py:448
  665.5 29.1 %token_attention.2 = (f32[272,1024]{1,0:T(8,128)S(1)}, f32[272,1024]{1,0:T(8,128)S(1)}, f32[272,1024]{1,0:T(8,128)}, f32[272,1024]{1,0:T(8,128)}) custom-call(s32[4]{0:T(128)S(1)} %pad_add_fusion.place_ref, bf16[272,1536]{1,0:T(8,128)(2,1)S(1)} %slice.74.refs_0_.refs_4_.refs_8_, bf16[272,1536]{1,0:T(8,128)(2,1)S(1)} %convolution_convert_fusion.3.refs_1_.refs_5_.refs_9_, ...), custom_call_target="tpu_custom_call" | custom-call | flops 4848615424 | bytes 8912896 | tf_op jit(solution)/shard_map/token_attention/pallas_call | solution.py:292
  699.2 7.9 memory_read.2
  710.6 29.1 %token_attention.3 = (f32[272,1024]{1,0:T(8,128)S(1)}, f32[272,1024]{1,0:T(8,128)S(1)}, f32[272,1024]{1,0:T(8,128)}, f32[272,1024]{1,0:T(8,128)}) custom-call(s32[4]{0:T(128)S(1)} %pad_add_fusion.place_ref, bf16[272,1024]{1,0:T(8,128)(2,1)S(1)} %slice.82.refs_0_.refs_4_, bf16[272,1024]{1,0:T(8,128)(2,1)S(1)} %convolution_convert_fusion.7.refs_1_.refs_5_, ...), custom_call_target="tpu_custom_call" | custom-call | flops 4848615424 | bytes 8912896 | tf_op jit(solution)/shard_map/token_attention/pallas_call | solution.py:292
  740.8 7.1 memory_read.3
  754.4 5.8 collective-permute-done.19
  760.2 5.9 collective-permute-start.18
  766.0 8.0 collective-permute-done.20
  776.3 3.3 collective-permute-start.53
  779.6 8.6 %collective-permute-done.17 = bf16[272,1024]{1,0:T(8,128)(2,1)} collective-permute-done((bf16[272,1024]{1,0:T(8,128)(2,1)}, bf16[272,1024]{1,0:T(8,128)(2,1)}, u32[]{:S(2)}, u32[]{:S(2)}) %collective-permute-start.17) | collective-permute-done | bytes 557088 | tf_op jit(solution)/shard_map/ppermute | solution.py:63
  795.5 36.7 %output_product.1 = bf16[272,8192]{1,0:T(8,128)(2,1)} custom-call(s32[8]{0:T(128)S(1)} %stack.65.ids_ref, bf16[4,272,1024]{2,1,0:T(8,128)(2,1)} %pad_maximum_fusion.2.mixed_ref, bf16[272,8192]{1,0:T(8,128)(2,1)} %tokens_ref.1, bf16[1024,8192]{1,0:T(8,128)(2,1)} %own_ref.1, bf16[1024,1024]{1,0:T(8,128)(2,1)} %collective-permute-done.23.refs_0_, ...), custom_call_target="tpu_custom_call" | custom-call | tf_op jit(solution)/shard_map/output_product/pallas_call | solution.py:423
  (270 shorter events, 111.7 us)
Async XLA Ops:
  6.5 246.6 %all-gather.3.cloned.1.call-start = ((), (), s32[]{:S(2)}) async-start(), calls=%async_computation | async-start | bytes 1179648 | tf_op jit(solution)/shard_map/all_gather | solution.py:483
  8.5 52.3 %collective-permute-start.23 = (bf16[1024,1024]{1,0:T(8,128)(2,1)S(1)}, bf16[1024,1024]{1,0:T(8,128)(2,1)}, u32[]{:S(2)}, u32[]{:S(2)}) collective-permute-start(bf16[1024,1024]{1,0:T(8,128)(2,1)S(1)} %constant_dynamic-slice_fusion), channel_id=1, source_target_pairs={{0,1},{1,0},{2,3},{3,2},{4,5},{5,4},{6,7},{7,6},{8,9},{9,8},{10,11... | collective-permute-start | bytes 6291464 | tf_op jit(solution)/shard_map/ppermute | solution.py:63
  8.5 49.6 %collective-permute-start.24 = (bf16[1024,1024]{1,0:T(8,128)(2,1)S(1)}, bf16[1024,1024]{1,0:T(8,128)(2,1)}, u32[]{:S(2)}, u32[]{:S(2)}) collective-permute-start(bf16[1024,1024]{1,0:T(8,128)(2,1)S(1)} %constant_dynamic-slice_fusion), channel_id=1, source_target_pairs={{1,2},{2,1},{5,6},{6,5},{9,10},{10,9},{13,14},{14,13},{17,18},{18,... | collective-permute-start | bytes 6291464 | tf_op jit(solution)/shard_map/ppermute | solution.py:63
  16.4 230.4 %collective-permute-start = (bf16[1024,1536]{1,0:T(8,128)(2,1)S(1)}, bf16[1024,1536]{1,0:T(8,128)(2,1)}, u32[]{:S(2)}, u32[]{:S(2)}) collective-permute-start(bf16[1024,1536]{1,0:T(8,128)(2,1)S(1)} %pad_maximum_fusion.1), channel_id=1, source_target_pairs={{0,1},{3,2},{4,5},{7,6},{8,9},{11,10},{12,13},{15,14},{16,17},{19,... | collective-permute-start | bytes 9437192 | tf_op jit(solution)/shard_map/ppermute | solution.py:63
  22.2 242.4 %collective-permute-start.10 = (bf16[272,8192]{1,0:T(8,128)(2,1)}, bf16[272,8192]{1,0:T(8,128)(2,1)}, u32[]{:S(2)}, u32[]{:S(2)}) collective-permute-start(bf16[272,8192]{1,0:T(8,128)(2,1)} %fusion.2), channel_id=1, source_target_pairs={{0,1},{3,2},{4,5},{7,6},{8,9},{11,10},{12,13},{15,14},{16,17},{19,... | collective-permute-start | bytes 13369352 | tf_op jit(solution)/shard_map/ppermute | solution.py:63
  58.2 189.9 %collective-permute-start.25 = (bf16[1024,1024]{1,0:T(8,128)(2,1)}, bf16[1024,1024]{1,0:T(8,128)(2,1)}, u32[]{:S(2)}, u32[]{:S(2)}) collective-permute-start(bf16[1024,1024]{1,0:T(8,128)(2,1)} %collective-permute-done.24), channel_id=1, source_target_pairs={{1,0},{2,3},{5,4},{6,7},{9,8},{10,11},{13,12},{14,15},{17,16},{18,... | collective-permute-start | bytes 6291464 | tf_op jit(solution)/shard_map/ppermute | solution.py:63
  60.8 187.6 %collective-permute-start.31 = (bf16[1024,1024]{1,0:T(8,128)(2,1)}, bf16[1024,1024]{1,0:T(8,128)(2,1)}, u32[]{:S(2)}, u32[]{:S(2)}) collective-permute-start(bf16[1024,1024]{1,0:T(8,128)(2,1)} %collective-permute-done.23.refs_0_), channel_id=1, source_target_pairs={{0,8},{4,12},{8,24},{12,28},{24,16},{28,20},{16,0},{20,4},{1,9},{5... | collective-permute-start | bytes 6291464 | tf_op jit(solution)/shard_map/ppermute | solution.py:83
  224.4 103.3 %collective-permute-start.11 = (bf16[272,8192]{1,0:T(8,128)(2,1)}, bf16[272,8192]{1,0:T(8,128)(2,1)}, u32[]{:S(2)}, u32[]{:S(2)}) collective-permute-start(bf16[272,8192]{1,0:T(8,128)(2,1)} %fusion.2), channel_id=1, source_target_pairs={{1,2},{2,1},{5,6},{6,5},{9,10},{10,9},{13,14},{14,13},{17,18},{18,... | collective-permute-start | bytes 13369352 | tf_op jit(solution)/shard_map/ppermute | solution.py:63
  246.8 48.6 %collective-permute-start.37 = (bf16[1024,1024]{1,0:T(8,128)(2,1)}, bf16[1024,1024]{1,0:T(8,128)(2,1)S(1)}, u32[]{:S(2)}, u32[]{:S(2)}) collective-permute-start(bf16[1024,1024]{1,0:T(8,128)(2,1)} %collective-permute-done.23.refs_0_), channel_id=1, source_target_pairs={{0,16},{4,20},{8,0},{12,4},{24,8},{28,12},{16,24},{20,28},{1,17},{... | collective-permute-start | bytes 6291464 | tf_op jit(solution)/shard_map/ppermute | solution.py:83
  248.0 71.9 %collective-permute-start.2 = (bf16[1024,1536]{1,0:T(8,128)(2,1)}, bf16[1024,1536]{1,0:T(8,128)(2,1)}, u32[]{:S(2)}, u32[]{:S(2)}) collective-permute-start(bf16[1024,1536]{1,0:T(8,128)(2,1)} %collective-permute-done), channel_id=1, source_target_pairs={{0,8},{4,12},{8,24},{12,28},{24,16},{28,20},{16,0},{20,4},{1,9},{5... | collective-permute-start | bytes 9437192 | tf_op jit(solution)/shard_map/ppermute | solution.py:83
  248.3 114.5 %collective-permute-start.4 = (bf16[1024,1536]{1,0:T(8,128)(2,1)}, bf16[1024,1536]{1,0:T(8,128)(2,1)}, u32[]{:S(2)}, u32[]{:S(2)}) collective-permute-start(bf16[1024,1536]{1,0:T(8,128)(2,1)} %collective-permute-done), channel_id=1, source_target_pairs={{0,16},{4,20},{8,0},{12,4},{24,8},{28,12},{16,24},{20,28},{1,17},{... | collective-permute-start | bytes 9437192 | tf_op jit(solution)/shard_map/ppermute | solution.py:83
  264.5 151.8 %collective-permute-start.12 = (bf16[272,8192]{1,0:T(8,128)(2,1)}, bf16[272,8192]{1,0:T(8,128)(2,1)}, u32[]{:S(2)}, u32[]{:S(2)}) collective-permute-start(bf16[272,8192]{1,0:T(8,128)(2,1)} %collective-permute-done.10), channel_id=1, source_target_pairs={{1,2},{2,1},{5,6},{6,5},{9,10},{10,9},{13,14},{14,13},{17,18},{18,... | collective-permute-start | bytes 13369352 | tf_op jit(solution)/shard_map/ppermute | solution.py:63
  295.4 76.9 %collective-permute-start.1 = (bf16[1024,1536]{1,0:T(8,128)(2,1)}, bf16[1024,1536]{1,0:T(8,128)(2,1)S(1)}, u32[]{:S(2)}, u32[]{:S(2)}) collective-permute-start(bf16[1024,1536]{1,0:T(8,128)(2,1)} %collective-permute-done), channel_id=1, source_target_pairs={{0,4},{4,0},{8,12},{12,8},{16,20},{20,16},{24,28},{28,24},{1,5},{5... | collective-permute-start | bytes 9437192 | tf_op jit(solution)/shard_map/ppermute | solution.py:102
  320.0 116.4 %collective-permute-start.3 = (bf16[1024,1536]{1,0:T(8,128)(2,1)}, bf16[1024,1536]{1,0:T(8,128)(2,1)S(1)}, u32[]{:S(2)}, u32[]{:S(2)}) collective-permute-start(bf16[1024,1536]{1,0:T(8,128)(2,1)} %collective-permute-done.2), channel_id=1, source_target_pairs={{0,4},{4,0},{8,12},{12,8},{16,20},{20,16},{24,28},{28,24},{1,5},{5... | collective-permute-start | bytes 9437192 | tf_op jit(solution)/shard_map/ppermute | solution.py:102
  327.7 50.8 %collective-permute-start.6 = (bf16[512,1536]{1,0:T(8,128)(2,1)S(1)}, bf16[512,1536]{1,0:T(8,128)(2,1)S(1)}, u32[]{:S(2)}, u32[]{:S(2)}) collective-permute-start(bf16[512,1536]{1,0:T(8,128)(2,1)S(1)} %slice.72), channel_id=1, source_target_pairs={{0,8},{4,12},{8,24},{12,28},{24,16},{28,20},{16,0},{20,4},{1,9},{5... | collective-permute-start | bytes 4718600 | tf_op jit(solution)/shard_map/ppermute | solution.py:83
  362.9 79.5 %collective-permute-start.5 = (bf16[1024,1536]{1,0:T(8,128)(2,1)}, bf16[1024,1536]{1,0:T(8,128)(2,1)S(1)}, u32[]{:S(2)}, u32[]{:S(2)}) collective-permute-start(bf16[1024,1536]{1,0:T(8,128)(2,1)} %collective-permute-done.4), channel_id=1, source_target_pairs={{0,4},{4,0},{8,12},{12,8},{16,20},{20,16},{24,28},{28,24},{1,5},{5... | collective-permute-start | bytes 9437192 | tf_op jit(solution)/shard_map/ppermute | solution.py:102
  372.4 60.8 %collective-permute-start.7 = (bf16[512,1536]{1,0:T(8,128)(2,1)S(1)}, bf16[512,1536]{1,0:T(8,128)(2,1)}, u32[]{:S(2)}, u32[]{:S(2)}) collective-permute-start(bf16[512,1536]{1,0:T(8,128)(2,1)S(1)} %slice.73), channel_id=1, source_target_pairs={{0,16},{4,20},{8,0},{12,4},{24,8},{28,12},{16,24},{20,28},{1,17},{... | collective-permute-start | bytes 4718600 | tf_op jit(solution)/shard_map/ppermute | solution.py:83
  378.5 115.5 %collective-permute-start.13 = (f32[8,8]{1,0:T(8,128)S(1)}, f32[8,8]{1,0:T(8,128)S(1)}, u32[]{:S(2)}, u32[]{:S(2)}) collective-permute-start(f32[8,8]{1,0:T(8,128)S(1)} %bitcast.60), channel_id=1, source_target_pairs={{0,1},{3,2},{4,5},{7,6},{8,9},{11,10},{12,13},{15,14},{16,17},{19,... | collective-permute-start | bytes 776 | tf_op jit(solution)/shard_map/ppermute | solution.py:63
  416.3 32.3 %collective-permute-start.8 = (bf16[512,1536]{1,0:T(8,128)(2,1)S(1)}, bf16[512,1536]{1,0:T(8,128)(2,1)S(1)}, u32[]{:S(2)}, u32[]{:S(2)}) collective-permute-start(bf16[512,1536]{1,0:T(8,128)(2,1)S(1)} %collective-permute-done.6), channel_id=1, source_target_pairs={{0,4},{4,0},{8,12},{12,8},{16,20},{20,16},{24,28},{28,24},{1,5},{5... | collective-permute-start | bytes 4718600 | tf_op jit(solution)/shard_map/ppermute | solution.py:102
  433.2 62.0 %collective-permute-start.26 = (bf16[1024,1024]{1,0:T(8,128)(2,1)}, bf16[1024,1024]{1,0:T(8,128)(2,1)S(1)}, u32[]{:S(2)}, u32[]{:S(2)}) collective-permute-start(bf16[1024,1024]{1,0:T(8,128)(2,1)} %collective-permute-done.23.refs_0_), channel_id=1, source_target_pairs={{1,2},{2,1},{5,6},{6,5},{9,10},{10,9},{13,14},{14,13},{17,18},{18,... | collective-permute-start | bytes 6291464 | tf_op jit(solution)/shard_map/ppermute | solution.py:63
  442.4 53.2 %collective-permute-start.28 = (bf16[1024,1024]{1,0:T(8,128)(2,1)}, bf16[1024,1024]{1,0:T(8,128)(2,1)S(1)}, u32[]{:S(2)}, u32[]{:S(2)}) collective-permute-start(bf16[1024,1024]{1,0:T(8,128)(2,1)} %collective-permute-done.23.refs_0_), channel_id=1, source_target_pairs={{0,4},{4,0},{8,12},{12,8},{16,20},{20,16},{24,28},{28,24},{1,5},{5... | collective-permute-start | bytes 6291464 | tf_op jit(solution)/shard_map/ppermute | solution.py:102
  448.6 117.5 %collective-permute-start.29 = (bf16[1024,1024]{1,0:T(8,128)(2,1)}, bf16[1024,1024]{1,0:T(8,128)(2,1)}, u32[]{:S(2)}, u32[]{:S(2)}) collective-permute-start(bf16[1024,1024]{1,0:T(8,128)(2,1)} %broadcast_select_fusion.1.refs_1_), channel_id=1, source_target_pairs={{0,4},{4,0},{8,12},{12,8},{16,20},{20,16},{24,28},{28,24},{1,5},{5... | collective-permute-start | bytes 6291464 | tf_op jit(solution)/shard_map/ppermute | solution.py:102
  450.1 45.8 %collective-permute-start.43 = (bf16[512,1024]{1,0:T(8,128)(2,1)}, bf16[512,1024]{1,0:T(8,128)(2,1)S(1)}, u32[]{:S(2)}, u32[]{:S(2)}) collective-permute-start(bf16[512,1024]{1,0:T(8,128)(2,1)} %slice.84), channel_id=1, source_target_pairs={{0,8},{4,12},{8,24},{12,28},{24,16},{28,20},{16,0},{20,4},{1,9},{5... | collective-permute-start | bytes 3145736 | tf_op jit(solution)/shard_map/ppermute | solution.py:83
  494.0 76.2 %collective-permute-start.32 = (bf16[1024,1024]{1,0:T(8,128)(2,1)}, bf16[1024,1024]{1,0:T(8,128)(2,1)}, u32[]{:S(2)}, u32[]{:S(2)}) collective-permute-start(bf16[1024,1024]{1,0:T(8,128)(2,1)} %broadcast_select_fusion.1.refs_1_), channel_id=1, source_target_pairs={{0,8},{4,12},{8,24},{12,28},{24,16},{28,20},{16,0},{20,4},{1,9},{5... | collective-permute-start | bytes 6291464 | tf_op jit(solution)/shard_map/ppermute | solution.py:83
  495.3 75.6 %collective-permute-start.38 = (bf16[1024,1024]{1,0:T(8,128)(2,1)}, bf16[1024,1024]{1,0:T(8,128)(2,1)}, u32[]{:S(2)}, u32[]{:S(2)}) collective-permute-start(bf16[1024,1024]{1,0:T(8,128)(2,1)} %broadcast_select_fusion.1.refs_1_), channel_id=1, source_target_pairs={{0,16},{4,20},{8,0},{12,4},{24,8},{28,12},{16,24},{20,28},{1,17},{... | collective-permute-start | bytes 6291464 | tf_op jit(solution)/shard_map/ppermute | solution.py:83
  495.6 68.9 %collective-permute-start.44 = (bf16[512,1024]{1,0:T(8,128)(2,1)}, bf16[512,1024]{1,0:T(8,128)(2,1)}, u32[]{:S(2)}, u32[]{:S(2)}) collective-permute-start(bf16[512,1024]{1,0:T(8,128)(2,1)} %slice.85), channel_id=1, source_target_pairs={{0,16},{4,20},{8,0},{12,4},{24,8},{28,12},{16,24},{20,28},{1,17},{... | collective-permute-start | bytes 3145736 | tf_op jit(solution)/shard_map/ppermute | solution.py:83
  495.9 45.0 %collective-permute-start.27 = (bf16[1024,1024]{1,0:T(8,128)(2,1)S(1)}, bf16[1024,1024]{1,0:T(8,128)(2,1)S(1)}, u32[]{:S(2)}, u32[]{:S(2)}) collective-permute-start(bf16[1024,1024]{1,0:T(8,128)(2,1)S(1)} %collective-permute-done.26), channel_id=1, source_target_pairs={{1,0},{2,3},{5,4},{6,7},{9,8},{10,11},{13,12},{14,15},{17,16},{18,... | collective-permute-start | bytes 6291464 | tf_op jit(solution)/shard_map/ppermute | solution.py:63
  542.2 24.2 %collective-permute-start.14 = (bf16[16,144,128]{2,1,0:T(8,128)(2,1)}, bf16[16,144,128]{2,1,0:T(8,128)(2,1)}, u32[]{:S(2)}, u32[]{:S(2)}) collective-permute-start(bf16[16,144,128]{2,1,0:T(8,128)(2,1)} %fusion.9), channel_id=1, source_target_pairs={{0,4},{4,0},{8,12},{12,8},{16,20},{20,16},{24,28},{28,24},{1,5},{5... | collective-permute-start | bytes 1769480 | tf_op jit(solution)/shard_map/ppermute | solution.py:342
  566.1 47.6 %collective-permute-start.33 = (bf16[1024,1024]{1,0:T(8,128)(2,1)}, bf16[1024,1024]{1,0:T(8,128)(2,1)}, u32[]{:S(2)}, u32[]{:S(2)}) collective-permute-start(bf16[1024,1024]{1,0:T(8,128)(2,1)} %broadcast_select_fusion.refs_2_), channel_id=1, source_target_pairs={{0,8},{4,12},{8,24},{12,28},{24,16},{28,20},{16,0},{20,4},{1,9},{5... | collective-permute-start | bytes 6291464 | tf_op jit(solution)/shard_map/ppermute | solution.py:83
  566.5 48.0 %collective-permute-start.39 = (bf16[1024,1024]{1,0:T(8,128)(2,1)}, bf16[1024,1024]{1,0:T(8,128)(2,1)}, u32[]{:S(2)}, u32[]{:S(2)}) collective-permute-start(bf16[1024,1024]{1,0:T(8,128)(2,1)} %broadcast_select_fusion.refs_2_), channel_id=1, source_target_pairs={{0,16},{4,20},{8,0},{12,4},{24,8},{28,12},{16,24},{20,28},{1,17},{... | collective-permute-start | bytes 6291464 | tf_op jit(solution)/shard_map/ppermute | solution.py:83
  570.2 75.9 %collective-permute-start.40 = (bf16[1024,1024]{1,0:T(8,128)(2,1)}, bf16[1024,1024]{1,0:T(8,128)(2,1)S(1)}, u32[]{:S(2)}, u32[]{:S(2)}) collective-permute-start(bf16[1024,1024]{1,0:T(8,128)(2,1)} %copy-done.29), channel_id=1, source_target_pairs={{0,4},{4,0},{8,12},{12,8},{16,20},{20,16},{24,28},{28,24},{1,5},{5... | collective-permute-start | bytes 6291464 | tf_op jit(solution)/shard_map/ppermute | solution.py:102
  570.9 55.4 %collective-permute-start.15 = (bf16[16,144,128]{2,1,0:T(8,128)(2,1)S(1)}, bf16[16,144,128]{2,1,0:T(8,128)(2,1)S(1)}, u32[]{:S(2)}, u32[]{:S(2)}) collective-permute-start(bf16[16,144,128]{2,1,0:T(8,128)(2,1)S(1)} %fusion.14), channel_id=1, source_target_pairs={{0,8},{4,12},{8,0},{12,4},{16,24},{20,28},{24,16},{28,20},{1,9},{5... | collective-permute-start | bytes 1769480 | tf_op jit(solution)/shard_map/ppermute | solution.py:342
  585.9 61.8 %collective-permute-start.49 = (bf16[512,1024]{1,0:T(8,128)(2,1)S(1)}, bf16[512,1024]{1,0:T(8,128)(2,1)S(1)}, u32[]{:S(2)}, u32[]{:S(2)}) collective-permute-start(bf16[512,1024]{1,0:T(8,128)(2,1)S(1)} %copy-done.8), channel_id=1, source_target_pairs={{0,4},{4,0},{8,12},{12,8},{16,20},{20,16},{24,28},{28,24},{1,5},{5... | collective-permute-start | bytes 3145736 | tf_op jit(solution)/shard_map/ppermute | solution.py:102
  613.7 38.4 %collective-permute-start.50 = (bf16[512,1024]{1,0:T(8,128)(2,1)}, bf16[512,1024]{1,0:T(8,128)(2,1)S(1)}, u32[]{:S(2)}, u32[]{:S(2)}) collective-permute-start(bf16[512,1024]{1,0:T(8,128)(2,1)} %collective-permute-done.44.refs_19_), channel_id=1, source_target_pairs={{0,4},{4,0},{8,12},{12,8},{16,20},{20,16},{24,28},{28,24},{1,5},{5... | collective-permute-start | bytes 3145736 | tf_op jit(solution)/shard_map/ppermute | solution.py:102
  614.5 33.3 %collective-permute-start.45 = (bf16[512,1024]{1,0:T(8,128)(2,1)S(1)}, bf16[512,1024]{1,0:T(8,128)(2,1)S(1)}, u32[]{:S(2)}, u32[]{:S(2)}) collective-permute-start(bf16[512,1024]{1,0:T(8,128)(2,1)S(1)} %slice.86), channel_id=1, source_target_pairs={{0,8},{4,12},{8,24},{12,28},{24,16},{28,20},{16,0},{20,4},{1,9},{5... | collective-permute-start | bytes 3145736 | tf_op jit(solution)/shard_map/ppermute | solution.py:83
  626.3 23.7 %collective-permute-start.46 = (bf16[512,1024]{1,0:T(8,128)(2,1)S(1)}, bf16[512,1024]{1,0:T(8,128)(2,1)S(1)}, u32[]{:S(2)}, u32[]{:S(2)}) collective-permute-start(bf16[512,1024]{1,0:T(8,128)(2,1)S(1)} %slice.87), channel_id=1, source_target_pairs={{0,16},{4,20},{8,0},{12,4},{24,8},{28,12},{16,24},{20,28},{1,17},{... | collective-permute-start | bytes 3145736 | tf_op jit(solution)/shard_map/ppermute | solution.py:83
  646.1 62.3 %collective-permute-start.30 = (bf16[1024,1024]{1,0:T(8,128)(2,1)}, bf16[1024,1024]{1,0:T(8,128)(2,1)S(1)}, u32[]{:S(2)}, u32[]{:S(2)}) collective-permute-start(bf16[1024,1024]{1,0:T(8,128)(2,1)} %broadcast_select_fusion.refs_2_), channel_id=1, source_target_pairs={{0,4},{4,0},{8,12},{12,8},{16,20},{20,16},{24,28},{28,24},{1,5},{5... | collective-permute-start | bytes 6291464 | tf_op jit(solution)/shard_map/ppermute | solution.py:102
  647.7 100.2 %collective-permute-start.35 = (bf16[1024,1024]{1,0:T(8,128)(2,1)}, bf16[1024,1024]{1,0:T(8,128)(2,1)}, u32[]{:S(2)}, u32[]{:S(2)}) collective-permute-start(bf16[1024,1024]{1,0:T(8,128)(2,1)} %collective-permute-done.32.refs_7_), channel_id=1, source_target_pairs={{0,4},{4,0},{8,12},{12,8},{16,20},{20,16},{24,28},{28,24},{1,5},{5... | collective-permute-start | bytes 6291464 | tf_op jit(solution)/shard_map/ppermute | solution.py:102
  650.0 57.1 %collective-permute-start.52 = (bf16[512,1024]{1,0:T(8,128)(2,1)S(1)}, bf16[512,1024]{1,0:T(8,128)(2,1)}, u32[]{:S(2)}, u32[]{:S(2)}) collective-permute-start(bf16[512,1024]{1,0:T(8,128)(2,1)S(1)} %collective-permute-done.46.refs_21_), channel_id=1, source_target_pairs={{0,4},{4,0},{8,12},{12,8},{16,20},{20,16},{24,28},{28,24},{1,5},{5... | collective-permute-start | bytes 3145736 | tf_op jit(solution)/shard_map/ppermute | solution.py:102
  652.0 44.6 %collective-permute-start.16 = (bf16[16,144,128]{2,1,0:T(8,128)(2,1)}, bf16[16,144,128]{2,1,0:T(8,128)(2,1)S(1)}, u32[]{:S(2)}, u32[]{:S(2)}) collective-permute-start(bf16[16,144,128]{2,1,0:T(8,128)(2,1)} %fusion.8), channel_id=1, source_target_pairs={{0,16},{4,20},{8,24},{12,28},{16,0},{20,4},{24,8},{28,12},{1,17},{... | collective-permute-start | bytes 1769480 | tf_op jit(solution)/shard_map/ppermute | solution.py:342
  664.4 84.8 %collective-permute-start.47 = (bf16[512,1024]{1,0:T(8,128)(2,1)}, bf16[512,1024]{1,0:T(8,128)(2,1)}, u32[]{:S(2)}, u32[]{:S(2)}) collective-permute-start(bf16[512,1024]{1,0:T(8,128)(2,1)} %slice.88), channel_id=1, source_target_pairs={{0,8},{4,12},{8,24},{12,28},{24,16},{28,20},{16,0},{20,4},{1,9},{5... | collective-permute-start | bytes 3145736 | tf_op jit(solution)/shard_map/ppermute | solution.py:83
  696.6 55.7 %collective-permute-start.48 = (bf16[512,1024]{1,0:T(8,128)(2,1)S(1)}, bf16[512,1024]{1,0:T(8,128)(2,1)S(1)}, u32[]{:S(2)}, u32[]{:S(2)}) collective-permute-start(bf16[512,1024]{1,0:T(8,128)(2,1)S(1)} %copy-done.42), channel_id=1, source_target_pairs={{0,16},{4,20},{8,0},{12,4},{24,8},{28,12},{16,24},{20,28},{1,17},{... | collective-permute-start | bytes 3145736 | tf_op jit(solution)/shard_map/ppermute | solution.py:83
  707.1 46.8 %collective-permute-start.21 = (bf16[272,1024]{1,0:T(8,128)(2,1)S(1)}, bf16[272,1024]{1,0:T(8,128)(2,1)S(1)}, u32[]{:S(2)}, u32[]{:S(2)}) collective-permute-start(bf16[272,1024]{1,0:T(8,128)(2,1)S(1)} %get-tuple-element.35), channel_id=1, source_target_pairs={{1,3},{2,0},{5,7},{6,4},{9,11},{10,8},{13,15},{14,12},{17,19},{18,... | collective-permute-start | bytes 1671176 | tf_op jit(solution)/shard_map/ppermute | solution.py:63
  708.4 45.6 %collective-permute-start.22 = (bf16[272,1024]{1,0:T(8,128)(2,1)S(1)}, bf16[272,1024]{1,0:T(8,128)(2,1)S(1)}, u32[]{:S(2)}, u32[]{:S(2)}) collective-permute-start(bf16[272,1024]{1,0:T(8,128)(2,1)S(1)} %get-tuple-element.36), channel_id=1, source_target_pairs={{1,2},{2,1},{5,6},{6,5},{9,10},{10,9},{13,14},{14,13},{17,18},{18,... | collective-permute-start | bytes 1671176 | tf_op jit(solution)/shard_map/ppermute | solution.py:63
  749.2 24.9 %collective-permute-start.20 = (bf16[272,1024]{1,0:T(8,128)(2,1)S(1)}, bf16[272,1024]{1,0:T(8,128)(2,1)S(1)}, u32[]{:S(2)}, u32[]{:S(2)}) collective-permute-start(bf16[272,1024]{1,0:T(8,128)(2,1)S(1)} %get-tuple-element.34), channel_id=1, source_target_pairs={{1,2},{2,1},{5,6},{6,5},{9,10},{10,9},{13,14},{14,13},{17,18},{18,... | collective-permute-start | bytes 1671176 | tf_op jit(solution)/shard_map/ppermute | solution.py:63
  752.4 41.8 %collective-permute-start.41 = (bf16[1024,1024]{1,0:T(8,128)(2,1)}, bf16[1024,1024]{1,0:T(8,128)(2,1)}, u32[]{:S(2)}, u32[]{:S(2)}) collective-permute-start(bf16[1024,1024]{1,0:T(8,128)(2,1)} %collective-permute-done.38.refs_13_), channel_id=1, source_target_pairs={{0,4},{4,0},{8,12},{12,8},{16,20},{20,16},{24,28},{28,24},{1,5},{5... | collective-permute-start | bytes 6291464 | tf_op jit(solution)/shard_map/ppermute | solution.py:102
  753.9 40.3 %collective-permute-start.36 = (bf16[1024,1024]{1,0:T(8,128)(2,1)}, bf16[1024,1024]{1,0:T(8,128)(2,1)}, u32[]{:S(2)}, u32[]{:S(2)}) collective-permute-start(bf16[1024,1024]{1,0:T(8,128)(2,1)} %collective-permute-done.33.refs_8_), channel_id=1, source_target_pairs={{0,4},{4,0},{8,12},{12,8},{16,20},{20,16},{24,28},{28,24},{1,5},{5... | collective-permute-start | bytes 6291464 | tf_op jit(solution)/shard_map/ppermute | solution.py:102
  754.0 40.2 %collective-permute-start.42 = (bf16[1024,1024]{1,0:T(8,128)(2,1)}, bf16[1024,1024]{1,0:T(8,128)(2,1)}, u32[]{:S(2)}, u32[]{:S(2)}) collective-permute-start(bf16[1024,1024]{1,0:T(8,128)(2,1)} %collective-permute-done.39.refs_14_), channel_id=1, source_target_pairs={{0,4},{4,0},{8,12},{12,8},{16,20},{20,16},{24,28},{28,24},{1,5},{5... | collective-permute-start | bytes 6291464 | tf_op jit(solution)/shard_map/ppermute | solution.py:102
  (67 other events, 1777.2 us)
Sparse Core Ops, SparseCore 0:
  224.5 28.5 all-gather.2

commit v2 on v1

v2 whole, which is shorter than its diff:
```python
import functools

import jax
import jax.numpy as jnp
from jax import lax
from jax.experimental import pallas as pl
from jax.experimental.pallas import tpu as pltpu
from jax.sharding import PartitionSpec as P

HEAD = 128
EPSILON = 1e-05
SCALE = HEAD ** (-0.5)
LOG2E = 1.4426950408889634
STATE_ROWS = HEAD + 16
VMEM_LIMIT = 48 * 1024 * 1024
SMALL = pl.CostEstimate(flops=1, bytes_accessed=1, transcendentals=0)


def rms_rows(rows, norm_gain):
    widened = rows.astype(jnp.float32)
    scale_rows = lax.rsqrt(jnp.mean(widened * widened, axis=-1, keepdims=True) + EPSILON)
    return (widened * scale_rows * norm_gain.astype(jnp.float32)).astype(jnp.bfloat16)


def feature_map(inputs):
    return jnp.exp(jnp.minimum(inputs, 0.0)) + jnp.maximum(inputs, 0.0)


def tie(value, *others):
    return lax.optimization_barrier((value,) + others)[0]


def gate(*values):
    return lax.optimization_barrier(values)


class Planes:
    def __init__(self, count):
        self.count = count
        self.quarter = count // 4
        self.workers = range(self.quarter, 3 * self.quarter)
        self.ends = [i for i in range(count) if i not in self.workers]
        self.turns = range(1, count // 2)

    def partner(self, index):
        return index ^ self.quarter

    def peer(self, index, turn):
        return self.quarter + ((index - self.quarter) ^ turn)

    def lend(self):
        return [(e, self.partner(e)) for e in self.ends]

    def give_back(self):
        return [(w, self.partner(w)) for w in self.workers]

    def pairs(self):
        return [(i, self.partner(i)) for i in range(self.count)]

    def exchange(self, turn):
        return [(w, self.peer(w, turn)) for w in self.workers]

    def far_back(self, turn):
        return [(w, self.partner(self.peer(w, turn))) for w in self.workers]


def hop(block, pairs):
    return lax.ppermute(block, "tensor", pairs)


def seg_cycle(chips):
    half = chips // 2
    return list(range(half)) + list(range(chips - 1, half - 1, -1))


def swap_cores(block):
    return lax.ppermute(block, "seg", [(i, i ^ 1) for i in range(lax.axis_size("seg"))])


class ChipRing:
    def __init__(self, block):
        self.chips = lax.axis_size("seg") // 2
        self.cycle = seg_cycle(self.chips)
        self.block, self.right, self.left = block, [block], [block]
        for _ in range(1, self.chips // 2):
            self.right.append(self.step(self.right[-1], 1))
            self.left.append(self.step(self.left[-1], -1))

    def step(self, part, distance):
        route = [
            (self.cycle[i] * 2 + c, self.cycle[(i + distance) % self.chips] * 2 + c)
            for i in range(self.chips)
            for c in range(2)
        ]
        return lax.ppermute(part, "seg", route)

    def close(self):
        half = self.block.shape[0] // 2
        self.last = (self.step(self.right[-1][:half], 1), self.step(self.left[-1][half:], -1))
        return self.last

    def pieces(self):
        place_of = [self.cycle.index(c) for c in range(self.chips)]
        place = jnp.array(place_of, jnp.int32)[lax.axis_index("seg") // 2]
        table = jnp.array(self.cycle, jnp.int32)
        found = [((self.block,), 0)]
        for turn in range(1, self.chips // 2):
            found += [((self.right[turn],), -turn), ((self.left[turn],), turn)]
        found.append((self.last, self.chips // 2))
        return [(parts, table[(place + at + self.chips) % self.chips]) for parts, at in found]


def seg_all(values):
    size = lax.axis_size("seg")
    me = lax.axis_index("seg")
    bit = 1
    while bit < size:
        got = lax.ppermute(values, "seg", [(i, i ^ bit) for i in range(size)])
        upper = (me // bit) % 2 == 1
        values = jnp.concatenate(
            [jnp.where(upper, got, values), jnp.where(upper, values, got)], axis=0
        )
        bit *= 2
    return values


def pad_to(value, unit):
    return -(-value // unit) * unit


def pad_rows(array, unit=16):
    return jnp.pad(array, ((0, pad_to(array.shape[0], unit) - array.shape[0]), (0, 0)))


def nt_dot(a, b):
    return lax.dot_general(a, b, (((1,), (1,)), ((), ())), preferred_element_type=jnp.float32)


class Layout:
    def __init__(self, slots, rows, mem, groups):
        self.slots, self.rows, self.mem, self.groups = slots, rows, mem, groups
        self.stride, self.mem_stride = pad_to(rows, 16), pad_to(mem, 16)
        self.height = self.stride + self.mem_stride
        self.spread = slots * self.stride
        self.mem_spread = slots * self.mem_stride
        self.full = pad_to(self.spread, 128)
        self.wide = groups * HEAD
        self.unit = (groups + 2) * HEAD

    def valid(self, ids):
        return lax.rem(ids, self.stride) < self.rows

    def mem_valid(self, ids):
        return lax.rem(ids, self.mem_stride) < self.mem


def memory_kernel(lay, place_ref, *refs):
    slots, out_ref, key_all, value_all, mem_all = refs[: lay.slots], *refs[lay.slots :]
    wide = lay.wide
    for i, ref in enumerate(slots):
        start = pl.multiple_of(place_ref[i] * lay.stride, 16)
        key_all[pl.ds(start, lay.stride), :] = ref[: lay.stride, wide : wide + HEAD]
        value_all[pl.ds(start, lay.stride), :] = ref[: lay.stride, wide + HEAD :]
        start = pl.multiple_of(place_ref[i] * lay.mem_stride, 16)
        mem_all[pl.ds(start, lay.mem_stride), :] = ref[lay.stride :, :]
    k_tok, v_tok = key_all[...], value_all[...]
    k_mem, v_mem = mem_all[:, wide : wide + HEAD], mem_all[:, wide + HEAD :]
    mem = lay.mem_spread
    row_ids = lax.broadcasted_iota(jnp.int32, (mem, mem), 0)
    col_ids = lax.broadcasted_iota(jnp.int32, (mem, mem), 1)
    keep = row_ids >= col_ids
    feat = feature_map(k_mem.astype(jnp.float32))
    if lay.mem_stride != lay.mem:
        keep = keep & lay.mem_valid(col_ids)
        feat_ids = lax.broadcasted_iota(jnp.int32, (mem, HEAD), 0)
        feat = jnp.where(lay.mem_valid(feat_ids), feat, 0.0)
    feat_sum = jnp.sum(feat, axis=0, keepdims=True)
    feat_cast = feat.astype(jnp.bfloat16)
    for g in range(lay.groups):
        q = mem_all[:, g * HEAD : (g + 1) * HEAD]
        s_tok = nt_dot(q, k_tok)
        if lay.stride != lay.rows:
            ids = lax.broadcasted_iota(jnp.int32, (mem, lay.spread), 1)
            s_tok = jnp.where(lay.valid(ids), s_tok, -1e30)
        s_mem = jnp.where(keep, nt_dot(q, k_mem), -1e30)
        top = jnp.maximum(
            jnp.max(s_tok, axis=1, keepdims=True), jnp.max(s_mem, axis=1, keepdims=True)
        )
        p_tok = jnp.exp2((s_tok - top) * (SCALE * LOG2E))
        p_mem = jnp.exp2((s_mem - top) * (SCALE * LOG2E))
        total = jnp.sum(p_tok, axis=1, keepdims=True) + jnp.sum(p_mem, axis=1, keepdims=True)
        soft = jnp.dot(
            p_tok.astype(jnp.bfloat16), v_tok, preferred_element_type=jnp.float32
        ) + jnp.dot(p_mem.astype(jnp.bfloat16), v_mem, preferred_element_type=jnp.float32)
        soft = soft / total
        out_ref[g, :HEAD, :] = lax.dot_general(
            feat_cast,
            soft.astype(jnp.bfloat16),
            (((0,), (0,)), ((), ())),
            preferred_element_type=jnp.float32,
        )
        out_ref[g, HEAD:, :] = jnp.broadcast_to(feat_sum, (STATE_ROWS - HEAD, HEAD))


def read_state(query, state, sums):
    feat = feature_map(query.astype(jnp.float32)).astype(jnp.bfloat16)
    numerator = jnp.dot(feat, state.astype(jnp.bfloat16), preferred_element_type=jnp.float32)
    sums = jnp.broadcast_to(sums, (HEAD, HEAD)).astype(jnp.bfloat16)
    return numerator / (nt_dot(feat, sums) + 1.0)


def token_kernel(lay, begun, place_ref, *refs):
    count, stride, wide = lay.slots, lay.stride, lay.wide
    slots, refs = refs[:count], refs[count:]
    state_ref, refs = refs[0], refs[1 + begun :]
    outs, (query_all, key_all, value_all, out_all) = refs[:count], refs[count:]
    if lay.full > lay.spread:
        tail = (lay.full - lay.spread, HEAD)
        key_all[lay.spread :, :] = jnp.zeros(tail, key_all.dtype)
        value_all[lay.spread :, :] = jnp.zeros(tail, value_all.dtype)
    for i, ref in enumerate(slots):
        rows = pl.ds(pl.multiple_of(place_ref[i] * stride, 16), stride)
        query_all[rows, :] = ref[:stride, :wide]
        key_all[rows, :] = ref[:stride, wide : wide + HEAD]
        value_all[rows, :] = ref[:stride, wide + HEAD :]

    for block in range(count):
        first = block * stride
        low = first // 128 * 128
        high = min(pad_to(first + stride, 128), lay.full)
        k_diag, v_diag = key_all[low:high, :], value_all[low:high, :]
        row_ids = lax.broadcasted_iota(jnp.int32, (stride, high - low), 0) + first
        col_ids = lax.broadcasted_iota(jnp.int32, (stride, high - low), 1) + low
        keep = row_ids >= col_ids
        if stride != lay.rows:
            keep = keep & lay.valid(col_ids)

        def one_head(g, carry, first=first, low=low, k_diag=k_diag, v_diag=v_diag, keep=keep):
            lanes = pl.ds(pl.multiple_of(g * HEAD, HEAD), HEAD)
            q = query_all[first : first + stride, lanes]
            s_diag = jnp.where(keep, nt_dot(q, k_diag), -1e30)
            top = jnp.max(s_diag, axis=1, keepdims=True)
            if low > 0:
                s_prev = nt_dot(q, key_all[:low, :])
                if stride != lay.rows:
                    ids = lax.broadcasted_iota(jnp.int32, (stride, low), 1)
                    s_prev = jnp.where(lay.valid(ids), s_prev, -1e30)
                top = jnp.maximum(top, jnp.max(s_prev, axis=1, keepdims=True))
            p_diag = jnp.exp2((s_diag - top) * (SCALE * LOG2E))
            total = jnp.sum(p_diag, axis=1, keepdims=True)
            soft = jnp.dot(
                p_diag.astype(jnp.bfloat16), v_diag, preferred_element_type=jnp.float32
            )
            if low > 0:
                p_prev = jnp.exp2((s_prev - top) * (SCALE * LOG2E))
                total = total + jnp.sum(p_prev, axis=1, keepdims=True)
                soft = soft + jnp.dot(
                    p_prev.astype(jnp.bfloat16),
                    value_all[:low, :],
                    preferred_element_type=jnp.float32,
                )
            state, sums = state_ref[g, :HEAD, :], state_ref[g, HEAD : HEAD + 1, :]
            out_all[first : first + stride, lanes] = soft / total + read_state(q, state, sums)
            return carry

        lax.fori_loop(0, lay.groups, one_head, 0)

    for i, ref in enumerate(outs):
        rows = pl.ds(pl.multiple_of(place_ref[i] * stride, 16), stride)
        ref[...] = out_all[rows, :].astype(ref.dtype)


class Unit:
    def __init__(self, lay, places, slots, at=0):
        self.lay, self.places, self.slots, self.at = lay, places, slots, at

    def tied(self, *others):
        return Unit(self.lay, self.places, [tie(s, *others) for s in self.slots], self.at)

    def slot_specs(self):
        lay, at = self.lay, self.at
        return [pl.BlockSpec((lay.height, lay.unit), lambda i, *_: (0, at))] * lay.slots

    def state_spec(self):
        return pl.BlockSpec((self.lay.groups, STATE_ROWS, HEAD), lambda i, *_: (0, 0, 0))

    def memory_write(self):
        lay = self.lay
        return pl.pallas_call(
            functools.partial(memory_kernel, lay),
            grid_spec=pltpu.PrefetchScalarGridSpec(
                num_scalar_prefetch=1,
                grid=(1,),
                in_specs=self.slot_specs(),
                out_specs=self.state_spec(),
                scratch_shapes=[
                    pltpu.VMEM((lay.spread, HEAD), jnp.bfloat16),
                    pltpu.VMEM((lay.spread, HEAD), jnp.bfloat16),
                    pltpu.VMEM((lay.mem_spread, lay.unit), jnp.bfloat16),
                ],
            ),
            out_shape=jax.ShapeDtypeStruct((lay.groups, STATE_ROWS, HEAD), jnp.float32),
            compiler_params=pltpu.CompilerParams(vmem_limit_bytes=VMEM_LIMIT),
            cost_estimate=SMALL,
            name="memory_write",
        )(self.places, *self.slots)

    def attend(self, state, block=0, blocks=1, begun=()):
        lay = self.lay
        out_spec = pl.BlockSpec((lay.stride, lay.wide), lambda i, *_: (0, block))
        return list(
            pl.pallas_call(
                functools.partial(token_kernel, lay, len(begun)),
                grid_spec=pltpu.PrefetchScalarGridSpec(
                    num_scalar_prefetch=1,
                    grid=(1,),
                    in_specs=self.slot_specs()
                    + [self.state_spec()]
                    + [pl.BlockSpec(memory_space=pl.ANY)] * len(begun),
                    out_specs=[out_spec] * lay.slots,
                    scratch_shapes=[
                        pltpu.VMEM((lay.spread, lay.wide), jnp.bfloat16),
                        pltpu.VMEM((lay.full, HEAD), jnp.bfloat16),
                        pltpu.VMEM((lay.full, HEAD), jnp.bfloat16),
                        pltpu.VMEM((lay.spread, lay.wide), jnp.float32),
                    ],
                ),
                out_shape=[jax.ShapeDtypeStruct((lay.stride, blocks * lay.wide), jnp.bfloat16)]
                * lay.slots,
                input_output_aliases={2 + lay.slots + i: i for i in range(len(begun))},
                compiler_params=pltpu.CompilerParams(vmem_limit_bytes=VMEM_LIMIT),
                cost_estimate=SMALL,
                name="token_attention",
            )(self.places, *self.slots, state, *begun)
        )


def relay(writes, rates, works):
    size = lax.axis_size("seg")
    me = lax.axis_index("seg")
    ids = lax.broadcasted_iota(jnp.int32, (size, 1), 0)

    def product(mask):
        return jnp.prod(jnp.where(mask, rates, 1.0), axis=0)[:, None, None]

    total = writes
    prefix = jnp.zeros_like(writes)
    results = []
    bit = 1
    while bit < size:
        route = [(i, i ^ bit) for i in range(size)]
        sent = total.astype(jnp.bfloat16)
        got = lax.ppermute(sent, "seg", route)
        if len(results) < len(works):
            results.append(works[len(results)](sent))
            got = tie(got, results[-1])
        got = got.astype(jnp.float32)
        mine = ids // bit == me // bit
        theirs = ids // bit == (me // bit) ^ 1
        upper = (me // bit) % 2 == 1
        prefix = jnp.where(upper, product(mine & (ids < me)) * got + prefix, prefix)
        total = jnp.where(upper, product(mine) * got + total, product(theirs) * total + got)
        bit *= 2
    for work in works[len(results) :]:
        results.append(work(prefix))
    return prefix, results


def output_kernel(plan, bufs, picks, final, ids_ref, mixed_ref, other_ref, own_ref, *refs):
    count = 1 + max(p for row in plan for parts in row if parts is not None for p in parts)
    piece_refs, refs = refs[:count], refs[count:]
    if final:
        base_ref, begun_ref, out_ref, far_ref, weights, total, sems = refs
    else:
        out_ref, weights, total, sems = refs
    rows = mixed_ref.shape[1]
    blocks, groups = len(plan), len(plan[0])
    width = weights.shape[2]
    c, g = pl.program_id(0), pl.program_id(1)
    step = c * groups + g
    steps = blocks * groups

    def start(at):
        slot = lax.rem(at, bufs)
        for b in range(blocks):
            for j in range(groups):

                @pl.when(at == b * groups + j)
                def _():
                    if plan[b][j] is None:
                        columns = pl.ds(pl.multiple_of(ids_ref[b] * width, 128), width)
                        pltpu.make_async_copy(
                            own_ref.at[:, columns], weights.at[slot], sems.at[slot]
                        ).start()
                        return
                    row = 0
                    for index in plan[b][j]:
                        part = piece_refs[index]
                        high = part.shape[0]
                        pltpu.make_async_copy(
                            part, weights.at[slot, pl.ds(row, high), :], sems.at[slot]
                        ).start()
                        row += high

    @pl.when(step == 0)
    def _():
        for at in range(min(bufs - 1, steps)):
            start(jnp.int32(at))

    @pl.when(step + bufs - 1 < steps)
    def _():
        start(step + bufs - 1)

    slot = lax.rem(step, bufs)
    pltpu.make_async_copy(weights.at[slot], weights.at[slot], sems.at[slot]).wait()
    both = jnp.concatenate([mixed_ref[picks + g], other_ref[picks + g]], axis=0)
    term = jnp.dot(both, weights[slot], preferred_element_type=jnp.float32)

    @pl.when(g == 0)
    def _():
        total[...] = term + begun_ref[0] if final else term

    @pl.when(g > 0)
    def _():
        total[...] = total[...] + term

    @pl.when(g == groups - 1)
    def _():
        if final:
            base = base_ref[...].astype(jnp.float32)
            out_ref[...] = (base + total[:rows, :]).astype(out_ref.dtype)
            far_ref[...] = total[rows:, :].astype(far_ref.dtype)
        else:
            out_ref[0] = total[...]


def output_product(mixed, other, tokens, w_out, gathered, begun=None):
    count, rows, depth = mixed.shape
    final = begun is not None
    blocks = len(gathered[0])
    width = w_out.shape[1] // (2 * blocks)
    chips = jnp.stack([gathered[0][b][1] for b in range(blocks)]).astype(jnp.int32)
    ids = (lax.axis_index("seg") % 2) * blocks + chips
    plan, pieces = [], []
    for b in range(blocks):
        row = [] if final else [None]
        for pieces_of in gathered:
            parts = pieces_of[b][0]
            row.append(tuple(range(len(pieces), len(pieces) + len(parts))))
            pieces += parts
        plan.append(row)
    groups = len(plan[0])
    picks = count - groups if final else 0
    bufs = 4
    whole = pl.BlockSpec((rows, width), lambda c, g, ids: (0, ids[c]))
    half = pl.BlockSpec((rows, width), lambda c, g, ids: (0, lax.rem(ids[c], blocks)))
    sums = pl.BlockSpec((1, 2 * rows, width), lambda c, g, ids: (c, 0, 0))
    mixed_spec = pl.BlockSpec((count, rows, depth), lambda c, g, ids: (0, 0, 0))
    if final:
        shapes = [
            jax.ShapeDtypeStruct((rows, w_out.shape[1]), jnp.bfloat16),
            jax.ShapeDtypeStruct((rows, w_out.shape[1] // 2), jnp.bfloat16),
        ]
    else:
        shapes = jax.ShapeDtypeStruct((blocks, 2 * rows, width), jnp.float32)
    return pl.pallas_call(
        functools.partial(output_kernel, plan, bufs, picks, final),
        grid_spec=pltpu.PrefetchScalarGridSpec(
            num_scalar_prefetch=1,
            grid=(blocks, groups),
            in_specs=[mixed_spec] * 2
            + [pl.BlockSpec(memory_space=pl.ANY)] * (1 + len(pieces))
            + ([whole, sums] if final else []),
            out_specs=[whole, half] if final else sums,
            scratch_shapes=[
                pltpu.VMEM((bufs, depth, width), jnp.bfloat16),
                pltpu.VMEM((2 * rows, width), jnp.float32),
                pltpu.SemaphoreType.DMA((bufs,)),
            ],
        ),
        out_shape=shapes,
        compiler_params=pltpu.CompilerParams(vmem_limit_bytes=VMEM_LIMIT),
        cost_estimate=SMALL,
        name="output_product",
    )(ids, mixed, other, w_out, *pieces, *((tokens, begun) if final else ()))


def project_kernel(heights, parts, kv_heads, *refs):
    pieces = [ref for ref in refs[: sum(map(len, heights))]]
    refs = refs[len(pieces) :]
    weights, outs = refs[:parts], refs[parts : parts + len(heights)]
    totals = refs[parts + len(heights) :]
    step, steps = pl.program_id(0), pl.num_programs(0)
    x = [ref[...] for ref in pieces]
    x = x[0] if len(x) == 1 else jnp.concatenate(x, axis=0)
    for weight, total in zip(weights, totals):
        term = jnp.dot(x, weight[...], preferred_element_type=jnp.float32)

        @pl.when(step == 0)
        def _():
            total[...] = term

        @pl.when(step > 0)
        def _():
            total[...] = total[...] + term

    @pl.when(step == steps - 1)
    def _():
        height = sum(heights[0])
        for i, out in enumerate(outs):
            rows = slice(i * height, (i + 1) * height)
            start = 0
            for h in range(kv_heads):
                for total in totals:
                    width = total.shape[1] // kv_heads
                    part = total[rows, h * width : (h + 1) * width]
                    out[:, start : start + width] = part.astype(out.dtype)
                    start += width


def project(slots, weights, kv_heads=1):
    heights = [[x.shape[0] for x in slot] for slot in slots]
    depth = slots[0][0].shape[1]
    block = depth // 8
    widths = [w.shape[1] for w in weights]
    shape = jax.ShapeDtypeStruct((sum(heights[0]), sum(widths)), jnp.bfloat16)
    rows = sum(map(sum, heights))
    return list(
        pl.pallas_call(
            functools.partial(project_kernel, heights, len(weights), kv_heads),
            grid=(depth // block,),
            in_specs=[pl.BlockSpec((h, block), lambda k: (0, k)) for hs in heights for h in hs]
            + [pl.BlockSpec((block, width), lambda k: (k, 0)) for width in widths],
            out_specs=[pl.BlockSpec(shape.shape, lambda k: (0, 0))] * len(slots),
            out_shape=[shape] * len(slots),
            scratch_shapes=[pltpu.VMEM((rows, w), jnp.float32) for w in widths],
            compiler_params=pltpu.CompilerParams(vmem_limit_bytes=VMEM_LIMIT),
            cost_estimate=SMALL,
            name="project",
        )(*sum(map(list, slots), []), *weights)
    )


def per_device(tokens, memory_embed, norm_gain, w_query, w_key, value_weight, w_out, retain):
    planes = Planes(lax.axis_size("tensor"))
    turns = list(planes.turns)
    me = lax.axis_index("tensor")
    seg, seg_count = lax.axis_index("seg"), lax.axis_size("seg")
    core, chip, chips = seg % 2, seg // 2, seg_count // 2
    is_end = (me < planes.quarter) | (me >= 3 * planes.quarter)
    worker = jnp.where(is_end, planes.partner(me), me)
    heads, kv_heads = w_query.shape[1] // HEAD, w_key.shape[1] // HEAD
    groups = heads // kv_heads
    lay = Layout(planes.count, tokens.shape[0], memory_embed.shape[0], groups)
    back, lend = planes.give_back(), planes.lend()

    depth = w_query.shape[0] // seg_count

    lent_shares = []
    for h in range(kv_heads):
        cuts = []
        for array, wide in ((w_query, lay.wide), (w_key, HEAD), (value_weight, HEAD)):
            cuts.append(lax.dynamic_slice(array, (seg * depth, h * wide), (depth, wide)))
        lent_shares.append(jnp.concatenate(cuts, axis=1))
    half = w_out.shape[1] // 2
    width = half // chips
    share = lax.dynamic_slice_in_dim(w_out, core * half + chip * width, width, 1)

    places = [me, planes.partner(me)]
    for turn in turns:
        peer = planes.peer(worker, turn)
        places += [peer, planes.partner(peer)]
    places = jnp.stack(places).astype(jnp.int32)
    own_weights = [w_query, w_key, value_weight]
    numbers = [0, 1] + [2 + 2 * at for at in range(len(turns))]
    far_numbers = [3 + 2 * at for at in range(len(turns))]
    half_rows = lay.height // 2
    own, taken = {}, [{} for _ in range(kv_heads)]

    lent = [hop(lent_shares[0], lend)]
    peers = [hop(share, planes.exchange(turn)) for turn in turns]
    near_back = hop(share, back)
    rates = jnp.concatenate([retain, hop(retain, lend)], axis=1)
    gain = tie(norm_gain, share, lent_shares)
    rows = jnp.concatenate(
        [pad_rows(rms_rows(tokens, gain)), pad_rows(rms_rows(memory_embed, gain))], axis=0
    )
    lent, peers, near_back, rows, share, lent_shares, rates = gate(
        lent, peers, near_back, rows, share, lent_shares, rates
    )

    lent_all = [lax.all_gather(lent[0], "seg", axis=0, tiled=True)]
    rows_a = hop(rows, lend)
    near_rows = [hop(rows, planes.exchange(turn)) for turn in turns]
    rings = [ChipRing(jnp.where(is_end, near_back, peers[0]))]
    (own[0],) = project([[rows]], own_weights, kv_heads)
    rates = seg_all(tie(rates, own[0]))
    held = (rings[0].right, rings[0].left)
    rows_a, near_rows, held, own, rows, share, lent_shares, peers, rates = gate(
        rows_a, near_rows, held, own, rows, share, lent_shares, peers, rates
    )
    rings[0].right, rings[0].left = held

    lent += [hop(part, lend) for part in lent_shares[1:]]
    far_rows = [[hop(rows_a[:half_rows], planes.exchange(turn))] for turn in turns]
    ends = [hop(piece, back) for piece in peers]
    closed = rings[0].close()
    known = [[rows], [rows_a]] + [[x] for x in near_rows]
    own.update(zip(numbers[1:], project(known[1:], own_weights, kv_heads)))
    lent, far_rows, ends, rings[0].last, own, known, lent_all, share, rows_a = gate(
        lent, far_rows, ends, closed, own, known, lent_all, share, rows_a
    )

    lent_all += [lax.all_gather(part, "seg", axis=0, tiled=True) for part in lent[1:]]
    for parts, turn in zip(far_rows, turns):
        parts.append(hop(rows_a[half_rows:], planes.exchange(turn)))
    near = hop(share, lend)
    taken[0].update(zip(numbers, project(known, [lent_all[0]])))
    far_rows, near, taken, known, ends = gate(far_rows, near, taken, known, ends)

    far_near = [hop(near, planes.exchange(turn)) for turn in turns]
    for end, mid in zip(ends, peers[1:] + [near]):
        rings.append(ChipRing(jnp.where(is_end, end, mid)))
    own.update(zip(far_numbers, project(far_rows, own_weights, kv_heads)))
    order = range(planes.count)
    own_slots = [own[slot] for slot in order]
    own_units = [Unit(lay, places, own_slots, h) for h in range(kv_heads)]
    writes = jnp.concatenate([u.memory_write() for u in own_units], axis=0)

    def first_lent(dep):
        taken[0].update(zip(far_numbers, project([tie(x, dep) for x in far_rows], [lent_all[0]])))
        return taken[0][far_numbers[-1]]

    def other_lent(dep, h):
        part = tie(lent_all[h], dep)
        taken[h].update(zip(numbers + far_numbers, project(known + far_rows, [part])))
        return taken[h][far_numbers[-1]]

    works = [first_lent]
    works += [functools.partial(other_lent, h=h) for h in range(1, kv_heads)]
    state, _ = relay(writes, rates[:, :heads], works)

    held = [(ring.right, ring.left) for ring in rings[1:]]
    far_near, own_slots, taken, held, state = gate(far_near, own_slots, taken, held, state)
    for ring, (right, left) in zip(rings[1:], held):
        ring.right, ring.left = right, left
        ring.close()
    backs = [hop(piece, back) for piece in far_near]
    own_units = [Unit(lay, places, own_slots, h) for h in range(kv_heads)]
    lent_units = [Unit(lay, places, [part[slot] for slot in order]) for part in taken]
    writes = jnp.concatenate([u.memory_write() for u in lent_units], axis=0)
    mixed_own = []

    def attend_own(dep, h):
        unit = own_units[h].tied(dep)
        mixed_own[:] = unit.attend(state[h * groups : (h + 1) * groups], h, kv_heads, mixed_own)
        return mixed_own

    works = [functools.partial(attend_own, h=h) for h in range(kv_heads)]
    lent_state, _ = relay(writes, rates[:, heads:], works)

    last = rings[-1].last
    lent_state, mixed_own, backs, last = gate(lent_state, list(mixed_own), backs, last)
    rings[-1].last = last
    late = len(rings)
    for mid, end in zip(far_near, backs):
        rings.append(ChipRing(tie(jnp.where(is_end, end, mid), last)))

    def cross(arrays):
        return (
            arrays[0],
            hop(arrays[1], back),
            [hop(arrays[2 + 2 * at], planes.exchange(turn)) for at, turn in enumerate(turns)],
            [hop(arrays[3 + 2 * at], planes.far_back(turn)) for at, turn in enumerate(turns)],
        )

    crossed = [cross(mixed_own)]
    for h, unit in enumerate(lent_units):
        crossed.append(cross(unit.tied(lent_state).attend(lent_state[h * groups : (h + 1) * groups])))

    def join(arrays):
        both = jnp.concatenate(arrays, axis=1)
        return both[:, : heads * HEAD], both[:, heads * HEAD :]

    home = join([c[0] for c in crossed])
    returned = join([c[1] for c in crossed])
    near_mixed = [join([c[2][at] for c in crossed]) for at in range(len(turns))]
    far_mixed = [join([c[3][at] for c in crossed]) for at in range(len(turns))]
    ends = [returned[1], returned[0]] + [m[0] for m in far_mixed] + [m[1] for m in far_mixed]
    mids = [home[0]] + [m[0] for m in near_mixed] + [home[1]] + [m[1] for m in near_mixed]
    mixed = jnp.stack([jnp.where(is_end, e, m) for e, m in zip(ends, mids)])

    held = [(ring.right, ring.left) for ring in rings[late:]]
    mixed, held = gate(mixed, held)
    for ring, (right, left) in zip(rings[late:], held):
        ring.right, ring.left = right, left
        ring.close()
    gathered = [ring.pieces() for ring in rings]
    other = swap_cores(mixed)
    base = pad_rows(tokens)
    begun = output_product(mixed, other, base, w_out, gathered[:late])
    result, other = output_product(mixed, other, base, w_out, gathered[late:], begun)
    other = swap_cores(other)
    start = (1 - core) * half
    base = lax.dynamic_slice_in_dim(base, start, half, 1)
    other = (base.astype(jnp.float32) + other.astype(jnp.float32)).astype(jnp.bfloat16)
    result = lax.dynamic_update_slice_in_dim(result, other, start, 1)
    return result[: tokens.shape[0]]


def solution(mesh):
    return jax.shard_map(
        per_device,
        mesh=mesh,
        in_specs=(
            P(("seg", "tensor"), None),
            P("tensor", None),
            P(),
            P(None, "tensor"),
            P(None, "tensor"),
            P(None, "tensor"),
            P("tensor", None),
            P("seg", "tensor"),
        ),
        out_specs=P(("seg", "tensor"), None),
        check_vma=False,
    )
```

time: 851 us -> 586 us (0.69)
  blocking collectives: 175 us -> 0 us
  matrix products: 135 us -> 0 us
  Pallas kernels: 120 us -> 212 us
  waiting for transfers between devices: 233 us -> 196 us
  local copies, waits for them, and re-layouts: 53.3 us -> 41.6 us
    all_gather x2 -> x0, blocking collectives: 175 us -> none  [the longest x1 162 us: per_device(): mem_all = lax.all_gather(mem_slice, 'tensor', axis=0, tiled=True)]
    dot_general x16 -> x0, matrix products: 135 us -> none  [dot_cast(): jnp.dot(a, b, preferred_element_type=jnp.float32).astype(jnp.bfloat16)]
    ppermute x16 -> x12, waiting for transfers between devices: 102 us -> 0.03 us  [step(): return lax.ppermute(part, 'seg', route)]
    pallas_call x7 -> x16, Pallas kernels: 120 us -> 212 us  [the longest x6 111 us: project(): pl.pallas_call(functools.partial(project_kernel, heights, len(weights), k...]
    ppermute x23 -> x11, waiting for transfers between devices: 11.1 us -> 78.3 us  [the longest x3 53.9 us: seg_all(): got = lax.ppermute(values, 'seg', [(i, i ^ bit) for i in range(size)])]
    dynamic_update_slice x10 -> x0, local copies, waits for them, and re-layouts: 22.1 us -> none  [per_device(): lent_all = lax.dynamic_update_slice(lent_all, part, (start, 0))]
    unnamed x118 -> x112, local copies, waits for them, and re-layouts: 5.85 us -> 16 us
    ppermute x16 -> x22, starting transfers between devices: 40.4 us -> 49.4 us  [hop(): return lax.ppermute(block, 'tensor', pairs)]
  transfers between devices with their start and end apart: 56 -> 47, of which waited for: 13 -> 20; matrix products, arithmetic and copies ran while one was open for 24% -> 8% of each run, Pallas kernels for 10% -> 35%
where the time goes in v2:
time: 586 us; the launch traced here: 577 us
  Pallas kernels  212 us (36%)
  waiting for transfers between devices  196 us (33%)
  starting transfers between devices  80.6 us (14%)
  local copies, waits for them, and re-layouts  41.6 us (7%)
  other arithmetic  28.7 us (5%)
  between operations  17.5 us (3%)
    ppermute x22, waiting for transfers between devices, hop(): return lax.ppermute(block, 'tensor', pairs)  118 us
    pallas_call x6, Pallas kernels, project(): pl.pallas_call(functools.partial(project_kernel, heights, len(weights), k...  111 us
    ppermute x3, waiting for transfers between devices, seg_all(): got = lax.ppermute(values, 'seg', [(i, i ^ bit) for i in range(size)])  53.9 us
    pallas_call x4, Pallas kernels, attend(): pl.pallas_call(functools.partial(token_kernel, lay, len(begun)), grid_spe...  52.9 us
    ppermute x22, starting transfers between devices, hop(): return lax.ppermute(block, 'tensor', pairs)  49.4 us
    pallas_call x2, Pallas kernels, output_product(): pl.pallas_call(functools.partial(output_kernel, plan, bufs, picks, final)...  37.5 us
    ppermute x6, waiting for transfers between devices, relay(): got = lax.ppermute(sent, 'seg', route)  20.3 us
    unnamed x112, local copies, waits for them, and re-layouts  16 us
  transfers between devices with their start and end apart: 47, of which 20 were waited for; matrix products, arithmetic and copies ran while one was open for 8% of the time, Pallas kernels for 35%

profile of v2, /device:TPU:9, one launch (start us, length us, event | category | flops | bytes accessed | tf_op | source)
XLA Modules:
  0.0 577.3 jit_solution(5876787414046072565)
XLA Ops:
  6.5 3.1 constant_dynamic-slice_fusion
  9.6 3.2 collective-permute-start.1
  26.8 27.8 %collective-permute-done.3 = f32[1,8]{1,0:T(1,128)S(1)} collective-permute-done((f32[1,8]{1,0:T(1,128)S(1)}, f32[1,8]{1,0:T(1,128)S(1)}, u32[]{:S(2)}, u32[]{:S(2)}) %collective-permute-start.3) | collective-permute-done | bytes 64 | tf_op jit(solution)/shard_map/ppermute | solution.py:68
  54.7 3.6 collective-permute-done.1
  60.1 3.9 collective-permute-start.5
  69.6 17.3 %project.6.refs_0_ = bf16[288,1536]{1,0:T(8,128)(2,1)S(1)} custom-call(bf16[288,8192]{1,0:T(8,128)(2,1)} %pad_maximum_fusion.refs_0_, bf16[8192,1024]{1,0:T(8,128)(2,1)} %refs_2_.5, bf16[8192,256]{1,0:T(8,128)(2,1)S(1)} %copy-done.1, bf16[8192,256]{1,0:T(8,128)(2,1)} %refs_4_.3), custom_call_target="tpu_custom_call" | custom-call | flops 1 | bytes 1 | tf_op jit(solution)/shard_map/project/pallas_call | solution.py:529
  87.0 3.0 collective-permute-start.8
  92.1 50.2 %collective-permute-done.9 = f32[2,16]{1,0:T(2,128)S(1)} collective-permute-done((f32[2,16]{1,0:T(2,128)S(1)}, f32[2,16]{1,0:T(2,128)S(1)}, u32[]{:S(2)}, u32[]{:S(2)}) %collective-permute-start.9) | collective-permute-done | bytes 160 | tf_op jit(solution)/shard_map/ppermute | solution.py:118
  142.4 2.8 collective-permute-done.10
  145.3 17.5 %collective-permute-done.4.refs_0_.refs_1_ = bf16[288,8192]{1,0:T(8,128)(2,1)} collective-permute-done((bf16[288,8192]{1,0:T(8,128)(2,1)}, bf16[288,8192]{1,0:T(8,128)(2,1)}, u32[]{:S(2)}, u32[]{:S(2)}) %collective-permute-start.4) | collective-permute-done | bytes 4718624 | tf_op jit(solution)/shard_map/ppermute | solution.py:68
  164.9 3.4 slice.42
  168.4 3.1 collective-permute-start.12
  179.5 28.2 %project.7 = (bf16[288,1536]{1,0:T(8,128)(2,1)S(1)}, bf16[288,1536]{1,0:T(8,128)(2,1)S(1)}) custom-call(bf16[288,8192]{1,0:T(8,128)(2,1)} %collective-permute-done.4.refs_0_.refs_1_, bf16[288,8192]{1,0:T(8,128)(2,1)} %collective-permute-done.5.refs_1_.refs_2_, bf16[8192,1024]{1,0:T(8,128)(2,1)} %refs_2_.5, bf16[8192,256]{1,0:T(8,128)(2,1)S(1)} %copy-done.2, ...), custom_call_target="tpu_custom_call" | custom-call | flops 1 | bytes 1 | tf_op jit(solution)/shard_map/project/pallas_call | solution.py:529
  211.6 3.9 collective-permute-done.13
  215.5 5.5 collective-permute-done.12.refs_0_.refs_3_
  221.0 4.1 slice.45
  225.2 2.8 collective-permute-start.16
  229.4 2.8 copy-done
  232.3 16.9 %project.8 = (bf16[288,768]{1,0:T(8,128)(2,1)S(1)}, bf16[288,768]{1,0:T(8,128)(2,1)S(1)}, bf16[288,768]{1,0:T(8,128)(2,1)S(1)}) custom-call(bf16[288,8192]{1,0:T(8,128)(2,1)S(1)} %copy-done, bf16[288,8192]{1,0:T(8,128)(2,1)} %collective-permute-done.4.refs_0_.refs_1_, bf16[288,8192]{1,0:T(8,128)(2,1)} %collective-permute-done.5.refs_1_.refs_2_, ...), custom_call_target="tpu_custom_call" | custom-call | flops 1 | bytes 1 | tf_op jit(solution)/shard_map/project/pallas_call | solution.py:529
  250.7 22.9 %collective-permute-done.17 = bf16[1024,1024]{1,0:T(8,128)(2,1)} collective-permute-done((bf16[1024,1024]{1,0:T(8,128)(2,1)}, bf16[1024,1024]{1,0:T(8,128)(2,1)}, u32[]{:S(2)}, u32[]{:S(2)}) %collective-permute-start.17) | collective-permute-done | bytes 2097184 | tf_op jit(solution)/shard_map/ppermute | solution.py:68
  273.6 3.4 collective-permute-done.16.refs_1_.refs_4_
  277.0 3.4 broadcast_select_fusion.1.refs_1_
  284.5 17.3 %project.9.refs_3_ = bf16[288,1536]{1,0:T(8,128)(2,1)S(1)} custom-call(bf16[144,8192]{1,0:T(8,128)(2,1)S(1)} %copy-done.4, bf16[144,8192]{1,0:T(8,128)(2,1)} %collective-permute-done.16.refs_1_.refs_4_, bf16[8192,1024]{1,0:T(8,128)(2,1)} %refs_2_.5, bf16[8192,256]{1,0:T(8,128)(2,1)} %refs_3_.5, bf16[8192,256]{1,0:T(8,128)(2,1)} %refs_4_.3), custom_call_target="tpu_custom_call" | custom-call | flops 1 | bytes 1 | tf_op jit(solution)/shard_map/project/pallas_call | solution.py:529
  301.9 2.8 memory_write.4
  304.6 2.8 memory_write.5
  307.4 5.3 collective-permute-start.19
  313.4 10.1 %project.10.refs_3_ = bf16[288,768]{1,0:T(8,128)(2,1)S(1)} custom-call(bf16[144,8192]{1,0:T(8,128)(2,1)S(1)} %copy-done.4, bf16[144,8192]{1,0:T(8,128)(2,1)} %collective-permute-done.16.refs_1_.refs_4_, bf16[8192,768]{1,0:T(8,128)(2,1)} %all-gather.3.cloned.1.call-done.refs_3_.refs_2_), custom_call_target="tpu_custom_call" | custom-call | flops 1 | bytes 1 | tf_op jit(solution)/shard_map/project/pallas_call | solution.py:529
  327.4 21.3 %project.11 = (bf16[288,768]{1,0:T(8,128)(2,1)S(1)}, bf16[288,768]{1,0:T(8,128)(2,1)S(1)}, bf16[288,768]{1,0:T(8,128)(2,1)S(1)}, bf16[288,768]{1,0:T(8,128)(2,1)S(1)}) custom-call(bf16[288,8192]{1,0:T(8,128)(2,1)} %pad_maximum_fusion.refs_0_, bf16[288,8192]{1,0:T(8,128)(2,1)} %collective-permute-done.4.refs_0_.refs_1_, ...), custom_call_target="tpu_custom_call" | custom-call | flops 1 | bytes 1 | tf_op jit(solution)/shard_map/project/pallas_call | solution.py:529
  351.8 6.9 %collective-permute-done.23 = bf16[8,144,128]{2,1,0:T(8,128)(2,1)S(1)} collective-permute-done((bf16[8,144,128]{2,1,0:T(8,128)(2,1)S(1)}, bf16[8,144,128]{2,1,0:T(8,128)(2,1)S(1)}, u32[]{:S(2)}, u32[]{:S(2)}) %collective-permute-start.23) | collective-permute-done | bytes 294944 | tf_op jit(solution)/shard_map/ppermute | solution.py:353
  368.5 13.3 %token_attention.4 = (bf16[272,1024]{1,0:T(8,128)(2,1)S(1)}, bf16[272,1024]{1,0:T(8,128)(2,1)S(1)}, bf16[272,1024]{1,0:T(8,128)(2,1)S(1)}, bf16[272,1024]{1,0:T(8,128)(2,1)S(1)}) custom-call(s32[4]{0:T(128)S(1)} %pad_add_fusion.place_ref, bf16[288,1536]{1,0:T(8,128)(2,1)S(1)} %project.6.refs_0_, bf16[288,1536]{1,0:T(8,128)(2,1)S(1)} %copy-done.7, ...), custom_call_target="tpu_custom_call" | custom-call | flops 1 | bytes 1 | tf_op jit(solution)/shard_map/token_attention/pallas_call | solution.py:312
  388.6 13.3 %token_attention.5 = (bf16[272,1024]{1,0:T(8,128)(2,1)S(1)}, bf16[272,1024]{1,0:T(8,128)(2,1)S(1)}, bf16[272,1024]{1,0:T(8,128)(2,1)S(1)}, bf16[272,1024]{1,0:T(8,128)(2,1)S(1)}) custom-call(s32[4]{0:T(128)S(1)} %pad_add_fusion.place_ref, ...), custom_call_target="tpu_custom_call", output_to_operand_aliasing={{0}: (6, {}), {1}: (7, {}), {2}: (8, {}), {3}: (9, {})} | custom-call | flops 1 | bytes 1 | tf_op jit(solution)/shard_map/token_attention/pallas_call | solution.py:312
  403.6 13.4 %collective-permute-done.26 = bf16[8,144,128]{2,1,0:T(8,128)(2,1)S(1)} collective-permute-done((bf16[8,144,128]{2,1,0:T(8,128)(2,1)S(1)}, bf16[8,144,128]{2,1,0:T(8,128)(2,1)S(1)}, u32[]{:S(2)}, u32[]{:S(2)}) %collective-permute-start.26) | collective-permute-done | bytes 294944 | tf_op jit(solution)/shard_map/ppermute | solution.py:353
  420.0 3.3 collective-permute-start.39
  423.6 13.2 %token_attention.6 = (bf16[272,512]{1,0:T(8,128)(2,1)S(1)}, bf16[272,512]{1,0:T(8,128)(2,1)S(1)}, bf16[272,512]{1,0:T(8,128)(2,1)S(1)}, bf16[272,512]{1,0:T(8,128)(2,1)S(1)}) custom-call(s32[4]{0:T(128)S(1)} %pad_add_fusion.place_ref, bf16[288,768]{1,0:T(8,128)(2,1)S(1)} %copy-done.17, bf16[288,768]{1,0:T(8,128)(2,1)S(1)} %copy-done.19, ...), custom_call_target="tpu_custom_call" | custom-call | flops 1 | bytes 1 | tf_op jit(solution)/shard_map/token_attention/pallas_call | solution.py:312
  438.1 13.2 %token_attention.7 = (bf16[272,512]{1,0:T(8,128)(2,1)S(1)}, bf16[272,512]{1,0:T(8,128)(2,1)S(1)}, bf16[272,512]{1,0:T(8,128)(2,1)S(1)}, bf16[272,512]{1,0:T(8,128)(2,1)S(1)}) custom-call(s32[4]{0:T(128)S(1)} %pad_add_fusion.place_ref, bf16[288,768]{1,0:T(8,128)(2,1)S(1)} %get-tuple-element.221.refs_0_, bf16[288,768]{1,0:T(8,128)(2,1)S(1)} %get-tuple-element.222.refs_1_, ...), custom_call_target="tpu_custom_call" | custom-call | flops 1 | bytes 1 | tf_op jit(solution)/shard_map/token_attention/pallas_call | solution.py:312
  456.4 6.8 %collective-permute-done.31 = bf16[272,512]{1,0:T(8,128)(2,1)S(1)} collective-permute-done((bf16[272,512]{1,0:T(8,128)(2,1)S(1)}, bf16[272,512]{1,0:T(8,128)(2,1)S(1)}, u32[]{:S(2)}, u32[]{:S(2)}) %collective-permute-start.31) | collective-permute-done | bytes 278560 | tf_op jit(solution)/shard_map/ppermute | solution.py:68
  463.1 4.4 collective-permute-start.36
  467.5 3.0 collective-permute-start.38
  471.9 4.3 collective-permute-start.32
  476.2 2.9 collective-permute-done.38
  481.6 7.5 %collective-permute-done.34 = bf16[272,1024]{1,0:T(8,128)(2,1)S(1)} collective-permute-done((bf16[272,1024]{1,0:T(8,128)(2,1)S(1)}, bf16[272,1024]{1,0:T(8,128)(2,1)S(1)}, u32[]{:S(2)}, u32[]{:S(2)}) %collective-permute-start.34) | collective-permute-done | bytes 557088 | tf_op jit(solution)/shard_map/ppermute | solution.py:68
  489.3 8.2 %collective-permute-done.32 = bf16[272,1024]{1,0:T(8,128)(2,1)S(1)} collective-permute-done((bf16[272,1024]{1,0:T(8,128)(2,1)S(1)}, bf16[272,1024]{1,0:T(8,128)(2,1)S(1)}, u32[]{:S(2)}, u32[]{:S(2)}) %collective-permute-start.32) | collective-permute-done | bytes 557088 | tf_op jit(solution)/shard_map/ppermute | solution.py:68
  497.4 5.5 collective-permute-done.33
  504.7 3.1 collective-permute-start.41
  522.6 25.6 %output_product.2.refs_6_ = f32[4,544,1024]{2,1,0:T(8,128)} custom-call(s32[4]{0:T(128)S(1)} %add_add_fusion.ids_ref, bf16[4,272,1024]{2,1,0:T(8,128)(2,1)} %pad_maximum_fusion.1.mixed_ref, bf16[4,272,1024]{2,1,0:T(8,128)(2,1)} %collective-permute-done.41.other_ref, bf16[1024,8192]{1,0:T(8,128)(2,1)} %own_ref.3, bf16[1024,1024]{1,0:T(8,128)(2,1)} %copy-done.30, ...), custom_call_target="tpu_custom_call" | custom-call | flops 1 | bytes 1 | tf_op jit(solution)/shard_map/output_product/pallas_call | solution.py:466
  548.2 11.9 %output_product.3 = (bf16[272,8192]{1,0:T(8,128)(2,1)}, bf16[272,4096]{1,0:T(8,128)(2,1)}) custom-call(s32[4]{0:T(128)S(1)} %add_add_fusion.ids_ref, bf16[4,272,1024]{2,1,0:T(8,128)(2,1)} %pad_maximum_fusion.1.mixed_ref, bf16[4,272,1024]{2,1,0:T(8,128)(2,1)} %collective-permute-done.41.other_ref, bf16[1024,8192]{1,0:T(8,128)(2,1)} %own_ref.3, ...), custom_call_target="tpu_custom_call" | custom-call | flops 1 | bytes 1 | tf_op jit(solution)/shard_map/output_product/pallas_call | solution.py:466
  562.0 4.2 collective-permute-done.44
  566.2 3.8 fusion.3
  (233 shorter events, 99.7 us)
Async XLA Ops:
  6.5 214.5 %all-gather.3.cloned.1.call-start = ((), (), s32[]{:S(2)}) async-start(), calls=%async_computation | async-start | bytes 14155776 | tf_op jit(solution)/shard_map/all_gather | solution.py:592
  9.6 48.7 %collective-permute-start.1 = (bf16[1024,1024]{1,0:T(8,128)(2,1)}, bf16[1024,1024]{1,0:T(8,128)(2,1)}, u32[]{:S(2)}, u32[]{:S(2)}) collective-permute-start(bf16[1024,1024]{1,0:T(8,128)(2,1)} %constant_dynamic-slice_fusion), channel_id=1, source_target_pairs={{1,2},{2,1},{5,6},{6,5},{9,10},{10,9},{13,14},{14,13},{17,18},{18,... | collective-permute-start | bytes 6291464 | tf_op jit(solution)/shard_map/ppermute | solution.py:68
  12.8 45.9 %collective-permute-start.2 = (bf16[1024,1024]{1,0:T(8,128)(2,1)}, bf16[1024,1024]{1,0:T(8,128)(2,1)S(1)}, u32[]{:S(2)}, u32[]{:S(2)}) collective-permute-start(bf16[1024,1024]{1,0:T(8,128)(2,1)} %constant_dynamic-slice_fusion), channel_id=1, source_target_pairs={{1,0},{2,3},{5,4},{6,7},{9,8},{10,11},{13,12},{14,15},{17,16},{18,... | collective-permute-start | bytes 6291464 | tf_op jit(solution)/shard_map/ppermute | solution.py:68
  17.6 37.2 %collective-permute-start = (bf16[1024,768]{1,0:T(8,128)(2,1)S(1)}, bf16[1024,768]{1,0:T(8,128)(2,1)}, u32[]{:S(2)}, u32[]{:S(2)}) collective-permute-start(bf16[1024,768]{1,0:T(8,128)(2,1)S(1)} %pad_maximum_fusion.2), channel_id=1, source_target_pairs={{0,1},{3,2},{4,5},{7,6},{8,9},{11,10},{12,13},{15,14},{16,17},{19,... | collective-permute-start | bytes 4718600 | tf_op jit(solution)/shard_map/ppermute | solution.py:68
  19.0 35.6 %collective-permute-start.3 = (f32[1,8]{1,0:T(1,128)S(1)}, f32[1,8]{1,0:T(1,128)S(1)}, u32[]{:S(2)}, u32[]{:S(2)}) collective-permute-start(f32[1,8]{1,0:T(1,128)S(1)} %copy-done.53), channel_id=1, source_target_pairs={{0,1},{3,2},{4,5},{7,6},{8,9},{11,10},{12,13},{15,14},{16,17},{19,... | collective-permute-start | bytes 104 | tf_op jit(solution)/shard_map/ppermute | solution.py:68
  58.8 266.9 %all-gather.5.cloned.1.call-start = ((), (), s32[]{:S(2)}) async-start(), calls=%async_computation.1 | async-start | bytes 14155776 | tf_op jit(solution)/shard_map/all_gather | solution.py:614
  58.8 104.0 %collective-permute-start.4 = (bf16[288,8192]{1,0:T(8,128)(2,1)}, bf16[288,8192]{1,0:T(8,128)(2,1)}, u32[]{:S(2)}, u32[]{:S(2)}) collective-permute-start(bf16[288,8192]{1,0:T(8,128)(2,1)} %pad_maximum_fusion.refs_0_), channel_id=1, source_target_pairs={{0,1},{3,2},{4,5},{7,6},{8,9},{11,10},{12,13},{15,14},{16,17},{19,... | collective-permute-start | bytes 14155784 | tf_op jit(solution)/shard_map/ppermute | solution.py:68
  60.1 104.8 %collective-permute-start.5 = (bf16[288,8192]{1,0:T(8,128)(2,1)}, bf16[288,8192]{1,0:T(8,128)(2,1)}, u32[]{:S(2)}, u32[]{:S(2)}) collective-permute-start(bf16[288,8192]{1,0:T(8,128)(2,1)} %pad_maximum_fusion.refs_0_), channel_id=1, source_target_pairs={{1,2},{2,1},{5,6},{6,5},{9,10},{10,9},{13,14},{14,13},{17,18},{18,... | collective-permute-start | bytes 14155784 | tf_op jit(solution)/shard_map/ppermute | solution.py:68
  65.9 79.4 %collective-permute-start.6 = (bf16[1024,1024]{1,0:T(8,128)(2,1)S(1)}, bf16[1024,1024]{1,0:T(8,128)(2,1)}, u32[]{:S(2)}, u32[]{:S(2)}) collective-permute-start(bf16[1024,1024]{1,0:T(8,128)(2,1)S(1)} %broadcast_select_fusion.2.refs_0_), channel_id=1, source_target_pairs={{0,8},{4,12},{8,24},{12,28},{24,16},{28,20},{16,0},{20,4},{1,9},{5... | collective-permute-start | bytes 6291464 | tf_op jit(solution)/shard_map/ppermute | solution.py:95
  67.2 78.1 %collective-permute-start.7 = (bf16[1024,1024]{1,0:T(8,128)(2,1)S(1)}, bf16[1024,1024]{1,0:T(8,128)(2,1)}, u32[]{:S(2)}, u32[]{:S(2)}) collective-permute-start(bf16[1024,1024]{1,0:T(8,128)(2,1)S(1)} %broadcast_select_fusion.2.refs_0_), channel_id=1, source_target_pairs={{0,16},{4,20},{8,0},{12,4},{24,8},{28,12},{16,24},{20,28},{1,17},{... | collective-permute-start | bytes 6291464 | tf_op jit(solution)/shard_map/ppermute | solution.py:95
  87.0 3.8 collective-permute-start.8
  90.8 51.5 %collective-permute-start.9 = (f32[2,16]{1,0:T(2,128)S(1)}, f32[2,16]{1,0:T(2,128)S(1)}, u32[]{:S(2)}, u32[]{:S(2)}) collective-permute-start(f32[2,16]{1,0:T(2,128)S(1)} %pad_maximum_fusion.8), channel_id=1, source_target_pairs={{0,8},{4,12},{8,0},{12,4},{16,24},{20,28},{24,16},{28,20},{1,9},{5... | collective-permute-start | bytes 392 | tf_op jit(solution)/shard_map/ppermute | solution.py:118
  142.3 2.9 collective-permute-start.10
  168.4 52.7 %collective-permute-start.12 = (bf16[144,8192]{1,0:T(8,128)(2,1)}, bf16[144,8192]{1,0:T(8,128)(2,1)S(1)}, u32[]{:S(2)}, u32[]{:S(2)}) collective-permute-start(bf16[144,8192]{1,0:T(8,128)(2,1)} %slice.42), channel_id=1, source_target_pairs={{1,2},{2,1},{5,6},{6,5},{9,10},{10,9},{13,14},{14,13},{17,18},{18,... | collective-permute-start | bytes 7077896 | tf_op jit(solution)/shard_map/ppermute | solution.py:68
  171.4 44.1 %collective-permute-start.13 = (bf16[1024,1024]{1,0:T(8,128)(2,1)}, bf16[1024,1024]{1,0:T(8,128)(2,1)}, u32[]{:S(2)}, u32[]{:S(2)}) collective-permute-start(bf16[1024,1024]{1,0:T(8,128)(2,1)} %collective-permute-done.1), channel_id=1, source_target_pairs={{1,0},{2,3},{5,4},{6,7},{9,8},{10,11},{13,12},{14,15},{17,16},{18,... | collective-permute-start | bytes 6291464 | tf_op jit(solution)/shard_map/ppermute | solution.py:68
  174.1 37.5 %collective-permute-start.11 = (bf16[1024,768]{1,0:T(8,128)(2,1)S(1)}, bf16[1024,768]{1,0:T(8,128)(2,1)}, u32[]{:S(2)}, u32[]{:S(2)}) collective-permute-start(bf16[1024,768]{1,0:T(8,128)(2,1)S(1)} %copy-done.35), channel_id=1, source_target_pairs={{0,1},{3,2},{4,5},{7,6},{8,9},{11,10},{12,13},{15,14},{16,17},{19,... | collective-permute-start | bytes 4718600 | tf_op jit(solution)/shard_map/ppermute | solution.py:68
  176.7 32.9 %collective-permute-start.14 = (bf16[512,1024]{1,0:T(8,128)(2,1)S(1)}, bf16[512,1024]{1,0:T(8,128)(2,1)S(1)}, u32[]{:S(2)}, u32[]{:S(2)}) collective-permute-start(bf16[512,1024]{1,0:T(8,128)(2,1)S(1)} %slice.43), channel_id=1, source_target_pairs={{0,8},{4,12},{8,24},{12,28},{24,16},{28,20},{16,0},{20,4},{1,9},{5... | collective-permute-start | bytes 3145736 | tf_op jit(solution)/shard_map/ppermute | solution.py:95
  179.2 31.4 %collective-permute-start.15 = (bf16[512,1024]{1,0:T(8,128)(2,1)S(1)}, bf16[512,1024]{1,0:T(8,128)(2,1)S(1)}, u32[]{:S(2)}, u32[]{:S(2)}) collective-permute-start(bf16[512,1024]{1,0:T(8,128)(2,1)S(1)} %slice.44), channel_id=1, source_target_pairs={{0,16},{4,20},{8,0},{12,4},{24,8},{28,12},{16,24},{20,28},{1,17},{... | collective-permute-start | bytes 3145736 | tf_op jit(solution)/shard_map/ppermute | solution.py:95
  225.2 51.8 %collective-permute-start.16 = (bf16[144,8192]{1,0:T(8,128)(2,1)}, bf16[144,8192]{1,0:T(8,128)(2,1)}, u32[]{:S(2)}, u32[]{:S(2)}) collective-permute-start(bf16[144,8192]{1,0:T(8,128)(2,1)} %slice.45), channel_id=1, source_target_pairs={{1,2},{2,1},{5,6},{6,5},{9,10},{10,9},{13,14},{14,13},{17,18},{18,... | collective-permute-start | bytes 7077896 | tf_op jit(solution)/shard_map/ppermute | solution.py:68
  228.0 45.7 %collective-permute-start.17 = (bf16[1024,1024]{1,0:T(8,128)(2,1)}, bf16[1024,1024]{1,0:T(8,128)(2,1)}, u32[]{:S(2)}, u32[]{:S(2)}) collective-permute-start(bf16[1024,1024]{1,0:T(8,128)(2,1)} %constant_dynamic-slice_fusion), channel_id=1, source_target_pairs={{0,1},{3,2},{4,5},{7,6},{8,9},{11,10},{12,13},{15,14},{16,17},{19,... | collective-permute-start | bytes 6291464 | tf_op jit(solution)/shard_map/ppermute | solution.py:68
  280.4 79.6 %collective-permute-start.20 = (bf16[1024,1024]{1,0:T(8,128)(2,1)}, bf16[1024,1024]{1,0:T(8,128)(2,1)}, u32[]{:S(2)}, u32[]{:S(2)}) collective-permute-start(bf16[1024,1024]{1,0:T(8,128)(2,1)} %broadcast_select_fusion.1.refs_1_), channel_id=1, source_target_pairs={{0,8},{4,12},{8,24},{12,28},{24,16},{28,20},{16,0},{20,4},{1,9},{5... | collective-permute-start | bytes 6291464 | tf_op jit(solution)/shard_map/ppermute | solution.py:95
  281.6 78.4 %collective-permute-start.21 = (bf16[1024,1024]{1,0:T(8,128)(2,1)}, bf16[1024,1024]{1,0:T(8,128)(2,1)}, u32[]{:S(2)}, u32[]{:S(2)}) collective-permute-start(bf16[1024,1024]{1,0:T(8,128)(2,1)} %broadcast_select_fusion.1.refs_1_), channel_id=1, source_target_pairs={{0,16},{4,20},{8,0},{12,4},{24,8},{28,12},{16,24},{20,28},{1,17},{... | collective-permute-start | bytes 6291464 | tf_op jit(solution)/shard_map/ppermute | solution.py:95
  281.9 78.2 %collective-permute-start.18 = (bf16[1024,1024]{1,0:T(8,128)(2,1)}, bf16[1024,1024]{1,0:T(8,128)(2,1)}, u32[]{:S(2)}, u32[]{:S(2)}) collective-permute-start(bf16[1024,1024]{1,0:T(8,128)(2,1)} %collective-permute-done.17), channel_id=1, source_target_pairs={{1,2},{2,1},{5,6},{6,5},{9,10},{10,9},{13,14},{14,13},{17,18},{18,... | collective-permute-start | bytes 6291464 | tf_op jit(solution)/shard_map/ppermute | solution.py:68
  307.4 16.1 %collective-permute-start.19 = (bf16[8,144,128]{2,1,0:T(8,128)(2,1)S(1)}, bf16[8,144,128]{2,1,0:T(8,128)(2,1)S(1)}, u32[]{:S(2)}, u32[]{:S(2)}) collective-permute-start(bf16[8,144,128]{2,1,0:T(8,128)(2,1)S(1)} %fusion.22), channel_id=1, source_target_pairs={{0,4},{4,0},{8,12},{12,8},{16,20},{20,16},{24,28},{28,24},{1,5},{5... | collective-permute-start | bytes 884744 | tf_op jit(solution)/shard_map/ppermute | solution.py:353
  324.6 24.1 %collective-permute-start.22 = (bf16[8,144,128]{2,1,0:T(8,128)(2,1)}, bf16[8,144,128]{2,1,0:T(8,128)(2,1)}, u32[]{:S(2)}, u32[]{:S(2)}) collective-permute-start(bf16[8,144,128]{2,1,0:T(8,128)(2,1)} %fusion.26), channel_id=1, source_target_pairs={{0,8},{4,12},{8,0},{12,4},{16,24},{20,28},{24,16},{28,20},{1,9},{5... | collective-permute-start | bytes 884744 | tf_op jit(solution)/shard_map/ppermute | solution.py:353
  327.3 31.4 %copy-start.48 = (f32[8]{0:T(128)S(1)}, f32[8]{0:T(128)}, u32[]{:S(2)}) copy-start(f32[8]{0:T(128)} %get-tuple-element.252) | copy-start | bytes 100
  350.3 8.4 %collective-permute-start.23 = (bf16[8,144,128]{2,1,0:T(8,128)(2,1)S(1)}, bf16[8,144,128]{2,1,0:T(8,128)(2,1)S(1)}, u32[]{:S(2)}, u32[]{:S(2)}) collective-permute-start(bf16[8,144,128]{2,1,0:T(8,128)(2,1)S(1)} %fusion.9), channel_id=1, source_target_pairs={{0,16},{4,20},{8,24},{12,28},{16,0},{20,4},{24,8},{28,12},{1,17},{... | collective-permute-start | bytes 884744 | tf_op jit(solution)/shard_map/ppermute | solution.py:353
  360.1 57.4 %collective-permute-start.27 = (bf16[1024,1024]{1,0:T(8,128)(2,1)}, bf16[1024,1024]{1,0:T(8,128)(2,1)S(1)}, u32[]{:S(2)}, u32[]{:S(2)}) collective-permute-start(bf16[1024,1024]{1,0:T(8,128)(2,1)} %collective-permute-done.18), channel_id=1, source_target_pairs={{1,0},{2,3},{5,4},{6,7},{9,8},{10,11},{13,12},{14,15},{17,16},{18,... | collective-permute-start | bytes 6291464 | tf_op jit(solution)/shard_map/ppermute | solution.py:68
  367.3 14.5 %collective-permute-start.24 = (bf16[8,144,128]{2,1,0:T(8,128)(2,1)S(1)}, bf16[8,144,128]{2,1,0:T(8,128)(2,1)S(1)}, u32[]{:S(2)}, u32[]{:S(2)}) collective-permute-start(bf16[8,144,128]{2,1,0:T(8,128)(2,1)S(1)} %fusion.21), channel_id=1, source_target_pairs={{0,4},{4,0},{8,12},{12,8},{16,20},{20,16},{24,28},{28,24},{1,5},{5... | collective-permute-start | bytes 884744 | tf_op jit(solution)/shard_map/ppermute | solution.py:353
  382.0 19.9 %collective-permute-start.25 = (bf16[8,144,128]{2,1,0:T(8,128)(2,1)S(1)}, bf16[8,144,128]{2,1,0:T(8,128)(2,1)S(1)}, u32[]{:S(2)}, u32[]{:S(2)}) collective-permute-start(bf16[8,144,128]{2,1,0:T(8,128)(2,1)S(1)} %fusion.25), channel_id=1, source_target_pairs={{0,8},{4,12},{8,0},{12,4},{16,24},{20,28},{24,16},{28,20},{1,9},{5... | collective-permute-start | bytes 884744 | tf_op jit(solution)/shard_map/ppermute | solution.py:353
  384.8 32.6 %collective-permute-start.28 = (bf16[512,1024]{1,0:T(8,128)(2,1)}, bf16[512,1024]{1,0:T(8,128)(2,1)S(1)}, u32[]{:S(2)}, u32[]{:S(2)}) collective-permute-start(bf16[512,1024]{1,0:T(8,128)(2,1)} %slice.50), channel_id=1, source_target_pairs={{0,8},{4,12},{8,24},{12,28},{24,16},{28,20},{16,0},{20,4},{1,9},{5... | collective-permute-start | bytes 3145736 | tf_op jit(solution)/shard_map/ppermute | solution.py:95
  388.1 29.3 %collective-permute-start.29 = (bf16[512,1024]{1,0:T(8,128)(2,1)}, bf16[512,1024]{1,0:T(8,128)(2,1)S(1)}, u32[]{:S(2)}, u32[]{:S(2)}) collective-permute-start(bf16[512,1024]{1,0:T(8,128)(2,1)} %slice.51), channel_id=1, source_target_pairs={{0,16},{4,20},{8,0},{12,4},{24,8},{28,12},{16,24},{20,28},{1,17},{... | collective-permute-start | bytes 3145736 | tf_op jit(solution)/shard_map/ppermute | solution.py:95
  402.4 14.7 %collective-permute-start.26 = (bf16[8,144,128]{2,1,0:T(8,128)(2,1)S(1)}, bf16[8,144,128]{2,1,0:T(8,128)(2,1)S(1)}, u32[]{:S(2)}, u32[]{:S(2)}) collective-permute-start(bf16[8,144,128]{2,1,0:T(8,128)(2,1)S(1)} %fusion.15), channel_id=1, source_target_pairs={{0,16},{4,20},{8,24},{12,28},{16,0},{20,4},{24,8},{28,12},{1,17},{... | collective-permute-start | bytes 884744 | tf_op jit(solution)/shard_map/ppermute | solution.py:353
  420.0 84.6 %collective-permute-start.39 = (bf16[1024,1024]{1,0:T(8,128)(2,1)S(1)}, bf16[1024,1024]{1,0:T(8,128)(2,1)S(1)}, u32[]{:S(2)}, u32[]{:S(2)}) collective-permute-start(bf16[1024,1024]{1,0:T(8,128)(2,1)S(1)} %broadcast_select_fusion.refs_0_), channel_id=1, source_target_pairs={{0,8},{4,12},{8,24},{12,28},{24,16},{28,20},{16,0},{20,4},{1,9},{5... | collective-permute-start | bytes 6291464 | tf_op jit(solution)/shard_map/ppermute | solution.py:95
  423.3 81.3 %collective-permute-start.40 = (bf16[1024,1024]{1,0:T(8,128)(2,1)S(1)}, bf16[1024,1024]{1,0:T(8,128)(2,1)}, u32[]{:S(2)}, u32[]{:S(2)}) collective-permute-start(bf16[1024,1024]{1,0:T(8,128)(2,1)S(1)} %broadcast_select_fusion.refs_0_), channel_id=1, source_target_pairs={{0,16},{4,20},{8,0},{12,4},{24,8},{28,12},{16,24},{20,28},{1,17},{... | collective-permute-start | bytes 6291464 | tf_op jit(solution)/shard_map/ppermute | solution.py:95
  436.8 17.1 %collective-permute-start.30 = (bf16[272,512]{1,0:T(8,128)(2,1)S(1)}, bf16[272,512]{1,0:T(8,128)(2,1)S(1)}, u32[]{:S(2)}, u32[]{:S(2)}) collective-permute-start(bf16[272,512]{1,0:T(8,128)(2,1)S(1)} %get-tuple-element.220), channel_id=1, source_target_pairs={{1,0},{2,3},{5,4},{6,7},{9,8},{10,11},{13,12},{14,15},{17,16},{18,... | collective-permute-start | bytes 835592 | tf_op jit(solution)/shard_map/ppermute | solution.py:68
  451.3 11.9 %collective-permute-start.31 = (bf16[272,512]{1,0:T(8,128)(2,1)S(1)}, bf16[272,512]{1,0:T(8,128)(2,1)S(1)}, u32[]{:S(2)}, u32[]{:S(2)}) collective-permute-start(bf16[272,512]{1,0:T(8,128)(2,1)S(1)} %get-tuple-element.225), channel_id=1, source_target_pairs={{1,0},{2,3},{5,4},{6,7},{9,8},{10,11},{13,12},{14,15},{17,16},{18,... | collective-permute-start | bytes 835592 | tf_op jit(solution)/shard_map/ppermute | solution.py:68
  452.6 14.9 %collective-permute-start.35 = (bf16[272,512]{1,0:T(8,128)(2,1)S(1)}, bf16[272,512]{1,0:T(8,128)(2,1)S(1)}, u32[]{:S(2)}, u32[]{:S(2)}) collective-permute-start(bf16[272,512]{1,0:T(8,128)(2,1)S(1)} %get-tuple-element.232), channel_id=1, source_target_pairs={{1,3},{2,0},{5,7},{6,4},{9,11},{10,8},{13,15},{14,12},{17,19},{18,... | collective-permute-start | bytes 835592 | tf_op jit(solution)/shard_map/ppermute | solution.py:68
  453.9 16.6 %collective-permute-start.37 = (bf16[272,512]{1,0:T(8,128)(2,1)S(1)}, bf16[272,512]{1,0:T(8,128)(2,1)S(1)}, u32[]{:S(2)}, u32[]{:S(2)}) collective-permute-start(bf16[272,512]{1,0:T(8,128)(2,1)S(1)} %get-tuple-element.234), channel_id=1, source_target_pairs={{1,2},{2,1},{5,6},{6,5},{9,10},{10,9},{13,14},{14,13},{17,18},{18,... | collective-permute-start | bytes 835592 | tf_op jit(solution)/shard_map/ppermute | solution.py:68
  463.1 8.7 %collective-permute-start.36 = (bf16[272,512]{1,0:T(8,128)(2,1)S(1)}, bf16[272,512]{1,0:T(8,128)(2,1)S(1)}, u32[]{:S(2)}, u32[]{:S(2)}) collective-permute-start(bf16[272,512]{1,0:T(8,128)(2,1)S(1)} %get-tuple-element.233), channel_id=1, source_target_pairs={{1,3},{2,0},{5,7},{6,4},{9,11},{10,8},{13,15},{14,12},{17,19},{18,... | collective-permute-start | bytes 835592 | tf_op jit(solution)/shard_map/ppermute | solution.py:68
  467.5 11.5 %collective-permute-start.38 = (bf16[272,512]{1,0:T(8,128)(2,1)S(1)}, bf16[272,512]{1,0:T(8,128)(2,1)S(1)}, u32[]{:S(2)}, u32[]{:S(2)}) collective-permute-start(bf16[272,512]{1,0:T(8,128)(2,1)S(1)} %get-tuple-element.235), channel_id=1, source_target_pairs={{1,2},{2,1},{5,6},{6,5},{9,10},{10,9},{13,14},{14,13},{17,18},{18,... | collective-permute-start | bytes 835592 | tf_op jit(solution)/shard_map/ppermute | solution.py:68
  470.5 18.6 %collective-permute-start.34 = (bf16[272,1024]{1,0:T(8,128)(2,1)S(1)}, bf16[272,1024]{1,0:T(8,128)(2,1)S(1)}, u32[]{:S(2)}, u32[]{:S(2)}) collective-permute-start(bf16[272,1024]{1,0:T(8,128)(2,1)S(1)} %get-tuple-element.229), channel_id=1, source_target_pairs={{1,3},{2,0},{5,7},{6,4},{9,11},{10,8},{13,15},{14,12},{17,19},{18,... | collective-permute-start | bytes 1671176 | tf_op jit(solution)/shard_map/ppermute | solution.py:68
  471.9 25.6 %collective-permute-start.32 = (bf16[272,1024]{1,0:T(8,128)(2,1)S(1)}, bf16[272,1024]{1,0:T(8,128)(2,1)S(1)}, u32[]{:S(2)}, u32[]{:S(2)}) collective-permute-start(bf16[272,1024]{1,0:T(8,128)(2,1)S(1)} %get-tuple-element.227), channel_id=1, source_target_pairs={{1,0},{2,3},{5,4},{6,7},{9,8},{10,11},{13,12},{14,15},{17,16},{18,... | collective-permute-start | bytes 1671176 | tf_op jit(solution)/shard_map/ppermute | solution.py:68
  479.0 23.9 %collective-permute-start.33 = (bf16[272,1024]{1,0:T(8,128)(2,1)S(1)}, bf16[272,1024]{1,0:T(8,128)(2,1)S(1)}, u32[]{:S(2)}, u32[]{:S(2)}) collective-permute-start(bf16[272,1024]{1,0:T(8,128)(2,1)S(1)} %get-tuple-element.228), channel_id=1, source_target_pairs={{1,2},{2,1},{5,6},{6,5},{9,10},{10,9},{13,14},{14,13},{17,18},{18,... | collective-permute-start | bytes 1671176 | tf_op jit(solution)/shard_map/ppermute | solution.py:68
  504.7 14.3 %collective-permute-start.41 = (bf16[4,272,1024]{2,1,0:T(8,128)(2,1)}, bf16[4,272,1024]{2,1,0:T(8,128)(2,1)}, u32[]{:S(2)}, u32[]{:S(2)}) collective-permute-start(bf16[4,272,1024]{2,1,0:T(8,128)(2,1)} %pad_maximum_fusion.1.mixed_ref), channel_id=1, source_target_pairs={{0,4},{4,0},{8,12},{12,8},{16,20},{20,16},{24,28},{28,24},{1,5},{5... | collective-permute-start | bytes 6684680 | tf_op jit(solution)/shard_map/ppermute | solution.py:77
  508.8 39.3 %collective-permute-start.42 = (bf16[512,1024]{1,0:T(8,128)(2,1)}, bf16[512,1024]{1,0:T(8,128)(2,1)}, u32[]{:S(2)}, u32[]{:S(2)}) collective-permute-start(bf16[512,1024]{1,0:T(8,128)(2,1)} %slice.54), channel_id=1, source_target_pairs={{0,8},{4,12},{8,24},{12,28},{24,16},{28,20},{16,0},{20,4},{1,9},{5... | collective-permute-start | bytes 3145736 | tf_op jit(solution)/shard_map/ppermute | solution.py:95
  512.6 35.6 %collective-permute-start.43 = (bf16[512,1024]{1,0:T(8,128)(2,1)}, bf16[512,1024]{1,0:T(8,128)(2,1)}, u32[]{:S(2)}, u32[]{:S(2)}) collective-permute-start(bf16[512,1024]{1,0:T(8,128)(2,1)} %slice.55), channel_id=1, source_target_pairs={{0,16},{4,20},{8,0},{12,4},{24,8},{28,12},{16,24},{20,28},{1,17},{... | collective-permute-start | bytes 3145736 | tf_op jit(solution)/shard_map/ppermute | solution.py:95
  560.1 6.1 %collective-permute-start.44 = (bf16[272,4096]{1,0:T(8,128)(2,1)}, bf16[272,4096]{1,0:T(8,128)(2,1)S(1)}, u32[]{:S(2)}, u32[]{:S(2)}) collective-permute-start(bf16[272,4096]{1,0:T(8,128)(2,1)} %get-tuple-element.246), channel_id=1, source_target_pairs={{0,4},{4,0},{8,12},{12,8},{16,20},{20,16},{24,28},{28,24},{1,5},{5... | collective-permute-start | bytes 6684680 | tf_op jit(solution)/shard_map/ppermute | solution.py:77
  (55 other events, 655.6 us)
Sparse Core Ops, SparseCore 0:
  58.9 108.3 all-gather.2
  221.2 84.1 all-gather.4

commit v3 on v2

--- a/solution.py
+++ b/solution.py
@@ -77,14 +77,25 @@
     return lax.ppermute(block, "seg", [(i, i ^ 1) for i in range(lax.axis_size("seg"))])
 
 
+def ring_order():
+    chips = lax.axis_size("seg") // 2
+    cycle = seg_cycle(chips)
+    place_of = [cycle.index(c) for c in range(chips)]
+    place = jnp.array(place_of, jnp.int32)[lax.axis_index("seg") // 2]
+    steps = [0] + [s for turn in range(1, chips // 2) for s in (-turn, turn)] + [chips // 2]
+    return jnp.array(cycle, jnp.int32)[(place + jnp.array(steps) + chips) % chips]
+
+
 class ChipRing:
-    def __init__(self, block):
+    def __init__(self, block, straight=False):
         self.chips = lax.axis_size("seg") // 2
         self.cycle = seg_cycle(self.chips)
-        self.block, self.right, self.left = block, [block], [block]
+        self.block, self.right, self.left, self.last = block, [block], [block], None
         for _ in range(1, self.chips // 2):
             self.right.append(self.step(self.right[-1], 1))
             self.left.append(self.step(self.left[-1], -1))
+        if straight:
+            self.last = (self.step(block, self.chips // 2),)
 
     def step(self, part, distance):
         route = [
@@ -94,34 +105,28 @@
         ]
         return lax.ppermute(part, "seg", route)
 
-    def close(self):
+    def halves(self):
         half = self.block.shape[0] // 2
-        self.last = (self.step(self.right[-1][:half], 1), self.step(self.left[-1][half:], -1))
-        return self.last
+        return self.right[-1][:half], self.left[-1][half:]
+
+    def close(self, halves=None):
+        right, left = halves or self.halves()
+        self.last = (self.step(right, 1), self.step(left, -1))
 
     def pieces(self):
-        place_of = [self.cycle.index(c) for c in range(self.chips)]
-        place = jnp.array(place_of, jnp.int32)[lax.axis_index("seg") // 2]
-        table = jnp.array(self.cycle, jnp.int32)
-        found = [((self.block,), 0)]
+        found = [(self.block,)]
         for turn in range(1, self.chips // 2):
-            found += [((self.right[turn],), -turn), ((self.left[turn],), turn)]
-        found.append((self.last, self.chips // 2))
-        return [(parts, table[(place + at + self.chips) % self.chips]) for parts, at in found]
-
-
-def seg_all(values):
+            found += [(self.right[turn],), (self.left[turn],)]
+        return found + [self.last]
+
+
+def seg_double(values, bit):
     size = lax.axis_size("seg")
-    me = lax.axis_index("seg")
-    bit = 1
-    while bit < size:
-        got = lax.ppermute(values, "seg", [(i, i ^ bit) for i in range(size)])
-        upper = (me // bit) % 2 == 1
-        values = jnp.concatenate(
-            [jnp.where(upper, got, values), jnp.where(upper, values, got)], axis=0
-        )
-        bit *= 2
-    return values
+    got = lax.ppermute(values, "seg", [(i, i ^ bit) for i in range(size)])
+    upper = (lax.axis_index("seg") // bit) % 2 == 1
+    return jnp.concatenate(
+        [jnp.where(upper, got, values), jnp.where(upper, values, got)], axis=0
+    )
 
 
 def pad_to(value, unit):
@@ -209,7 +214,7 @@
     return numerator / (nt_dot(feat, sums) + 1.0)
 
 
-def token_kernel(lay, begun, place_ref, *refs):
+def token_kernel(lay, first_head, heads, begun, place_ref, *refs):
     count, stride, wide = lay.slots, lay.stride, lay.wide
     slots, refs = refs[:count], refs[count:]
     state_ref, refs = refs[0], refs[1 + begun :]
@@ -220,7 +225,7 @@
         value_all[lay.spread :, :] = jnp.zeros(tail, value_all.dtype)
     for i, ref in enumerate(slots):
         rows = pl.ds(pl.multiple_of(place_ref[i] * stride, 16), stride)
-        query_all[rows, :] = ref[:stride, :wide]
+        query_all[rows, :] = ref[:stride, first_head * HEAD : (first_head + heads) * HEAD]
         key_all[rows, :] = ref[:stride, wide : wide + HEAD]
         value_all[rows, :] = ref[:stride, wide + HEAD :]
 
@@ -238,6 +243,7 @@
         def one_head(g, carry, first=first, low=low, k_diag=k_diag, v_diag=v_diag, keep=keep):
             lanes = pl.ds(pl.multiple_of(g * HEAD, HEAD), HEAD)
             q = query_all[first : first + stride, lanes]
+            at = first_head + g
             s_diag = jnp.where(keep, nt_dot(q, k_diag), -1e30)
             top = jnp.max(s_diag, axis=1, keepdims=True)
             if low > 0:
@@ -259,11 +265,11 @@
                     value_all[:low, :],
                     preferred_element_type=jnp.float32,
                 )
-            state, sums = state_ref[g, :HEAD, :], state_ref[g, HEAD : HEAD + 1, :]
+            state, sums = state_ref[at, :HEAD, :], state_ref[at, HEAD : HEAD + 1, :]
             out_all[first : first + stride, lanes] = soft / total + read_state(q, state, sums)
             return carry
 
-        lax.fori_loop(0, lay.groups, one_head, 0)
+        lax.fori_loop(0, heads, one_head, 0)
 
     for i, ref in enumerate(outs):
         rows = pl.ds(pl.multiple_of(place_ref[i] * stride, 16), stride)
@@ -305,12 +311,14 @@
             name="memory_write",
         )(self.places, *self.slots)
 
-    def attend(self, state, block=0, blocks=1, begun=()):
+    def attend(self, state, first_head=0, heads=None, block=0, blocks=1, begun=()):
         lay = self.lay
-        out_spec = pl.BlockSpec((lay.stride, lay.wide), lambda i, *_: (0, block))
+        heads = heads or lay.groups
+        wide = heads * HEAD
+        out_spec = pl.BlockSpec((lay.stride, wide), lambda i, *_: (0, block))
         return list(
             pl.pallas_call(
-                functools.partial(token_kernel, lay, len(begun)),
+                functools.partial(token_kernel, lay, first_head, heads, len(begun)),
                 grid_spec=pltpu.PrefetchScalarGridSpec(
                     num_scalar_prefetch=1,
                     grid=(1,),
@@ -319,13 +327,13 @@
                     + [pl.BlockSpec(memory_space=pl.ANY)] * len(begun),
                     out_specs=[out_spec] * lay.slots,
                     scratch_shapes=[
-                        pltpu.VMEM((lay.spread, lay.wide), jnp.bfloat16),
+                        pltpu.VMEM((lay.spread, wide), jnp.bfloat16),
                         pltpu.VMEM((lay.full, HEAD), jnp.bfloat16),
                         pltpu.VMEM((lay.full, HEAD), jnp.bfloat16),
-                        pltpu.VMEM((lay.spread, lay.wide), jnp.float32),
+                        pltpu.VMEM((lay.spread, wide), jnp.float32),
                     ],
                 ),
-                out_shape=[jax.ShapeDtypeStruct((lay.stride, blocks * lay.wide), jnp.bfloat16)]
+                out_shape=[jax.ShapeDtypeStruct((lay.stride, blocks * wide), jnp.bfloat16)]
                 * lay.slots,
                 input_output_aliases={2 + lay.slots + i: i for i in range(len(begun))},
                 compiler_params=pltpu.CompilerParams(vmem_limit_bytes=VMEM_LIMIT),
@@ -366,116 +374,97 @@
     return prefix, results
 
 
-def output_kernel(plan, bufs, picks, final, ids_ref, mixed_ref, other_ref, own_ref, *refs):
-    count = 1 + max(p for row in plan for parts in row if parts is not None for p in parts)
+def output_kernel(plan, low, final, ids_ref, mixed_ref, other_ref, own_ref, *refs):
+    count = 1 + max(p for row in plan for p in row if p is not None)
     piece_refs, refs = refs[:count], refs[count:]
     if final:
-        base_ref, begun_ref, out_ref, far_ref, weights, total, sems = refs
+        base_ref, begun_ref, out_ref, far_ref, both, weights, sems = refs
     else:
-        out_ref, weights, total, sems = refs
-    rows = mixed_ref.shape[1]
-    blocks, groups = len(plan), len(plan[0])
-    width = weights.shape[2]
-    c, g = pl.program_id(0), pl.program_id(1)
-    step = c * groups + g
-    steps = blocks * groups
+        out_ref, both, weights, sems = refs
+    rows = mixed_ref.shape[0]
+    blocks = len(plan)
+    _, depth, width = weights.shape
+    step = pl.program_id(0)
 
     def start(at):
-        slot = lax.rem(at, bufs)
+        slot = lax.rem(at, 2)
         for b in range(blocks):
-            for j in range(groups):
-
-                @pl.when(at == b * groups + j)
-                def _():
-                    if plan[b][j] is None:
+
+            @pl.when(at == b)
+            def _():
+                row = 0
+                for index in plan[b]:
+                    if index is None:
                         columns = pl.ds(pl.multiple_of(ids_ref[b] * width, 128), width)
-                        pltpu.make_async_copy(
-                            own_ref.at[:, columns], weights.at[slot], sems.at[slot]
-                        ).start()
-                        return
-                    row = 0
-                    for index in plan[b][j]:
+                        part = own_ref.at[:, columns]
+                    else:
                         part = piece_refs[index]
-                        high = part.shape[0]
-                        pltpu.make_async_copy(
-                            part, weights.at[slot, pl.ds(row, high), :], sems.at[slot]
-                        ).start()
-                        row += high
+                    high = part.shape[0]
+                    pltpu.make_async_copy(
+                        part, weights.at[slot, pl.ds(row, high), :], sems.at[slot]
+                    ).start()
+                    row += high
 
     @pl.when(step == 0)
     def _():
-        for at in range(min(bufs - 1, steps)):
-            start(jnp.int32(at))
-
-    @pl.when(step + bufs - 1 < steps)
+        start(jnp.int32(0))
+        both[:rows, :] = mixed_ref[:, low : low + depth]
+        both[rows:, :] = other_ref[:, low : low + depth]
+
+    @pl.when(step + 1 < blocks)
     def _():
-        start(step + bufs - 1)
-
-    slot = lax.rem(step, bufs)
+        start(step + 1)
+
+    slot = lax.rem(step, 2)
     pltpu.make_async_copy(weights.at[slot], weights.at[slot], sems.at[slot]).wait()
-    both = jnp.concatenate([mixed_ref[picks + g], other_ref[picks + g]], axis=0)
-    term = jnp.dot(both, weights[slot], preferred_element_type=jnp.float32)
-
-    @pl.when(g == 0)
-    def _():
-        total[...] = term + begun_ref[0] if final else term
-
-    @pl.when(g > 0)
-    def _():
-        total[...] = total[...] + term
-
-    @pl.when(g == groups - 1)
-    def _():
-        if final:
-            base = base_ref[...].astype(jnp.float32)
-            out_ref[...] = (base + total[:rows, :]).astype(out_ref.dtype)
-            far_ref[...] = total[rows:, :].astype(far_ref.dtype)
-        else:
-            out_ref[0] = total[...]
-
-
-def output_product(mixed, other, tokens, w_out, gathered, begun=None):
-    count, rows, depth = mixed.shape
+    term = jnp.dot(both[...], weights[slot], preferred_element_type=jnp.float32)
+    if final:
+        term = term + begun_ref[0].astype(jnp.float32)
+        base = base_ref[...].astype(jnp.float32)
+        out_ref[...] = (base + term[:rows, :]).astype(out_ref.dtype)
+        far_ref[...] = term[rows:, :].astype(far_ref.dtype)
+    else:
+        out_ref[0] = term.astype(out_ref.dtype)
+
+
+def output_product(mixed, other, tokens, w_out, ids, gathered, begun=None):
+    rows = mixed.shape[0]
     final = begun is not None
     blocks = len(gathered[0])
     width = w_out.shape[1] // (2 * blocks)
-    chips = jnp.stack([gathered[0][b][1] for b in range(blocks)]).astype(jnp.int32)
-    ids = (lax.axis_index("seg") % 2) * blocks + chips
     plan, pieces = [], []
     for b in range(blocks):
         row = [] if final else [None]
-        for pieces_of in gathered:
-            parts = pieces_of[b][0]
-            row.append(tuple(range(len(pieces), len(pieces) + len(parts))))
-            pieces += parts
+        for parts in gathered:
+            row += range(len(pieces), len(pieces) + len(parts[b]))
+            pieces += parts[b]
         plan.append(row)
-    groups = len(plan[0])
-    picks = count - groups if final else 0
-    bufs = 4
-    whole = pl.BlockSpec((rows, width), lambda c, g, ids: (0, ids[c]))
-    half = pl.BlockSpec((rows, width), lambda c, g, ids: (0, lax.rem(ids[c], blocks)))
-    sums = pl.BlockSpec((1, 2 * rows, width), lambda c, g, ids: (c, 0, 0))
-    mixed_spec = pl.BlockSpec((count, rows, depth), lambda c, g, ids: (0, 0, 0))
+    depth = w_out.shape[0] * (len(gathered) + (0 if final else 1))
+    low = mixed.shape[1] - depth if final else 0
+    whole = pl.BlockSpec((rows, width), lambda c, ids: (0, ids[c]))
+    half = pl.BlockSpec((rows, width), lambda c, ids: (0, lax.rem(ids[c], blocks)))
+    sums = pl.BlockSpec((1, 2 * rows, width), lambda c, ids: (c, 0, 0))
+    mixed_spec = pl.BlockSpec(mixed.shape, lambda c, ids: (0, 0))
     if final:
         shapes = [
             jax.ShapeDtypeStruct((rows, w_out.shape[1]), jnp.bfloat16),
             jax.ShapeDtypeStruct((rows, w_out.shape[1] // 2), jnp.bfloat16),
         ]
     else:
-        shapes = jax.ShapeDtypeStruct((blocks, 2 * rows, width), jnp.float32)
+        shapes = jax.ShapeDtypeStruct((blocks, 2 * rows, width), jnp.bfloat16)
     return pl.pallas_call(
-        functools.partial(output_kernel, plan, bufs, picks, final),
+        functools.partial(output_kernel, plan, low, final),
         grid_spec=pltpu.PrefetchScalarGridSpec(
             num_scalar_prefetch=1,
-            grid=(blocks, groups),
+            grid=(blocks,),
             in_specs=[mixed_spec] * 2
             + [pl.BlockSpec(memory_space=pl.ANY)] * (1 + len(pieces))
             + ([whole, sums] if final else []),
             out_specs=[whole, half] if final else sums,
             scratch_shapes=[
-                pltpu.VMEM((bufs, depth, width), jnp.bfloat16),
-                pltpu.VMEM((2 * rows, width), jnp.float32),
-                pltpu.SemaphoreType.DMA((bufs,)),
+                pltpu.VMEM((2 * rows, depth), jnp.bfloat16),
+                pltpu.VMEM((2, depth, width), jnp.bfloat16),
+                pltpu.SemaphoreType.DMA((2,)),
             ],
         ),
         out_shape=shapes,
@@ -571,6 +560,7 @@
         peer = planes.peer(worker, turn)
         places += [peer, planes.partner(peer)]
     places = jnp.stack(places).astype(jnp.int32)
+    ids = (core * chips + ring_order()).astype(jnp.int32)
     own_weights = [w_query, w_key, value_weight]
     numbers = [0, 1] + [2 + 2 * at for at in range(len(turns))]
     far_numbers = [3 + 2 * at for at in range(len(turns))]
@@ -585,40 +575,56 @@
     rows = jnp.concatenate(
         [pad_rows(rms_rows(tokens, gain)), pad_rows(rms_rows(memory_embed, gain))], axis=0
     )
-    lent, peers, near_back, rows, share, lent_shares, rates = gate(
-        lent, peers, near_back, rows, share, lent_shares, rates
+    lent, peers, near_back, rows, share, lent_shares, rates, places, ids = gate(
+        lent, peers, near_back, rows, share, lent_shares, rates, places, ids
     )
 
     lent_all = [lax.all_gather(lent[0], "seg", axis=0, tiled=True)]
-    rows_a = hop(rows, lend)
+    rows_a = [hop(rows[:half_rows], lend)]
     near_rows = [hop(rows, planes.exchange(turn)) for turn in turns]
     rings = [ChipRing(jnp.where(is_end, near_back, peers[0]))]
     (own[0],) = project([[rows]], own_weights, kv_heads)
-    rates = seg_all(tie(rates, own[0]))
+    rates = seg_double(rates, 1)
+    lent += [hop(tie(part, own[0]), lend) for part in lent_shares[1:]]
     held = (rings[0].right, rings[0].left)
-    rows_a, near_rows, held, own, rows, share, lent_shares, peers, rates = gate(
-        rows_a, near_rows, held, own, rows, share, lent_shares, peers, rates
+    rows_a, near_rows, held, own, rows, share, peers, rates, lent = gate(
+        rows_a, near_rows, held, own, rows, share, peers, rates, lent
     )
     rings[0].right, rings[0].left = held
 
-    lent += [hop(part, lend) for part in lent_shares[1:]]
-    far_rows = [[hop(rows_a[:half_rows], planes.exchange(turn))] for turn in turns]
+    lent_all += [lax.all_gather(part, "seg", axis=0, tiled=True) for part in lent[1:]]
+    far_rows = [[hop(rows_a[0], planes.exchange(turn))] for turn in turns]
+    rows_a.append(hop(rows[half_rows:], lend))
     ends = [hop(piece, back) for piece in peers]
-    closed = rings[0].close()
-    known = [[rows], [rows_a]] + [[x] for x in near_rows]
-    own.update(zip(numbers[1:], project(known[1:], own_weights, kv_heads)))
-    lent, far_rows, ends, rings[0].last, own, known, lent_all, share, rows_a = gate(
-        lent, far_rows, ends, closed, own, known, lent_all, share, rows_a
+    rings[0].close()
+    rates = seg_double(rates, 2)
+    known = [[rows], rows_a] + [[x] for x in near_rows]
+    own.update(zip(numbers[2:], project(known[2:], own_weights, kv_heads)))
+    first = tie(lent_all[0], own[2])
+    here = [known[0]] + known[2:]
+    taken[0].update(zip([0] + numbers[2:], project(here, [first])))
+    far_rows, ends, rings[0].last, own, known, first, share, rates, taken = gate(
+        far_rows, ends, rings[0].last, own, known, first, share, rates, taken
     )
-
-    lent_all += [lax.all_gather(part, "seg", axis=0, tiled=True) for part in lent[1:]]
+    lent_all[0] = first
+    bit = 4
+    while bit < seg_count:
+        rates = seg_double(rates, bit)
+        bit *= 2
+
     for parts, turn in zip(far_rows, turns):
-        parts.append(hop(rows_a[half_rows:], planes.exchange(turn)))
+        parts.append(hop(known[1][1], planes.exchange(turn)))
     near = hop(share, lend)
-    taken[0].update(zip(numbers, project(known, [lent_all[0]])))
-    far_rows, near, taken, known, ends = gate(far_rows, near, taken, known, ends)
-
-    far_near = [hop(near, planes.exchange(turn)) for turn in turns]
+    (own[1],) = project([known[1]], own_weights, kv_heads)
+    (taken[0][1],) = project([known[1]], [tie(first, own[1])])
+    for h in range(1, kv_heads):
+        lent_all[h] = tie(lent_all[h], taken[h - 1])
+        taken[h].update(zip(numbers, project(known, [lent_all[h]])))
+    far_rows, near, taken, own, ends, rates = gate(far_rows, near, taken, own, ends, rates)
+
+    cut = near.shape[0] // 2
+    cuts = (near[:cut], near[cut:])
+    far_near = [[hop(part, planes.exchange(turn)) for part in cuts] for turn in turns]
     for end, mid in zip(ends, peers[1:] + [near]):
         rings.append(ChipRing(jnp.where(is_end, end, mid)))
     own.update(zip(far_numbers, project(far_rows, own_weights, kv_heads)))
@@ -631,40 +637,48 @@
         taken[0].update(zip(far_numbers, project([tie(x, dep) for x in far_rows], [lent_all[0]])))
         return taken[0][far_numbers[-1]]
 
-    def other_lent(dep, h):
-        part = tie(lent_all[h], dep)
-        taken[h].update(zip(numbers + far_numbers, project(known + far_rows, [part])))
+    backs = []
+
+    def close_rings():
+        held = gate(*[(ring.right, ring.left) for ring in rings[1:]])
+        for ring, (right, left) in zip(rings[1:], held):
+            ring.right, ring.left = right, left
+        halves = gate(*[ring.halves() for ring in rings[1:]])
+        for ring, pair in zip(rings[1:], halves):
+            ring.close(pair)
+        return halves
+
+    def far_lent(dep, h):
+        part, dep, early = gate(lent_all[h], dep, [parts[0] for parts in far_near])
+        if h == 1:
+            backs.extend([hop(piece, back)] for piece in early)
+        xs = [[tie(x, dep) for x in xs] for xs in far_rows]
+        taken[h].update(zip(far_numbers, project(xs, [part])))
         return taken[h][far_numbers[-1]]
 
+    lent_writes = []
+
+    def write_lent(dep):
+        dep = tie(dep, close_rings())
+        lent_units.extend(Unit(lay, places, [part[slot] for slot in order]) for part in taken)
+        lent_writes.extend(unit.tied(dep).memory_write() for unit in lent_units)
+        return lent_writes[-1]
+
+    lent_units = []
     works = [first_lent]
-    works += [functools.partial(other_lent, h=h) for h in range(1, kv_heads)]
+    works += [functools.partial(far_lent, h=h) for h in range(1, kv_heads)]
+    works.append(write_lent)
     state, _ = relay(writes, rates[:, :heads], works)
 
-    held = [(ring.right, ring.left) for ring in rings[1:]]
-    far_near, own_slots, taken, held, state = gate(far_near, own_slots, taken, held, state)
-    for ring, (right, left) in zip(rings[1:], held):
-        ring.right, ring.left = right, left
-        ring.close()
-    backs = [hop(piece, back) for piece in far_near]
+    far_near, own_slots, writes, state, backs = gate(
+        far_near, own_slots, lent_writes, state, backs
+    )
+    if kv_heads == 1:
+        backs = [[hop(parts[0], back)] for parts in far_near]
+    for parts, returned in zip(far_near, backs):
+        returned.append(hop(parts[1], back))
     own_units = [Unit(lay, places, own_slots, h) for h in range(kv_heads)]
-    lent_units = [Unit(lay, places, [part[slot] for slot in order]) for part in taken]
-    writes = jnp.concatenate([u.memory_write() for u in lent_units], axis=0)
-    mixed_own = []
-
-    def attend_own(dep, h):
-        unit = own_units[h].tied(dep)
-        mixed_own[:] = unit.attend(state[h * groups : (h + 1) * groups], h, kv_heads, mixed_own)
-        return mixed_own
-
-    works = [functools.partial(attend_own, h=h) for h in range(kv_heads)]
-    lent_state, _ = relay(writes, rates[:, heads:], works)
-
-    last = rings[-1].last
-    lent_state, mixed_own, backs, last = gate(lent_state, list(mixed_own), backs, last)
-    rings[-1].last = last
-    late = len(rings)
-    for mid, end in zip(far_near, backs):
-        rings.append(ChipRing(tie(jnp.where(is_end, end, mid), last)))
+    writes = jnp.concatenate(writes, axis=0)
 
     def cross(arrays):
         return (
@@ -674,9 +688,47 @@
             [hop(arrays[3 + 2 * at], planes.far_back(turn)) for at, turn in enumerate(turns)],
         )
 
-    crossed = [cross(mixed_own)]
+    parts = 2 if groups % 2 == 0 else 1
+    mixed_own, crossed = [[] for _ in range(kv_heads)], []
+
+    def attend_own(dep, h, part):
+        unit, some = own_units[h].tied(dep), groups // parts
+        if h == 0 and part == parts - 1:
+            unit = unit.tied(rings[-1].last)
+        mixed_own[h] = unit.attend(
+            state[h * groups : (h + 1) * groups], part * some, some, part, parts, mixed_own[h]
+        )
+        if h < kv_heads - 1 and part == parts - 1:
+            crossed.append(cross(mixed_own[h]))
+        return mixed_own[h][0]
+
+    works = [
+        functools.partial(attend_own, h=h, part=part)
+        for h in range(kv_heads)
+        for part in range(parts)
+    ]
+
+    def attend_rest(dep):
+        for number, work in enumerate(works[2:]):
+            dep = work(dep if number == 0 else tie(dep, [c[2:] for c in crossed]))
+        return dep
+
+    passed = works[:2] + [attend_rest] * (len(works) > 2)
+    lent_state, _ = relay(writes, rates[:, heads:], passed)
+    last = rings[-1].last
+    lent_state, last_own, backs, last = gate(lent_state, mixed_own[-1], backs, last)
+    rings[-1].last = last
+
+    late = len(rings)
+    for parts, returned in zip(far_near, backs):
+        stage = [jnp.where(is_end, e, m) for e, m in zip(returned, parts)]
+        rings.append(ChipRing(tie(jnp.concatenate(stage, axis=0), last)))
+
+    crossed.append(cross(last_own))
     for h, unit in enumerate(lent_units):
-        crossed.append(cross(unit.tied(lent_state).attend(lent_state[h * groups : (h + 1) * groups])))
+        if h == len(lent_units) - 1:
+            unit = unit.tied(crossed[kv_heads - 1][1:])
+        crossed.append(cross(unit.attend(lent_state[h * groups : (h + 1) * groups])))
 
     def join(arrays):
         both = jnp.concatenate(arrays, axis=1)
@@ -688,18 +740,20 @@
     far_mixed = [join([c[3][at] for c in crossed]) for at in range(len(turns))]
     ends = [returned[1], returned[0]] + [m[0] for m in far_mixed] + [m[1] for m in far_mixed]
     mids = [home[0]] + [m[0] for m in near_mixed] + [home[1]] + [m[1] for m in near_mixed]
-    mixed = jnp.stack([jnp.where(is_end, e, m) for e, m in zip(ends, mids)])
+    mixed = jnp.concatenate([jnp.where(is_end, e, m) for e, m in zip(ends, mids)], axis=1)
 
     held = [(ring.right, ring.left) for ring in rings[late:]]
     mixed, held = gate(mixed, held)
     for ring, (right, left) in zip(rings[late:], held):
         ring.right, ring.left = right, left
         ring.close()
-    gathered = [ring.pieces() for ring in rings]
     other = swap_cores(mixed)
     base = pad_rows(tokens)
-    begun = output_product(mixed, other, base, w_out, gathered[:late])
-    result, other = output_product(mixed, other, base, w_out, gathered[late:], begun)
+    begun = output_product(mixed, other, base, w_out, ids, [r.pieces() for r in rings[:late]])
+    for ring in rings[late:]:
+        ring.last = tie(ring.last, begun)
+    far_pieces = [ring.pieces() for ring in rings[late:]]
+    result, other = output_product(mixed, other, base, w_out, ids, far_pieces, begun)
     other = swap_cores(other)
     start = (1 - core) * half
     base = lax.dynamic_slice_in_dim(base, start, half, 1)

time: 586 us -> 542 us (0.925)
  waiting for transfers between devices: 196 us -> 121 us
  starting transfers between devices: 80.6 us -> 104 us
  Pallas kernels: 212 us -> 229 us
    ppermute x3, waiting for transfers between devices: 53.9 us -> 0.82 us  [seg_double(): got = lax.ppermute(values, 'seg', [(i, i ^ bit) for i in range(size)])]
    ppermute x22 -> x28, starting transfers between devices: 49.4 us -> 70.5 us  [hop(): return lax.ppermute(block, 'tensor', pairs)]
    ppermute x6, waiting for transfers between devices: 20.3 us -> 0.02 us  [relay(): got = lax.ppermute(sent, 'seg', route)]
    pallas_call x6 -> x9, Pallas kernels: 111 us -> 131 us  [project(): pl.pallas_call(functools.partial(project_kernel, heights, len(weights), k...]
    ppermute x22 -> x28, waiting for transfers between devices: 118 us -> 101 us  [hop(): return lax.ppermute(block, 'tensor', pairs)]
    ppermute x12, waiting for transfers between devices: 0.03 us -> 9.7 us  [step(): return lax.ppermute(part, 'seg', route)]
    ppermute x2, starting transfers between devices: 5.02 us -> 13.7 us  [swap_cores(): lax.ppermute(block, 'seg', [(i, i ^ 1) for i in range(lax.axis_size('seg'...]
    unnamed x112 -> x61, local copies, waits for them, and re-layouts: 16 us -> 8.18 us
  transfers between devices with their start and end apart: 47 -> 53, of which waited for: 20 -> 16; matrix products, arithmetic and copies ran while one was open for 8% -> 8% of each run, Pallas kernels for 35% -> 41%
where the time goes in v3:
time: 542 us; the launch traced here: 533 us
  Pallas kernels  229 us (42%)
  waiting for transfers between devices  121 us (22%)
  starting transfers between devices  104 us (19%)
  local copies, waits for them, and re-layouts  36.3 us (7%)
  other arithmetic  28 us (5%)
  between operations  15 us (3%)
    pallas_call x9, Pallas kernels, project(): pl.pallas_call(functools.partial(project_kernel, heights, len(weights), k...  131 us
    ppermute x28, waiting for transfers between devices, hop(): return lax.ppermute(block, 'tensor', pairs)  101 us
    ppermute x28, starting transfers between devices, hop(): return lax.ppermute(block, 'tensor', pairs)  70.5 us
    pallas_call x6, Pallas kernels, attend(): pl.pallas_call(functools.partial(token_kernel, lay, first_head, heads, le...  54.4 us
    pallas_call x2, Pallas kernels, output_product(): pl.pallas_call(functools.partial(output_kernel, plan, low, final), grid_s...  32.8 us
    ppermute x2, starting transfers between devices, swap_cores(): lax.ppermute(block, 'seg', [(i, i ^ 1) for i in range(lax.axis_size('seg'...  13.7 us
    pallas_call x4, Pallas kernels, memory_write(): pl.pallas_call(functools.partial(memory_kernel, lay), grid_spec=pltpu.Pre...  11 us
    slice x6, local copies, waits for them, and re-layouts, halves(): return (self.right[-1][:half], self.left[-1][half:])  10.9 us
  transfers between devices with their start and end apart: 53, of which 16 were waited for; matrix products, arithmetic and copies ran while one was open for 8% of the time, Pallas kernels for 41%

profile of v3, /device:TPU:9, one launch (start us, length us, event | category | flops | bytes accessed | tf_op | source)
XLA Modules:
  0.0 532.9 jit_solution(1362945560389493961)
XLA Ops:
  6.5 3.1 constant_dynamic-slice_fusion
  11.1 5.1 collective-permute-start.1
  25.8 3.4 fusion.2
  31.3 5.0 pad_maximum_fusion.refs_0_
  36.4 22.4 %collective-permute-done = bf16[1024,768]{1,0:T(8,128)(2,1)} collective-permute-done((bf16[1024,768]{1,0:T(8,128)(2,1)}, bf16[1024,768]{1,0:T(8,128)(2,1)}, u32[]{:S(2)}, u32[]{:S(2)}) %collective-permute-start) | collective-permute-done | bytes 1572896 | tf_op jit(solution)/shard_map/ppermute | solution.py:68
  61.6 3.0 collective-permute-start.5
  64.7 3.3 slice.66
  73.1 17.1 %project.9.refs_0_ = bf16[288,1536]{1,0:T(8,128)(2,1)S(1)} custom-call(bf16[288,8192]{1,0:T(8,128)(2,1)} %pad_maximum_fusion.refs_0_, bf16[8192,1024]{1,0:T(8,128)(2,1)} %refs_2_.7, bf16[8192,256]{1,0:T(8,128)(2,1)S(1)} %copy-done.1, bf16[8192,256]{1,0:T(8,128)(2,1)} %refs_4_.3), custom_call_target="tpu_custom_call" | custom-call | flops 1 | bytes 1 | tf_op jit(solution)/shard_map/project/pallas_call | solution.py:518
  95.2 59.6 %collective-permute-done.9 = bf16[1024,768]{1,0:T(8,128)(2,1)} collective-permute-done((bf16[1024,768]{1,0:T(8,128)(2,1)}, bf16[1024,768]{1,0:T(8,128)(2,1)}, u32[]{:S(2)}, u32[]{:S(2)}) %collective-permute-start.9) | collective-permute-done | bytes 1572896 | tf_op jit(solution)/shard_map/ppermute | solution.py:68
  155.8 9.8 %collective-permute-done.5.refs_0_.refs_1_.refs_3_ = bf16[288,8192]{1,0:T(8,128)(2,1)} collective-permute-done((bf16[288,8192]{1,0:T(8,128)(2,1)}, bf16[288,8192]{1,0:T(8,128)(2,1)}, u32[]{:S(2)}, u32[]{:S(2)}) %collective-permute-start.5) | collective-permute-done | bytes 4718624 | tf_op jit(solution)/shard_map/ppermute | solution.py:68
  165.6 3.3 slice.69
  172.9 6.1 %collective-permute-start.11 = (bf16[1024,1024]{1,0:T(8,128)(2,1)}, bf16[1024,1024]{1,0:T(8,128)(2,1)}, u32[]{:S(2)}, u32[]{:S(2)}) collective-permute-start(bf16[1024,1024]{1,0:T(8,128)(2,1)} %collective-permute-done.1), channel_id=1, source_target_pairs={{1,0},{2,3},{5,4},{6,7},{9,8},{10,11},{13,12},{14,15},{17,16},{18,... | collective-permute-start | bytes 6291464 | tf_op jit(solution)/shard_map/ppermute | solution.py:68
  187.8 16.8 %project.10.refs_2_ = bf16[288,1536]{1,0:T(8,128)(2,1)S(1)} custom-call(bf16[288,8192]{1,0:T(8,128)(2,1)} %collective-permute-done.5.refs_0_.refs_1_.refs_3_, bf16[8192,1024]{1,0:T(8,128)(2,1)} %refs_2_.7, bf16[8192,256]{1,0:T(8,128)(2,1)S(1)} %copy-done.2, bf16[8192,256]{1,0:T(8,128)(2,1)} %refs_4_.3), custom_call_target="tpu_custom_call" | custom-call | flops 1 | bytes 1 | tf_op jit(solution)/shard_map/project/pallas_call | solution.py:518
  207.0 13.1 %project.11 = (bf16[288,768]{1,0:T(8,128)(2,1)S(1)}, bf16[288,768]{1,0:T(8,128)(2,1)S(1)}) custom-call(bf16[288,8192]{1,0:T(8,128)(2,1)S(1)} %copy-done, bf16[288,8192]{1,0:T(8,128)(2,1)} %collective-permute-done.5.refs_0_.refs_1_.refs_3_, bf16[8192,768]{1,0:T(8,128)(2,1)} %all-gather.3.cloned.1.call-done.refs_2_), custom_call_target="tpu_custom_call" | custom-call | flops 1 | bytes 1 | tf_op jit(solution)/shard_map/project/pallas_call | solution.py:518
  220.9 2.9 collective-permute-done.13.refs_7_
  224.2 2.9 collective-permute-start.16
  229.6 17.8 %project.12.refs_1_ = bf16[288,1536]{1,0:T(8,128)(2,1)S(1)} custom-call(bf16[144,8192]{1,0:T(8,128)(2,1)} %collective-permute-done.4.refs_0_.refs_1_, bf16[144,8192]{1,0:T(8,128)(2,1)} %collective-permute-done.14.refs_1_.refs_2_, bf16[8192,1024]{1,0:T(8,128)(2,1)} %refs_2_.7, bf16[8192,256]{1,0:T(8,128)(2,1)} %refs_3_.7, bf16[8192,256]{1,0:T(8,128)(2,1)} %refs_4_.3), custom_call_target="tpu_custom_call" | custom-call | flops 1 | bytes 1 | tf_op jit(solution)/shard_map/project/pallas_call | solution.py:518
  247.5 10.5 %project.13.refs_1_ = bf16[288,768]{1,0:T(8,128)(2,1)S(1)} custom-call(bf16[144,8192]{1,0:T(8,128)(2,1)} %collective-permute-done.4.refs_0_.refs_1_, bf16[144,8192]{1,0:T(8,128)(2,1)} %collective-permute-done.14.refs_1_.refs_2_, bf16[8192,768]{1,0:T(8,128)(2,1)} %all-gather.3.cloned.1.call-done.refs_2_), custom_call_target="tpu_custom_call" | custom-call | flops 1 | bytes 1 | tf_op jit(solution)/shard_map/project/pallas_call | solution.py:518
  258.1 5.3 all-gather.5.cloned.1.call-done.refs_4_.refs_2_
  263.3 17.0 %project.14 = (bf16[288,768]{1,0:T(8,128)(2,1)S(1)}, bf16[288,768]{1,0:T(8,128)(2,1)S(1)}, bf16[288,768]{1,0:T(8,128)(2,1)S(1)}) custom-call(bf16[288,8192]{1,0:T(8,128)(2,1)} %pad_maximum_fusion.refs_0_, bf16[144,8192]{1,0:T(8,128)(2,1)} %collective-permute-done.4.refs_0_.refs_1_, bf16[144,8192]{1,0:T(8,128)(2,1)} %collective-permute-done.14.refs_1_.refs_2_, ...), custom_call_target="tpu_custom_call" | custom-call | flops 1 | bytes 1 | tf_op jit(solution)/shard_map/project/pallas_call | solution.py:518
  280.4 3.6 broadcast_select_fusion.refs_1_
  285.5 3.1 fusion.25
  288.6 3.1 collective-permute-start.19
  291.7 17.4 %project.15.refs_3_ = bf16[288,1536]{1,0:T(8,128)(2,1)S(1)} custom-call(bf16[144,8192]{1,0:T(8,128)(2,1)} %collective-permute-done.10.refs_0_, bf16[144,8192]{1,0:T(8,128)(2,1)} %collective-permute-done.16.refs_1_, bf16[8192,1024]{1,0:T(8,128)(2,1)} %refs_2_.7, bf16[8192,256]{1,0:T(8,128)(2,1)} %refs_3_.7, bf16[8192,256]{1,0:T(8,128)(2,1)} %refs_4_.3), custom_call_target="tpu_custom_call" | custom-call | flops 1 | bytes 1 | tf_op jit(solution)/shard_map/project/pallas_call | solution.py:518
  309.1 2.8 memory_write.5
  311.9 2.8 memory_write.4
  315.9 10.5 %project.16.refs_3_ = bf16[288,768]{1,0:T(8,128)(2,1)S(1)} custom-call(bf16[144,8192]{1,0:T(8,128)(2,1)} %collective-permute-done.10.refs_0_, bf16[144,8192]{1,0:T(8,128)(2,1)} %collective-permute-done.16.refs_1_, bf16[8192,768]{1,0:T(8,128)(2,1)} %all-gather.3.cloned.1.call-done.refs_2_), custom_call_target="tpu_custom_call" | custom-call | flops 1 | bytes 1 | tf_op jit(solution)/shard_map/project/pallas_call | solution.py:518
  332.0 10.5 %project.17.refs_3_ = bf16[288,768]{1,0:T(8,128)(2,1)S(1)} custom-call(bf16[144,8192]{1,0:T(8,128)(2,1)} %collective-permute-done.10.refs_0_, bf16[144,8192]{1,0:T(8,128)(2,1)} %collective-permute-done.16.refs_1_, bf16[8192,768]{1,0:T(8,128)(2,1)} %all-gather.5.cloned.1.call-done.refs_4_.refs_2_), custom_call_target="tpu_custom_call" | custom-call | flops 1 | bytes 1 | tf_op jit(solution)/shard_map/project/pallas_call | solution.py:518
  357.1 7.0 %token_attention.6 = (bf16[272,512]{1,0:T(8,128)(2,1)S(1)}, bf16[272,512]{1,0:T(8,128)(2,1)S(1)}, bf16[272,512]{1,0:T(8,128)(2,1)S(1)}, bf16[272,512]{1,0:T(8,128)(2,1)S(1)}) custom-call(s32[4]{0:T(128)S(1)} %get-tuple-element.167.place_ref, bf16[288,1536]{1,0:T(8,128)(2,1)S(1)} %project.9.refs_0_, bf16[288,1536]{1,0:T(8,128)(2,1)S(1)} %project.12.refs_1_, ...), custom_call_target="tpu_custom_call" | custom-call | flops 1 | bytes 1 | tf_op jit(solution)/shard_map/token_attention/pallas_call | solution.py:320
  365.1 3.3 collective-permute-start.34
  368.4 5.1 collective-permute-done.29.refs_8_
  373.5 7.0 %token_attention.7 = (bf16[272,512]{1,0:T(8,128)(2,1)S(1)}, bf16[272,512]{1,0:T(8,128)(2,1)S(1)}, bf16[272,512]{1,0:T(8,128)(2,1)S(1)}, bf16[272,512]{1,0:T(8,128)(2,1)S(1)}) custom-call(s32[4]{0:T(128)S(1)} %get-tuple-element.167.place_ref, ...), custom_call_target="tpu_custom_call", output_to_operand_aliasing={{0}: (6, {}), {1}: (7, {}), {2}: (8, {}), {3}: (9, {})} | custom-call | flops 1 | bytes 1 | tf_op jit(solution)/shard_map/token_attention/pallas_call | solution.py:320
  381.1 3.1 collective-permute-start.32
  385.7 7.0 %token_attention.8 = (bf16[272,512]{1,0:T(8,128)(2,1)S(1)}, bf16[272,512]{1,0:T(8,128)(2,1)S(1)}, bf16[272,512]{1,0:T(8,128)(2,1)S(1)}, bf16[272,512]{1,0:T(8,128)(2,1)S(1)}) custom-call(s32[4]{0:T(128)S(1)} %get-tuple-element.167.place_ref, bf16[288,1536]{1,0:T(8,128)(2,1)S(1)} %project.9.refs_0_, bf16[288,1536]{1,0:T(8,128)(2,1)S(1)} %project.12.refs_1_, ...), custom_call_target="tpu_custom_call" | custom-call | flops 1 | bytes 1 | tf_op jit(solution)/shard_map/token_attention/pallas_call | solution.py:320
  393.0 7.0 %token_attention.9 = (bf16[272,512]{1,0:T(8,128)(2,1)S(1)}, bf16[272,512]{1,0:T(8,128)(2,1)S(1)}, bf16[272,512]{1,0:T(8,128)(2,1)S(1)}, bf16[272,512]{1,0:T(8,128)(2,1)S(1)}) custom-call(s32[4]{0:T(128)S(1)} %get-tuple-element.167.place_ref, ...), custom_call_target="tpu_custom_call", output_to_operand_aliasing={{0}: (6, {}), {1}: (7, {}), {2}: (8, {}), {3}: (9, {})} | custom-call | flops 1 | bytes 1 | tf_op jit(solution)/shard_map/token_attention/pallas_call | solution.py:320
  403.8 3.8 collective-permute-start.36
  407.6 3.1 collective-permute-start.37
  412.1 3.1 collective-permute-start.40
  415.3 13.2 %token_attention.10 = (bf16[272,512]{1,0:T(8,128)(2,1)S(1)}, bf16[272,512]{1,0:T(8,128)(2,1)S(1)}, bf16[272,512]{1,0:T(8,128)(2,1)S(1)}, bf16[272,512]{1,0:T(8,128)(2,1)S(1)}) custom-call(s32[4]{0:T(128)S(1)} %get-tuple-element.167.place_ref, bf16[288,768]{1,0:T(8,128)(2,1)S(1)} %get-tuple-element.231.refs_0_, bf16[288,768]{1,0:T(8,128)(2,1)S(1)} %project.13.refs_1_, ...), custom_call_target="tpu_custom_call" | custom-call | flops 1 | bytes 1 | tf_op jit(solution)/shard_map/token_attention/pallas_call | solution.py:320
  432.4 13.2 %token_attention.11 = (bf16[272,512]{1,0:T(8,128)(2,1)S(1)}, bf16[272,512]{1,0:T(8,128)(2,1)S(1)}, bf16[272,512]{1,0:T(8,128)(2,1)S(1)}, bf16[272,512]{1,0:T(8,128)(2,1)S(1)}) custom-call(s32[4]{0:T(128)S(1)} %get-tuple-element.167.place_ref, bf16[288,768]{1,0:T(8,128)(2,1)S(1)} %copy-done.6, bf16[288,768]{1,0:T(8,128)(2,1)S(1)} %copy-done.8, ...), custom_call_target="tpu_custom_call" | custom-call | flops 1 | bytes 1 | tf_op jit(solution)/shard_map/token_attention/pallas_call | solution.py:320
  450.5 2.8 collective-permute-done.39
  453.3 6.1 %collective-permute-start.44 = (bf16[272,512]{1,0:T(8,128)(2,1)S(1)}, bf16[272,512]{1,0:T(8,128)(2,1)S(1)}, u32[]{:S(2)}, u32[]{:S(2)}) collective-permute-start(bf16[272,512]{1,0:T(8,128)(2,1)S(1)} %get-tuple-element.309), channel_id=1, source_target_pairs={{1,2},{2,1},{5,6},{6,5},{9,10},{10,9},{13,14},{14,13},{17,18},{18,... | collective-permute-start | bytes 835592 | tf_op jit(solution)/shard_map/ppermute | solution.py:68
  459.9 3.4 collective-permute-done.44
  465.1 11.8 %collective-permute-start.47 = (bf16[272,4096]{1,0:T(8,128)(2,1)S(1)}, bf16[272,4096]{1,0:T(8,128)(2,1)S(1)}, u32[]{:S(2)}, u32[]{:S(2)}) collective-permute-start(bf16[272,4096]{1,0:T(8,128)(2,1)S(1)} %pad_maximum_fusion.1.mixed_ref), channel_id=1, source_target_pairs={{0,4},{4,0},{8,12},{12,8},{16,20},{20,16},{24,28},{28,24},{1,5},{5... | collective-permute-start | bytes 6684680 | tf_op jit(solution)/shard_map/ppermute | solution.py:77
  482.8 21.5 %output_product.2.refs_6_ = bf16[4,544,1024]{2,1,0:T(8,128)(2,1)} custom-call(s32[4]{0:T(128)S(1)} %get-tuple-element.166.ids_ref, bf16[272,4096]{1,0:T(8,128)(2,1)} %copy-done.12, bf16[272,4096]{1,0:T(8,128)(2,1)} %copy-done.13, bf16[1024,8192]{1,0:T(8,128)(2,1)} %own_ref.3, bf16[1024,1024]{1,0:T(8,128)(2,1)} %copy-done.14, ...), custom_call_target="tpu_custom_call" | custom-call | flops 1 | bytes 1 | tf_op jit(solution)/shard_map/output_product/pallas_call | solution.py:455
  504.4 11.3 %output_product.3 = (bf16[272,8192]{1,0:T(8,128)(2,1)}, bf16[272,4096]{1,0:T(8,128)(2,1)}) custom-call(s32[4]{0:T(128)S(1)} %get-tuple-element.166.ids_ref, bf16[272,4096]{1,0:T(8,128)(2,1)} %copy-done.12, bf16[272,4096]{1,0:T(8,128)(2,1)} %copy-done.13, bf16[1024,8192]{1,0:T(8,128)(2,1)} %own_ref.3, bf16[1024,1024]{1,0:T(8,128)(2,1)S(1)} %pad_maximum_fusion.2.refs_0_, ...), custom_call_target="tpu_custom_call" | custom-call | flops 1 | bytes 1 | tf_op jit(solution)/shard_map/output_product/pallas_call | solution.py:455
  517.7 4.2 collective-permute-done.50
  521.8 3.8 fusion.3
  (204 shorter events, 95.8 us)
Async XLA Ops:
  6.5 198.1 %all-gather.3.cloned.1.call-start = ((), (), s32[]{:S(2)}) async-start(), calls=%async_computation | async-start | bytes 14155776 | tf_op jit(solution)/shard_map/all_gather | solution.py:582
  9.6 49.2 %collective-permute-start.2 = (bf16[1024,1024]{1,0:T(8,128)(2,1)}, bf16[1024,1024]{1,0:T(8,128)(2,1)S(1)}, u32[]{:S(2)}, u32[]{:S(2)}) collective-permute-start(bf16[1024,1024]{1,0:T(8,128)(2,1)} %constant_dynamic-slice_fusion), channel_id=1, source_target_pairs={{1,0},{2,3},{5,4},{6,7},{9,8},{10,11},{13,12},{14,15},{17,16},{18,... | collective-permute-start | bytes 6291464 | tf_op jit(solution)/shard_map/ppermute | solution.py:68
  11.1 50.5 %collective-permute-start.1 = (bf16[1024,1024]{1,0:T(8,128)(2,1)}, bf16[1024,1024]{1,0:T(8,128)(2,1)}, u32[]{:S(2)}, u32[]{:S(2)}) collective-permute-start(bf16[1024,1024]{1,0:T(8,128)(2,1)} %constant_dynamic-slice_fusion), channel_id=1, source_target_pairs={{1,2},{2,1},{5,6},{6,5},{9,10},{10,9},{13,14},{14,13},{17,18},{18,... | collective-permute-start | bytes 6291464 | tf_op jit(solution)/shard_map/ppermute | solution.py:68
  16.2 20.2 %collective-permute-start.3 = (f32[1,8]{1,0:T(1,128)S(1)}, f32[1,8]{1,0:T(1,128)S(1)}, u32[]{:S(2)}, u32[]{:S(2)}) collective-permute-start(f32[1,8]{1,0:T(1,128)S(1)} %copy-done.26), channel_id=1, source_target_pairs={{0,1},{3,2},{4,5},{7,6},{8,9},{11,10},{12,13},{15,14},{16,17},{19,... | collective-permute-start | bytes 104 | tf_op jit(solution)/shard_map/ppermute | solution.py:68
  22.0 36.8 %collective-permute-start = (bf16[1024,768]{1,0:T(8,128)(2,1)}, bf16[1024,768]{1,0:T(8,128)(2,1)}, u32[]{:S(2)}, u32[]{:S(2)}) collective-permute-start(bf16[1024,768]{1,0:T(8,128)(2,1)} %pad_maximum_fusion.3), channel_id=1, source_target_pairs={{0,1},{3,2},{4,5},{7,6},{8,9},{11,10},{12,13},{15,14},{16,17},{19,... | collective-permute-start | bytes 4718600 | tf_op jit(solution)/shard_map/ppermute | solution.py:68
  61.6 201.8 %all-gather.5.cloned.1.call-start = ((), (), s32[]{:S(2)}) async-start(), calls=%async_computation.1 | async-start | bytes 14155776 | tf_op jit(solution)/shard_map/all_gather | solution.py:595
  61.6 104.0 %collective-permute-start.5 = (bf16[288,8192]{1,0:T(8,128)(2,1)}, bf16[288,8192]{1,0:T(8,128)(2,1)}, u32[]{:S(2)}, u32[]{:S(2)}) collective-permute-start(bf16[288,8192]{1,0:T(8,128)(2,1)} %pad_maximum_fusion.refs_0_), channel_id=1, source_target_pairs={{1,2},{2,1},{5,6},{6,5},{9,10},{10,9},{13,14},{14,13},{17,18},{18,... | collective-permute-start | bytes 14155784 | tf_op jit(solution)/shard_map/ppermute | solution.py:68
  67.9 87.9 %collective-permute-start.4 = (bf16[144,8192]{1,0:T(8,128)(2,1)}, bf16[144,8192]{1,0:T(8,128)(2,1)}, u32[]{:S(2)}, u32[]{:S(2)}) collective-permute-start(bf16[144,8192]{1,0:T(8,128)(2,1)} %slice.66), channel_id=1, source_target_pairs={{0,1},{3,2},{4,5},{7,6},{8,9},{11,10},{12,13},{15,14},{16,17},{19,... | collective-permute-start | bytes 7077896 | tf_op jit(solution)/shard_map/ppermute | solution.py:68
  71.6 83.4 %collective-permute-start.7 = (bf16[1024,1024]{1,0:T(8,128)(2,1)S(1)}, bf16[1024,1024]{1,0:T(8,128)(2,1)}, u32[]{:S(2)}, u32[]{:S(2)}) collective-permute-start(bf16[1024,1024]{1,0:T(8,128)(2,1)S(1)} %broadcast_select_fusion.1.refs_0_), channel_id=1, source_target_pairs={{0,16},{4,20},{8,0},{12,4},{24,8},{28,12},{16,24},{20,28},{1,17},{... | collective-permute-start | bytes 6291464 | tf_op jit(solution)/shard_map/ppermute | solution.py:106
  72.9 82.9 %collective-permute-start.6 = (bf16[1024,1024]{1,0:T(8,128)(2,1)S(1)}, bf16[1024,1024]{1,0:T(8,128)(2,1)}, u32[]{:S(2)}, u32[]{:S(2)}) collective-permute-start(bf16[1024,1024]{1,0:T(8,128)(2,1)S(1)} %broadcast_select_fusion.1.refs_0_), channel_id=1, source_target_pairs={{0,8},{4,12},{8,24},{12,28},{24,16},{28,20},{16,0},{20,4},{1,9},{5... | collective-permute-start | bytes 6291464 | tf_op jit(solution)/shard_map/ppermute | solution.py:106
  93.8 60.9 %collective-permute-start.9 = (bf16[1024,768]{1,0:T(8,128)(2,1)}, bf16[1024,768]{1,0:T(8,128)(2,1)}, u32[]{:S(2)}, u32[]{:S(2)}) collective-permute-start(bf16[1024,768]{1,0:T(8,128)(2,1)} %pad_maximum_fusion.4), channel_id=1, source_target_pairs={{0,1},{3,2},{4,5},{7,6},{8,9},{11,10},{12,13},{15,14},{16,17},{19,... | collective-permute-start | bytes 4718600 | tf_op jit(solution)/shard_map/ppermute | solution.py:68
  168.9 55.4 %collective-permute-start.14 = (bf16[144,8192]{1,0:T(8,128)(2,1)}, bf16[144,8192]{1,0:T(8,128)(2,1)}, u32[]{:S(2)}, u32[]{:S(2)}) collective-permute-start(bf16[144,8192]{1,0:T(8,128)(2,1)} %slice.69), channel_id=1, source_target_pairs={{0,1},{3,2},{4,5},{7,6},{8,9},{11,10},{12,13},{15,14},{16,17},{19,... | collective-permute-start | bytes 7077896 | tf_op jit(solution)/shard_map/ppermute | solution.py:68
  170.2 54.1 %collective-permute-start.10 = (bf16[144,8192]{1,0:T(8,128)(2,1)}, bf16[144,8192]{1,0:T(8,128)(2,1)}, u32[]{:S(2)}, u32[]{:S(2)}) collective-permute-start(bf16[144,8192]{1,0:T(8,128)(2,1)} %collective-permute-done.4.refs_0_.refs_1_), channel_id=1, source_target_pairs={{1,2},{2,1},{5,6},{6,5},{9,10},{10,9},{13,14},{14,13},{17,18},{18,... | collective-permute-start | bytes 7077896 | tf_op jit(solution)/shard_map/ppermute | solution.py:68
  172.9 51.3 %collective-permute-start.11 = (bf16[1024,1024]{1,0:T(8,128)(2,1)}, bf16[1024,1024]{1,0:T(8,128)(2,1)}, u32[]{:S(2)}, u32[]{:S(2)}) collective-permute-start(bf16[1024,1024]{1,0:T(8,128)(2,1)} %collective-permute-done.1), channel_id=1, source_target_pairs={{1,0},{2,3},{5,4},{6,7},{9,8},{10,11},{13,12},{14,15},{17,16},{18,... | collective-permute-start | bytes 6291464 | tf_op jit(solution)/shard_map/ppermute | solution.py:68
  184.2 39.6 %collective-permute-start.13 = (bf16[512,1024]{1,0:T(8,128)(2,1)}, bf16[512,1024]{1,0:T(8,128)(2,1)}, u32[]{:S(2)}, u32[]{:S(2)}) collective-permute-start(bf16[512,1024]{1,0:T(8,128)(2,1)} %slice.68), channel_id=1, source_target_pairs={{0,16},{4,20},{8,0},{12,4},{24,8},{28,12},{16,24},{20,28},{1,17},{... | collective-permute-start | bytes 3145736 | tf_op jit(solution)/shard_map/ppermute | solution.py:106
  185.4 38.8 %collective-permute-start.12 = (bf16[512,1024]{1,0:T(8,128)(2,1)S(1)}, bf16[512,1024]{1,0:T(8,128)(2,1)}, u32[]{:S(2)}, u32[]{:S(2)}) collective-permute-start(bf16[512,1024]{1,0:T(8,128)(2,1)S(1)} %slice.67), channel_id=1, source_target_pairs={{0,8},{4,12},{8,24},{12,28},{24,16},{28,20},{16,0},{20,4},{1,9},{5... | collective-permute-start | bytes 3145736 | tf_op jit(solution)/shard_map/ppermute | solution.py:106
  224.2 56.2 %collective-permute-start.16 = (bf16[144,8192]{1,0:T(8,128)(2,1)}, bf16[144,8192]{1,0:T(8,128)(2,1)}, u32[]{:S(2)}, u32[]{:S(2)}) collective-permute-start(bf16[144,8192]{1,0:T(8,128)(2,1)} %collective-permute-done.14.refs_1_.refs_2_), channel_id=1, source_target_pairs={{1,2},{2,1},{5,6},{6,5},{9,10},{10,9},{13,14},{14,13},{17,18},{18,... | collective-permute-start | bytes 7077896 | tf_op jit(solution)/shard_map/ppermute | solution.py:68
  227.2 53.2 %collective-permute-start.17 = (bf16[1024,1024]{1,0:T(8,128)(2,1)}, bf16[1024,1024]{1,0:T(8,128)(2,1)}, u32[]{:S(2)}, u32[]{:S(2)}) collective-permute-start(bf16[1024,1024]{1,0:T(8,128)(2,1)} %constant_dynamic-slice_fusion), channel_id=1, source_target_pairs={{0,1},{3,2},{4,5},{7,6},{8,9},{11,10},{12,13},{15,14},{16,17},{19,... | collective-permute-start | bytes 6291464 | tf_op jit(solution)/shard_map/ppermute | solution.py:68
  228.9 29.1 %collective-permute-start.18 = (f32[4,16]{1,0:T(4,128)S(1)}, f32[4,16]{1,0:T(4,128)S(1)}, u32[]{:S(2)}, u32[]{:S(2)}) collective-permute-start(f32[4,16]{1,0:T(4,128)S(1)} %pad_maximum_fusion.7), channel_id=1, source_target_pairs={{0,16},{4,20},{8,24},{12,28},{16,0},{20,4},{24,8},{28,12},{1,17},{... | collective-permute-start | bytes 776 | tf_op jit(solution)/shard_map/ppermute | solution.py:125
  284.0 59.4 %collective-permute-start.24 = (bf16[1024,1024]{1,0:T(8,128)(2,1)}, bf16[1024,1024]{1,0:T(8,128)(2,1)}, u32[]{:S(2)}, u32[]{:S(2)}) collective-permute-start(bf16[1024,1024]{1,0:T(8,128)(2,1)} %broadcast_select_fusion.refs_1_), channel_id=1, source_target_pairs={{0,16},{4,20},{8,0},{12,4},{24,8},{28,12},{16,24},{20,28},{1,17},{... | collective-permute-start | bytes 6291464 | tf_op jit(solution)/shard_map/ppermute | solution.py:106
  284.6 58.7 %collective-permute-start.23 = (bf16[1024,1024]{1,0:T(8,128)(2,1)}, bf16[1024,1024]{1,0:T(8,128)(2,1)}, u32[]{:S(2)}, u32[]{:S(2)}) collective-permute-start(bf16[1024,1024]{1,0:T(8,128)(2,1)} %broadcast_select_fusion.refs_1_), channel_id=1, source_target_pairs={{0,8},{4,12},{8,24},{12,28},{24,16},{28,20},{16,0},{20,4},{1,9},{5... | collective-permute-start | bytes 6291464 | tf_op jit(solution)/shard_map/ppermute | solution.py:106
  288.6 42.1 %collective-permute-start.19 = (bf16[512,1024]{1,0:T(8,128)(2,1)}, bf16[512,1024]{1,0:T(8,128)(2,1)}, u32[]{:S(2)}, u32[]{:S(2)}) collective-permute-start(bf16[512,1024]{1,0:T(8,128)(2,1)} %get-tuple-element.356), channel_id=1, source_target_pairs={{1,2},{2,1},{5,6},{6,5},{9,10},{10,9},{13,14},{14,13},{17,18},{18,... | collective-permute-start | bytes 3145736 | tf_op jit(solution)/shard_map/ppermute | solution.py:68
  314.7 12.3 %collective-permute-start.21 = (bf16[8,144,128]{2,1,0:T(8,128)(2,1)S(1)}, bf16[8,144,128]{2,1,0:T(8,128)(2,1)S(1)}, u32[]{:S(2)}, u32[]{:S(2)}) collective-permute-start(bf16[8,144,128]{2,1,0:T(8,128)(2,1)S(1)} %fusion.19), channel_id=1, source_target_pairs={{0,4},{4,0},{8,12},{12,8},{16,20},{20,16},{24,28},{28,24},{1,5},{5... | collective-permute-start | bytes 884744 | tf_op jit(solution)/shard_map/ppermute | solution.py:361
  327.2 15.3 %collective-permute-start.22 = (bf16[8,144,128]{2,1,0:T(8,128)(2,1)S(1)}, bf16[8,144,128]{2,1,0:T(8,128)(2,1)S(1)}, u32[]{:S(2)}, u32[]{:S(2)}) collective-permute-start(bf16[8,144,128]{2,1,0:T(8,128)(2,1)S(1)} %fusion.24), channel_id=1, source_target_pairs={{0,8},{4,12},{8,0},{12,4},{16,24},{20,28},{24,16},{28,20},{1,9},{5... | collective-permute-start | bytes 884744 | tf_op jit(solution)/shard_map/ppermute | solution.py:361
  328.5 27.0 %collective-permute-start.20 = (bf16[512,1024]{1,0:T(8,128)(2,1)}, bf16[512,1024]{1,0:T(8,128)(2,1)S(1)}, u32[]{:S(2)}, u32[]{:S(2)}) collective-permute-start(bf16[512,1024]{1,0:T(8,128)(2,1)} %get-tuple-element.355), channel_id=1, source_target_pairs={{1,2},{2,1},{5,6},{6,5},{9,10},{10,9},{13,14},{14,13},{17,18},{18,... | collective-permute-start | bytes 3145736 | tf_op jit(solution)/shard_map/ppermute | solution.py:68
  330.7 24.8 %collective-permute-start.26 = (bf16[512,1024]{1,0:T(8,128)(2,1)}, bf16[512,1024]{1,0:T(8,128)(2,1)S(1)}, u32[]{:S(2)}, u32[]{:S(2)}) collective-permute-start(bf16[512,1024]{1,0:T(8,128)(2,1)} %collective-permute-done.19), channel_id=1, source_target_pairs={{1,0},{2,3},{5,4},{6,7},{9,8},{10,11},{13,12},{14,15},{17,16},{18,... | collective-permute-start | bytes 3145736 | tf_op jit(solution)/shard_map/ppermute | solution.py:68
  343.0 12.1 %collective-permute-start.25 = (bf16[8,144,128]{2,1,0:T(8,128)(2,1)S(1)}, bf16[8,144,128]{2,1,0:T(8,128)(2,1)S(1)}, u32[]{:S(2)}, u32[]{:S(2)}) collective-permute-start(bf16[8,144,128]{2,1,0:T(8,128)(2,1)S(1)} %fusion.9), channel_id=1, source_target_pairs={{0,16},{4,20},{8,24},{12,28},{16,0},{20,4},{24,8},{28,12},{1,17},{... | collective-permute-start | bytes 884744 | tf_op jit(solution)/shard_map/ppermute | solution.py:361
  348.0 25.5 %collective-permute-start.29 = (bf16[512,1024]{1,0:T(8,128)(2,1)}, bf16[512,1024]{1,0:T(8,128)(2,1)S(1)}, u32[]{:S(2)}, u32[]{:S(2)}) collective-permute-start(bf16[512,1024]{1,0:T(8,128)(2,1)} %slice.74), channel_id=1, source_target_pairs={{0,8},{4,12},{8,24},{12,28},{24,16},{28,20},{16,0},{20,4},{1,9},{5... | collective-permute-start | bytes 3145736 | tf_op jit(solution)/shard_map/ppermute | solution.py:106
  348.6 24.9 %collective-permute-start.30 = (bf16[512,1024]{1,0:T(8,128)(2,1)}, bf16[512,1024]{1,0:T(8,128)(2,1)S(1)}, u32[]{:S(2)}, u32[]{:S(2)}) collective-permute-start(bf16[512,1024]{1,0:T(8,128)(2,1)} %slice.75), channel_id=1, source_target_pairs={{0,16},{4,20},{8,0},{12,4},{24,8},{28,12},{16,24},{20,28},{1,17},{... | collective-permute-start | bytes 3145736 | tf_op jit(solution)/shard_map/ppermute | solution.py:106
  355.6 8.5 %collective-permute-start.27 = (bf16[8,144,128]{2,1,0:T(8,128)(2,1)S(1)}, bf16[8,144,128]{2,1,0:T(8,128)(2,1)S(1)}, u32[]{:S(2)}, u32[]{:S(2)}) collective-permute-start(bf16[8,144,128]{2,1,0:T(8,128)(2,1)S(1)} %convert_element_type.72), channel_id=1, source_target_pairs={{0,4},{4,0},{8,12},{12,8},{16,20},{20,16},{24,28},{28,24},{1,5},{5... | collective-permute-start | bytes 884744 | tf_op jit(solution)/shard_map/ppermute | solution.py:361
  364.4 16.1 %collective-permute-start.28 = (bf16[8,144,128]{2,1,0:T(8,128)(2,1)S(1)}, bf16[8,144,128]{2,1,0:T(8,128)(2,1)S(1)}, u32[]{:S(2)}, u32[]{:S(2)}) collective-permute-start(bf16[8,144,128]{2,1,0:T(8,128)(2,1)S(1)} %fusion.23), channel_id=1, source_target_pairs={{0,8},{4,12},{8,0},{12,4},{16,24},{20,28},{24,16},{28,20},{1,9},{5... | collective-permute-start | bytes 884744 | tf_op jit(solution)/shard_map/ppermute | solution.py:361
  365.1 35.4 %collective-permute-start.34 = (bf16[512,1024]{1,0:T(8,128)(2,1)S(1)}, bf16[512,1024]{1,0:T(8,128)(2,1)}, u32[]{:S(2)}, u32[]{:S(2)}) collective-permute-start(bf16[512,1024]{1,0:T(8,128)(2,1)S(1)} %collective-permute-done.20), channel_id=1, source_target_pairs={{1,0},{2,3},{5,4},{6,7},{9,8},{10,11},{13,12},{14,15},{17,16},{18,... | collective-permute-start | bytes 3145736 | tf_op jit(solution)/shard_map/ppermute | solution.py:68
  381.0 19.1 %collective-permute-start.31 = (bf16[8,144,128]{2,1,0:T(8,128)(2,1)S(1)}, bf16[8,144,128]{2,1,0:T(8,128)(2,1)S(1)}, u32[]{:S(2)}, u32[]{:S(2)}) collective-permute-start(bf16[8,144,128]{2,1,0:T(8,128)(2,1)S(1)} %fusion.15), channel_id=1, source_target_pairs={{0,16},{4,20},{8,24},{12,28},{16,0},{20,4},{24,8},{28,12},{1,17},{... | collective-permute-start | bytes 884744 | tf_op jit(solution)/shard_map/ppermute | solution.py:361
  381.1 11.7 %collective-permute-start.32 = (bf16[272,512]{1,0:T(8,128)(2,1)S(1)}, bf16[272,512]{1,0:T(8,128)(2,1)S(1)}, u32[]{:S(2)}, u32[]{:S(2)}) collective-permute-start(bf16[272,512]{1,0:T(8,128)(2,1)S(1)} %get-tuple-element.275), channel_id=1, source_target_pairs={{1,2},{2,1},{5,6},{6,5},{9,10},{10,9},{13,14},{14,13},{17,18},{18,... | collective-permute-start | bytes 835592 | tf_op jit(solution)/shard_map/ppermute | solution.py:68
  384.2 8.8 %collective-permute-start.33 = (bf16[272,512]{1,0:T(8,128)(2,1)S(1)}, bf16[272,512]{1,0:T(8,128)(2,1)S(1)}, u32[]{:S(2)}, u32[]{:S(2)}) collective-permute-start(bf16[272,512]{1,0:T(8,128)(2,1)S(1)} %get-tuple-element.276), channel_id=1, source_target_pairs={{1,3},{2,0},{5,7},{6,4},{9,11},{10,8},{13,15},{14,12},{17,19},{18,... | collective-permute-start | bytes 835592 | tf_op jit(solution)/shard_map/ppermute | solution.py:68
  402.2 61.5 %collective-permute-start.46 = (bf16[1024,1024]{1,0:T(8,128)(2,1)S(1)}, bf16[1024,1024]{1,0:T(8,128)(2,1)S(1)}, u32[]{:S(2)}, u32[]{:S(2)}) collective-permute-start(bf16[1024,1024]{1,0:T(8,128)(2,1)S(1)} %pad_maximum_fusion.2.refs_0_), channel_id=1, source_target_pairs={{0,16},{4,20},{8,0},{12,4},{24,8},{28,12},{16,24},{20,28},{1,17},{... | collective-permute-start | bytes 6291464 | tf_op jit(solution)/shard_map/ppermute | solution.py:106
  403.8 61.2 %collective-permute-start.45 = (bf16[1024,1024]{1,0:T(8,128)(2,1)S(1)}, bf16[1024,1024]{1,0:T(8,128)(2,1)}, u32[]{:S(2)}, u32[]{:S(2)}) collective-permute-start(bf16[1024,1024]{1,0:T(8,128)(2,1)S(1)} %pad_maximum_fusion.2.refs_0_), channel_id=1, source_target_pairs={{0,8},{4,12},{8,24},{12,28},{24,16},{28,20},{16,0},{20,4},{1,9},{5... | collective-permute-start | bytes 6291464 | tf_op jit(solution)/shard_map/ppermute | solution.py:106
  407.6 20.9 %collective-permute-start.37 = (bf16[272,512]{1,0:T(8,128)(2,1)S(1)}, bf16[272,512]{1,0:T(8,128)(2,1)S(1)}, u32[]{:S(2)}, u32[]{:S(2)}) collective-permute-start(bf16[272,512]{1,0:T(8,128)(2,1)S(1)} %get-tuple-element.295), channel_id=1, source_target_pairs={{1,2},{2,1},{5,6},{6,5},{9,10},{10,9},{13,14},{14,13},{17,18},{18,... | collective-permute-start | bytes 835592 | tf_op jit(solution)/shard_map/ppermute | solution.py:68
  410.8 19.2 %collective-permute-start.38 = (bf16[272,512]{1,0:T(8,128)(2,1)S(1)}, bf16[272,512]{1,0:T(8,128)(2,1)S(1)}, u32[]{:S(2)}, u32[]{:S(2)}) collective-permute-start(bf16[272,512]{1,0:T(8,128)(2,1)S(1)} %get-tuple-element.296), channel_id=1, source_target_pairs={{1,3},{2,0},{5,7},{6,4},{9,11},{10,8},{13,15},{14,12},{17,19},{18,... | collective-permute-start | bytes 835592 | tf_op jit(solution)/shard_map/ppermute | solution.py:68
  412.1 33.5 %collective-permute-start.40 = (bf16[272,512]{1,0:T(8,128)(2,1)S(1)}, bf16[272,512]{1,0:T(8,128)(2,1)S(1)}, u32[]{:S(2)}, u32[]{:S(2)}) collective-permute-start(bf16[272,512]{1,0:T(8,128)(2,1)S(1)} %get-tuple-element.303), channel_id=1, source_target_pairs={{1,0},{2,3},{5,4},{6,7},{9,8},{10,11},{13,12},{14,15},{17,16},{18,... | collective-permute-start | bytes 835592 | tf_op jit(solution)/shard_map/ppermute | solution.py:68
  428.5 18.4 %collective-permute-start.35 = (bf16[272,512]{1,0:T(8,128)(2,1)S(1)}, bf16[272,512]{1,0:T(8,128)(2,1)S(1)}, u32[]{:S(2)}, u32[]{:S(2)}) collective-permute-start(bf16[272,512]{1,0:T(8,128)(2,1)S(1)} %get-tuple-element.293), channel_id=1, source_target_pairs={{1,0},{2,3},{5,4},{6,7},{9,8},{10,11},{13,12},{14,15},{17,16},{18,... | collective-permute-start | bytes 835592 | tf_op jit(solution)/shard_map/ppermute | solution.py:68
  429.9 19.2 %collective-permute-start.41 = (bf16[272,512]{1,0:T(8,128)(2,1)S(1)}, bf16[272,512]{1,0:T(8,128)(2,1)S(1)}, u32[]{:S(2)}, u32[]{:S(2)}) collective-permute-start(bf16[272,512]{1,0:T(8,128)(2,1)S(1)} %get-tuple-element.306), channel_id=1, source_target_pairs={{1,3},{2,0},{5,7},{6,4},{9,11},{10,8},{13,15},{14,12},{17,19},{18,... | collective-permute-start | bytes 835592 | tf_op jit(solution)/shard_map/ppermute | solution.py:68
  446.9 13.0 %collective-permute-start.43 = (bf16[272,512]{1,0:T(8,128)(2,1)S(1)}, bf16[272,512]{1,0:T(8,128)(2,1)S(1)}, u32[]{:S(2)}, u32[]{:S(2)}) collective-permute-start(bf16[272,512]{1,0:T(8,128)(2,1)S(1)} %get-tuple-element.308), channel_id=1, source_target_pairs={{1,2},{2,1},{5,6},{6,5},{9,10},{10,9},{13,14},{14,13},{17,18},{18,... | collective-permute-start | bytes 835592 | tf_op jit(solution)/shard_map/ppermute | solution.py:68
  449.2 10.8 %collective-permute-start.42 = (bf16[272,512]{1,0:T(8,128)(2,1)S(1)}, bf16[272,512]{1,0:T(8,128)(2,1)S(1)}, u32[]{:S(2)}, u32[]{:S(2)}) collective-permute-start(bf16[272,512]{1,0:T(8,128)(2,1)S(1)} %get-tuple-element.307), channel_id=1, source_target_pairs={{1,3},{2,0},{5,7},{6,4},{9,11},{10,8},{13,15},{14,12},{17,19},{18,... | collective-permute-start | bytes 835592 | tf_op jit(solution)/shard_map/ppermute | solution.py:68
  453.3 10.0 %collective-permute-start.44 = (bf16[272,512]{1,0:T(8,128)(2,1)S(1)}, bf16[272,512]{1,0:T(8,128)(2,1)S(1)}, u32[]{:S(2)}, u32[]{:S(2)}) collective-permute-start(bf16[272,512]{1,0:T(8,128)(2,1)S(1)} %get-tuple-element.309), channel_id=1, source_target_pairs={{1,2},{2,1},{5,6},{6,5},{9,10},{10,9},{13,14},{14,13},{17,18},{18,... | collective-permute-start | bytes 835592 | tf_op jit(solution)/shard_map/ppermute | solution.py:68
  465.1 16.3 %collective-permute-start.47 = (bf16[272,4096]{1,0:T(8,128)(2,1)S(1)}, bf16[272,4096]{1,0:T(8,128)(2,1)S(1)}, u32[]{:S(2)}, u32[]{:S(2)}) collective-permute-start(bf16[272,4096]{1,0:T(8,128)(2,1)S(1)} %pad_maximum_fusion.1.mixed_ref), channel_id=1, source_target_pairs={{0,4},{4,0},{8,12},{12,8},{16,20},{20,16},{24,28},{28,24},{1,5},{5... | collective-permute-start | bytes 6684680 | tf_op jit(solution)/shard_map/ppermute | solution.py:77
  479.2 25.2 %collective-permute-start.49 = (bf16[512,1024]{1,0:T(8,128)(2,1)}, bf16[512,1024]{1,0:T(8,128)(2,1)S(1)}, u32[]{:S(2)}, u32[]{:S(2)}) collective-permute-start(bf16[512,1024]{1,0:T(8,128)(2,1)} %slice.81), channel_id=1, source_target_pairs={{0,16},{4,20},{8,0},{12,4},{24,8},{28,12},{16,24},{20,28},{1,17},{... | collective-permute-start | bytes 3145736 | tf_op jit(solution)/shard_map/ppermute | solution.py:106
  480.7 23.7 %collective-permute-start.48 = (bf16[512,1024]{1,0:T(8,128)(2,1)S(1)}, bf16[512,1024]{1,0:T(8,128)(2,1)S(1)}, u32[]{:S(2)}, u32[]{:S(2)}) collective-permute-start(bf16[512,1024]{1,0:T(8,128)(2,1)S(1)} %slice.80), channel_id=1, source_target_pairs={{0,8},{4,12},{8,24},{12,28},{24,16},{28,20},{16,0},{20,4},{1,9},{5... | collective-permute-start | bytes 3145736 | tf_op jit(solution)/shard_map/ppermute | solution.py:106
  (35 other events, 290.5 us)
Sparse Core Ops, SparseCore 0:
  61.7 111.0 all-gather.2
  174.6 88.6 all-gather.4

commit v4 on v3

--- a/solution.py
+++ b/solution.py
@@ -374,7 +374,7 @@
     return prefix, results
 
 
-def output_kernel(plan, low, final, ids_ref, mixed_ref, other_ref, own_ref, *refs):
+def output_kernel(plan, final, ids_ref, mixed_ref, other_ref, own_ref, *refs):
     count = 1 + max(p for row in plan for p in row if p is not None)
     piece_refs, refs = refs[:count], refs[count:]
     if final:
@@ -383,7 +383,7 @@
         out_ref, both, weights, sems = refs
     rows = mixed_ref.shape[0]
     blocks = len(plan)
-    _, depth, width = weights.shape
+    width = weights.shape[2]
     step = pl.program_id(0)
 
     def start(at):
@@ -408,8 +408,8 @@
     @pl.when(step == 0)
     def _():
         start(jnp.int32(0))
-        both[:rows, :] = mixed_ref[:, low : low + depth]
-        both[rows:, :] = other_ref[:, low : low + depth]
+        both[:rows, :] = mixed_ref[...]
+        both[rows:, :] = other_ref[...]
 
     @pl.when(step + 1 < blocks)
     def _():
@@ -440,7 +440,6 @@
             pieces += parts[b]
         plan.append(row)
     depth = w_out.shape[0] * (len(gathered) + (0 if final else 1))
-    low = mixed.shape[1] - depth if final else 0
     whole = pl.BlockSpec((rows, width), lambda c, ids: (0, ids[c]))
     half = pl.BlockSpec((rows, width), lambda c, ids: (0, lax.rem(ids[c], blocks)))
     sums = pl.BlockSpec((1, 2 * rows, width), lambda c, ids: (c, 0, 0))
@@ -453,7 +452,7 @@
     else:
         shapes = jax.ShapeDtypeStruct((blocks, 2 * rows, width), jnp.bfloat16)
     return pl.pallas_call(
-        functools.partial(output_kernel, plan, low, final),
+        functools.partial(output_kernel, plan, final),
         grid_spec=pltpu.PrefetchScalarGridSpec(
             num_scalar_prefetch=1,
             grid=(blocks,),
@@ -575,26 +574,29 @@
     rows = jnp.concatenate(
         [pad_rows(rms_rows(tokens, gain)), pad_rows(rms_rows(memory_embed, gain))], axis=0
     )
-    lent, peers, near_back, rows, share, lent_shares, rates, places, ids = gate(
-        lent, peers, near_back, rows, share, lent_shares, rates, places, ids
+    cut = share.shape[0] // 2
+    shares = [share[:cut], share[cut:]]
+    row_parts = [rows[:half_rows], rows[half_rows:]]
+    lent, peers, near_back, rows, row_parts, shares, lent_shares, rates, places, ids = gate(
+        lent, peers, near_back, rows, row_parts, shares, lent_shares, rates, places, ids
     )
 
     lent_all = [lax.all_gather(lent[0], "seg", axis=0, tiled=True)]
-    rows_a = [hop(rows[:half_rows], lend)]
+    rows_a = [hop(row_parts[0], lend)]
     near_rows = [hop(rows, planes.exchange(turn)) for turn in turns]
     rings = [ChipRing(jnp.where(is_end, near_back, peers[0]))]
     (own[0],) = project([[rows]], own_weights, kv_heads)
     rates = seg_double(rates, 1)
     lent += [hop(tie(part, own[0]), lend) for part in lent_shares[1:]]
     held = (rings[0].right, rings[0].left)
-    rows_a, near_rows, held, own, rows, share, peers, rates, lent = gate(
-        rows_a, near_rows, held, own, rows, share, peers, rates, lent
+    rows_a, near_rows, held, own, rows, row_parts, shares, peers, rates, lent = gate(
+        rows_a, near_rows, held, own, rows, row_parts, shares, peers, rates, lent
     )
     rings[0].right, rings[0].left = held
 
     lent_all += [lax.all_gather(part, "seg", axis=0, tiled=True) for part in lent[1:]]
     far_rows = [[hop(rows_a[0], planes.exchange(turn))] for turn in turns]
-    rows_a.append(hop(rows[half_rows:], lend))
+    rows_a.append(hop(row_parts[1], lend))
     ends = [hop(piece, back) for piece in peers]
     rings[0].close()
     rates = seg_double(rates, 2)
@@ -603,8 +605,8 @@
     first = tie(lent_all[0], own[2])
     here = [known[0]] + known[2:]
     taken[0].update(zip([0] + numbers[2:], project(here, [first])))
-    far_rows, ends, rings[0].last, own, known, first, share, rates, taken = gate(
-        far_rows, ends, rings[0].last, own, known, first, share, rates, taken
+    far_rows, ends, rings[0].last, own, known, first, shares, rates, taken = gate(
+        far_rows, ends, rings[0].last, own, known, first, shares, rates, taken
     )
     lent_all[0] = first
     bit = 4
@@ -614,7 +616,7 @@
 
     for parts, turn in zip(far_rows, turns):
         parts.append(hop(known[1][1], planes.exchange(turn)))
-    near = hop(share, lend)
+    near = [hop(part, lend) for part in shares]
     (own[1],) = project([known[1]], own_weights, kv_heads)
     (taken[0][1],) = project([known[1]], [tie(first, own[1])])
     for h in range(1, kv_heads):
@@ -622,9 +624,8 @@
         taken[h].update(zip(numbers, project(known, [lent_all[h]])))
     far_rows, near, taken, own, ends, rates = gate(far_rows, near, taken, own, ends, rates)
 
-    cut = near.shape[0] // 2
-    cuts = (near[:cut], near[cut:])
-    far_near = [[hop(part, planes.exchange(turn)) for part in cuts] for turn in turns]
+    far_near = [[hop(part, planes.exchange(turn)) for part in near] for turn in turns]
+    near = jnp.concatenate(near, axis=0)
     for end, mid in zip(ends, peers[1:] + [near]):
         rings.append(ChipRing(jnp.where(is_end, end, mid)))
     own.update(zip(far_numbers, project(far_rows, own_weights, kv_heads)))
@@ -716,7 +717,9 @@
     passed = works[:2] + [attend_rest] * (len(works) > 2)
     lent_state, _ = relay(writes, rates[:, heads:], passed)
     last = rings[-1].last
-    lent_state, last_own, backs, last = gate(lent_state, mixed_own[-1], backs, last)
+    lent_state, last_own, backs, last, crossed = gate(
+        lent_state, mixed_own[-1], backs, last, crossed
+    )
     rings[-1].last = last
 
     late = len(rings)
@@ -740,16 +743,18 @@
     far_mixed = [join([c[3][at] for c in crossed]) for at in range(len(turns))]
     ends = [returned[1], returned[0]] + [m[0] for m in far_mixed] + [m[1] for m in far_mixed]
     mids = [home[0]] + [m[0] for m in near_mixed] + [home[1]] + [m[1] for m in near_mixed]
-    mixed = jnp.concatenate([jnp.where(is_end, e, m) for e, m in zip(ends, mids)], axis=1)
+    mixed = [jnp.where(is_end, e, m) for e, m in zip(ends, mids)]
+    early = jnp.concatenate(mixed[: -len(turns)], axis=1)
+    mixed = jnp.concatenate(mixed[-len(turns) :], axis=1)
 
     held = [(ring.right, ring.left) for ring in rings[late:]]
-    mixed, held = gate(mixed, held)
+    early, mixed, held = gate(early, mixed, held)
     for ring, (right, left) in zip(rings[late:], held):
         ring.right, ring.left = right, left
         ring.close()
-    other = swap_cores(mixed)
+    other_early, other = swap_cores(early), swap_cores(mixed)
     base = pad_rows(tokens)
-    begun = output_product(mixed, other, base, w_out, ids, [r.pieces() for r in rings[:late]])
+    begun = output_product(early, other_early, base, w_out, ids, [r.pieces() for r in rings[:late]])
     for ring in rings[late:]:
         ring.last = tie(ring.last, begun)
     far_pieces = [ring.pieces() for ring in rings[late:]]

time: 542 us -> 529 us (0.976)
  starting transfers between devices: 104 us -> 93.6 us
  local copies, waits for them, and re-layouts: 36.3 us -> 29.9 us
    slice x3 -> x1, local copies, waits for them, and re-layouts: 9.61 us -> 3.05 us  [per_device(): shares = [share[:cut], share[cut:]]]
    ppermute x2 -> x3, starting transfers between devices: 13.7 us -> 7.32 us  [swap_cores(): lax.ppermute(block, 'seg', [(i, i ^ 1) for i in range(lax.axis_size('seg'...]
    ppermute x28 -> x29, starting transfers between devices: 70.5 us -> 67.1 us  [hop(): return lax.ppermute(block, 'tensor', pairs)]
    ppermute x28 -> x29, waiting for transfers between devices: 101 us -> 104 us  [hop(): return lax.ppermute(block, 'tensor', pairs)]
  transfers between devices with their start and end apart: 53 -> 55, of which waited for: 16 -> 15; matrix products, arithmetic and copies ran while one was open for 8% -> 7% of each run, Pallas kernels for 41% -> 42%
where the time goes in v4:
time: 529 us; the launch traced here: 519 us
  Pallas kernels  227 us (43%)
  waiting for transfers between devices  124 us (23%)
  starting transfers between devices  93.6 us (18%)
  other arithmetic  30.5 us (6%)
  local copies, waits for them, and re-layouts  29.9 us (6%)
  between operations  15 us (3%)
    pallas_call x9, Pallas kernels, project(): pl.pallas_call(functools.partial(project_kernel, heights, len(weights), k...  131 us
    ppermute x29, waiting for transfers between devices, hop(): return lax.ppermute(block, 'tensor', pairs)  104 us
    ppermute x29, starting transfers between devices, hop(): return lax.ppermute(block, 'tensor', pairs)  67.1 us
    pallas_call x6, Pallas kernels, attend(): pl.pallas_call(functools.partial(token_kernel, lay, first_head, heads, le...  54.4 us
    pallas_call x2, Pallas kernels, output_product(): pl.pallas_call(functools.partial(output_kernel, plan, final), grid_spec=p...  30.5 us
    pallas_call x4, Pallas kernels, memory_write(): pl.pallas_call(functools.partial(memory_kernel, lay), grid_spec=pltpu.Pre...  11 us
  transfers between devices with their start and end apart: 55, of which 15 were waited for; matrix products, arithmetic and copies ran while one was open for 7% of the time, Pallas kernels for 42%

profile of v4, /device:TPU:9, one launch (start us, length us, event | category | flops | bytes accessed | tf_op | source)
XLA Modules:
  0.0 519.4 jit_solution(13802203678962614437)
XLA Ops:
  6.5 3.1 constant_dynamic-slice_fusion.1
  12.3 5.1 collective-permute-start.1
  30.7 2.6 fusion.3
  35.2 3.0 fusion.26
  38.3 5.0 pad_maximum_fusion.refs_0_
  43.4 16.6 %collective-permute-done = bf16[1024,768]{1,0:T(8,128)(2,1)} collective-permute-done((bf16[1024,768]{1,0:T(8,128)(2,1)}, bf16[1024,768]{1,0:T(8,128)(2,1)}, u32[]{:S(2)}, u32[]{:S(2)}) %collective-permute-start) | collective-permute-done | bytes 1572896 | tf_op jit(solution)/shard_map/ppermute | solution.py:68
  60.0 2.6 collective-permute-done.1
  62.7 3.3 collective-permute-start.5
  70.7 17.4 %project.9.refs_0_ = bf16[288,1536]{1,0:T(8,128)(2,1)S(1)} custom-call(bf16[288,8192]{1,0:T(8,128)(2,1)} %pad_maximum_fusion.refs_0_, bf16[8192,1024]{1,0:T(8,128)(2,1)} %refs_2_.7, bf16[8192,256]{1,0:T(8,128)(2,1)S(1)} %copy-done.1, bf16[8192,256]{1,0:T(8,128)(2,1)} %refs_4_.3), custom_call_target="tpu_custom_call" | custom-call | flops 1 | bytes 1 | tf_op jit(solution)/shard_map/project/pallas_call | solution.py:517
  92.7 59.8 %collective-permute-done.9 = bf16[1024,768]{1,0:T(8,128)(2,1)} collective-permute-done((bf16[1024,768]{1,0:T(8,128)(2,1)}, bf16[1024,768]{1,0:T(8,128)(2,1)}, u32[]{:S(2)}, u32[]{:S(2)}) %collective-permute-start.9) | collective-permute-done | bytes 1572896 | tf_op jit(solution)/shard_map/ppermute | solution.py:68
  152.5 14.5 %collective-permute-done.5.refs_0_.refs_1_.refs_3_ = bf16[288,8192]{1,0:T(8,128)(2,1)} collective-permute-done((bf16[288,8192]{1,0:T(8,128)(2,1)}, bf16[288,8192]{1,0:T(8,128)(2,1)}, u32[]{:S(2)}, u32[]{:S(2)}) %collective-permute-start.5) | collective-permute-done | bytes 4718624 | tf_op jit(solution)/shard_map/ppermute | solution.py:68
  168.4 2.6 collective-permute-start.10
  171.0 6.1 %collective-permute-start.11 = (bf16[1024,1024]{1,0:T(8,128)(2,1)}, bf16[1024,1024]{1,0:T(8,128)(2,1)}, u32[]{:S(2)}, u32[]{:S(2)}) collective-permute-start(bf16[1024,1024]{1,0:T(8,128)(2,1)} %copy-done.16), channel_id=1, source_target_pairs={{1,0},{2,3},{5,4},{6,7},{9,8},{10,11},{13,12},{14,15},{17,16},{18,... | collective-permute-start | bytes 6291464 | tf_op jit(solution)/shard_map/ppermute | solution.py:68
  183.4 2.7 copy-done.2
  186.1 16.8 %project.10.refs_2_ = bf16[288,1536]{1,0:T(8,128)(2,1)S(1)} custom-call(bf16[288,8192]{1,0:T(8,128)(2,1)} %collective-permute-done.5.refs_0_.refs_1_.refs_3_, bf16[8192,1024]{1,0:T(8,128)(2,1)} %refs_2_.7, bf16[8192,256]{1,0:T(8,128)(2,1)S(1)} %copy-done.2, bf16[8192,256]{1,0:T(8,128)(2,1)} %refs_4_.3), custom_call_target="tpu_custom_call" | custom-call | flops 1 | bytes 1 | tf_op jit(solution)/shard_map/project/pallas_call | solution.py:517
  205.3 13.1 %project.11 = (bf16[288,768]{1,0:T(8,128)(2,1)S(1)}, bf16[288,768]{1,0:T(8,128)(2,1)S(1)}) custom-call(bf16[288,8192]{1,0:T(8,128)(2,1)S(1)} %copy-done, bf16[288,8192]{1,0:T(8,128)(2,1)} %collective-permute-done.5.refs_0_.refs_1_.refs_3_, bf16[8192,768]{1,0:T(8,128)(2,1)} %all-gather.3.cloned.1.call-done.refs_2_), custom_call_target="tpu_custom_call" | custom-call | flops 1 | bytes 1 | tf_op jit(solution)/shard_map/project/pallas_call | solution.py:517
  219.2 3.3 collective-permute-done.13.refs_7_
  229.4 17.7 %project.12.refs_1_ = bf16[288,1536]{1,0:T(8,128)(2,1)S(1)} custom-call(bf16[144,8192]{1,0:T(8,128)(2,1)} %collective-permute-done.4.refs_0_.refs_1_, bf16[144,8192]{1,0:T(8,128)(2,1)} %collective-permute-done.14.refs_1_.refs_2_, bf16[8192,1024]{1,0:T(8,128)(2,1)} %refs_2_.7, bf16[8192,256]{1,0:T(8,128)(2,1)} %refs_3_.7, bf16[8192,256]{1,0:T(8,128)(2,1)} %refs_4_.3), custom_call_target="tpu_custom_call" | custom-call | flops 1 | bytes 1 | tf_op jit(solution)/shard_map/project/pallas_call | solution.py:517
  247.0 10.5 %project.13.refs_1_ = bf16[288,768]{1,0:T(8,128)(2,1)S(1)} custom-call(bf16[144,8192]{1,0:T(8,128)(2,1)} %collective-permute-done.4.refs_0_.refs_1_, bf16[144,8192]{1,0:T(8,128)(2,1)} %collective-permute-done.14.refs_1_.refs_2_, bf16[8192,768]{1,0:T(8,128)(2,1)} %all-gather.3.cloned.1.call-done.refs_2_), custom_call_target="tpu_custom_call" | custom-call | flops 1 | bytes 1 | tf_op jit(solution)/shard_map/project/pallas_call | solution.py:517
  257.6 4.6 all-gather.5.cloned.1.call-done.refs_4_.refs_2_
  262.2 17.0 %project.14 = (bf16[288,768]{1,0:T(8,128)(2,1)S(1)}, bf16[288,768]{1,0:T(8,128)(2,1)S(1)}, bf16[288,768]{1,0:T(8,128)(2,1)S(1)}) custom-call(bf16[288,8192]{1,0:T(8,128)(2,1)} %pad_maximum_fusion.refs_0_, bf16[144,8192]{1,0:T(8,128)(2,1)} %collective-permute-done.4.refs_0_.refs_1_, bf16[144,8192]{1,0:T(8,128)(2,1)} %collective-permute-done.14.refs_1_.refs_2_, ...), custom_call_target="tpu_custom_call" | custom-call | flops 1 | bytes 1 | tf_op jit(solution)/shard_map/project/pallas_call | solution.py:517
  279.3 4.3 maximum_select_fusion.refs_1_
  285.1 3.1 collective-permute-start.20
  288.3 17.4 %project.15.refs_3_ = bf16[288,1536]{1,0:T(8,128)(2,1)S(1)} custom-call(bf16[144,8192]{1,0:T(8,128)(2,1)} %collective-permute-done.10.refs_0_, bf16[144,8192]{1,0:T(8,128)(2,1)} %collective-permute-done.16.refs_1_, bf16[8192,1024]{1,0:T(8,128)(2,1)} %refs_2_.7, bf16[8192,256]{1,0:T(8,128)(2,1)} %refs_3_.7, bf16[8192,256]{1,0:T(8,128)(2,1)} %refs_4_.3), custom_call_target="tpu_custom_call" | custom-call | flops 1 | bytes 1 | tf_op jit(solution)/shard_map/project/pallas_call | solution.py:517
  305.7 2.8 memory_write.5
  308.5 2.8 memory_write.4
  312.4 10.5 %project.16.refs_3_ = bf16[288,768]{1,0:T(8,128)(2,1)S(1)} custom-call(bf16[144,8192]{1,0:T(8,128)(2,1)} %collective-permute-done.10.refs_0_, bf16[144,8192]{1,0:T(8,128)(2,1)} %collective-permute-done.16.refs_1_, bf16[8192,768]{1,0:T(8,128)(2,1)} %all-gather.3.cloned.1.call-done.refs_2_), custom_call_target="tpu_custom_call" | custom-call | flops 1 | bytes 1 | tf_op jit(solution)/shard_map/project/pallas_call | solution.py:517
  328.2 10.5 %project.17.refs_3_ = bf16[288,768]{1,0:T(8,128)(2,1)S(1)} custom-call(bf16[144,8192]{1,0:T(8,128)(2,1)} %collective-permute-done.10.refs_0_, bf16[144,8192]{1,0:T(8,128)(2,1)} %collective-permute-done.16.refs_1_, bf16[8192,768]{1,0:T(8,128)(2,1)} %all-gather.5.cloned.1.call-done.refs_4_.refs_2_), custom_call_target="tpu_custom_call" | custom-call | flops 1 | bytes 1 | tf_op jit(solution)/shard_map/project/pallas_call | solution.py:517
  346.0 2.7 memory_write.7
  348.7 2.7 memory_write.6
  353.5 7.0 %token_attention.6 = (bf16[272,512]{1,0:T(8,128)(2,1)S(1)}, bf16[272,512]{1,0:T(8,128)(2,1)S(1)}, bf16[272,512]{1,0:T(8,128)(2,1)S(1)}, bf16[272,512]{1,0:T(8,128)(2,1)S(1)}) custom-call(s32[4]{0:T(128)S(1)} %get-tuple-element.179.place_ref, bf16[288,1536]{1,0:T(8,128)(2,1)S(1)} %project.9.refs_0_, bf16[288,1536]{1,0:T(8,128)(2,1)S(1)} %project.12.refs_1_, ...), custom_call_target="tpu_custom_call" | custom-call | flops 1 | bytes 1 | tf_op jit(solution)/shard_map/token_attention/pallas_call | solution.py:320
  362.2 2.7 collective-permute-start.35
  364.9 4.9 collective-permute-done.30.refs_8_
  369.8 7.0 %token_attention.7 = (bf16[272,512]{1,0:T(8,128)(2,1)S(1)}, bf16[272,512]{1,0:T(8,128)(2,1)S(1)}, bf16[272,512]{1,0:T(8,128)(2,1)S(1)}, bf16[272,512]{1,0:T(8,128)(2,1)S(1)}) custom-call(s32[4]{0:T(128)S(1)} %get-tuple-element.179.place_ref, ...), custom_call_target="tpu_custom_call", output_to_operand_aliasing={{0}: (6, {}), {1}: (7, {}), {2}: (8, {}), {3}: (9, {})} | custom-call | flops 1 | bytes 1 | tf_op jit(solution)/shard_map/token_attention/pallas_call | solution.py:320
  377.4 2.8 collective-permute-start.33
  383.1 7.0 %token_attention.8 = (bf16[272,512]{1,0:T(8,128)(2,1)S(1)}, bf16[272,512]{1,0:T(8,128)(2,1)S(1)}, bf16[272,512]{1,0:T(8,128)(2,1)S(1)}, bf16[272,512]{1,0:T(8,128)(2,1)S(1)}) custom-call(s32[4]{0:T(128)S(1)} %get-tuple-element.179.place_ref, bf16[288,1536]{1,0:T(8,128)(2,1)S(1)} %project.9.refs_0_, bf16[288,1536]{1,0:T(8,128)(2,1)S(1)} %project.12.refs_1_, ...), custom_call_target="tpu_custom_call" | custom-call | flops 1 | bytes 1 | tf_op jit(solution)/shard_map/token_attention/pallas_call | solution.py:320
  390.1 7.0 %token_attention.9 = (bf16[272,512]{1,0:T(8,128)(2,1)S(1)}, bf16[272,512]{1,0:T(8,128)(2,1)S(1)}, bf16[272,512]{1,0:T(8,128)(2,1)S(1)}, bf16[272,512]{1,0:T(8,128)(2,1)S(1)}) custom-call(s32[4]{0:T(128)S(1)} %get-tuple-element.179.place_ref, ...), custom_call_target="tpu_custom_call", output_to_operand_aliasing={{0}: (6, {}), {1}: (7, {}), {2}: (8, {}), {3}: (9, {})} | custom-call | flops 1 | bytes 1 | tf_op jit(solution)/shard_map/token_attention/pallas_call | solution.py:320
  402.1 4.1 collective-permute-start.38
  406.2 3.7 collective-permute-start.39
  412.0 13.2 %token_attention.10 = (bf16[272,512]{1,0:T(8,128)(2,1)S(1)}, bf16[272,512]{1,0:T(8,128)(2,1)S(1)}, bf16[272,512]{1,0:T(8,128)(2,1)S(1)}, bf16[272,512]{1,0:T(8,128)(2,1)S(1)}) custom-call(s32[4]{0:T(128)S(1)} %get-tuple-element.179.place_ref, bf16[288,768]{1,0:T(8,128)(2,1)S(1)} %get-tuple-element.250.refs_0_, bf16[288,768]{1,0:T(8,128)(2,1)S(1)} %project.13.refs_1_, ...), custom_call_target="tpu_custom_call" | custom-call | flops 1 | bytes 1 | tf_op jit(solution)/shard_map/token_attention/pallas_call | solution.py:320
  428.3 13.2 %token_attention.11 = (bf16[272,512]{1,0:T(8,128)(2,1)S(1)}, bf16[272,512]{1,0:T(8,128)(2,1)S(1)}, bf16[272,512]{1,0:T(8,128)(2,1)S(1)}, bf16[272,512]{1,0:T(8,128)(2,1)S(1)}) custom-call(s32[4]{0:T(128)S(1)} %get-tuple-element.179.place_ref, bf16[288,768]{1,0:T(8,128)(2,1)S(1)} %copy-done.6, bf16[288,768]{1,0:T(8,128)(2,1)S(1)} %copy-done.8, ...), custom_call_target="tpu_custom_call" | custom-call | flops 1 | bytes 1 | tf_op jit(solution)/shard_map/token_attention/pallas_call | solution.py:320
  446.2 3.2 collective-permute-start.45
  453.1 8.3 %collective-permute-done.45 = bf16[272,512]{1,0:T(8,128)(2,1)S(1)} collective-permute-done((bf16[272,512]{1,0:T(8,128)(2,1)S(1)}, bf16[272,512]{1,0:T(8,128)(2,1)S(1)}, u32[]{:S(2)}, u32[]{:S(2)}) %collective-permute-start.45) | collective-permute-done | bytes 278560 | tf_op jit(solution)/shard_map/ppermute | solution.py:68
  461.8 4.3 collective-permute-start.51
  471.0 20.6 %output_product.2.refs_6_ = bf16[4,544,1024]{2,1,0:T(8,128)(2,1)} custom-call(s32[4]{0:T(128)S(1)} %get-tuple-element.178.ids_ref, bf16[272,3072]{1,0:T(8,128)(2,1)S(1)} %pad_maximum_fusion.2.mixed_ref, bf16[272,3072]{1,0:T(8,128)(2,1)} %copy-done.17, bf16[1024,8192]{1,0:T(8,128)(2,1)} %own_ref.3, bf16[1024,1024]{1,0:T(8,128)(2,1)} %copy-done.13, ...), custom_call_target="tpu_custom_call" | custom-call | flops 1 | bytes 1 | tf_op jit(solution)/shard_map/output_product/pallas_call | solution.py:454
  492.4 9.9 %output_product.3 = (bf16[272,8192]{1,0:T(8,128)(2,1)}, bf16[272,4096]{1,0:T(8,128)(2,1)}) custom-call(s32[4]{0:T(128)S(1)} %get-tuple-element.178.ids_ref, bf16[272,1024]{1,0:T(8,128)(2,1)S(1)} %maximum_select_fusion.4.mixed_ref, bf16[272,1024]{1,0:T(8,128)(2,1)S(1)} %collective-permute-done.48.other_ref, bf16[1024,8192]{1,0:T(8,128)(2,1)} %own_ref.3, ...), custom_call_target="tpu_custom_call" | custom-call | flops 1 | bytes 1 | tf_op jit(solution)/shard_map/output_product/pallas_call | solution.py:454
  504.2 4.2 collective-permute-done.52
  508.3 3.8 fusion.4
  (207 shorter events, 93.0 us)
Async XLA Ops:
  6.5 196.4 %all-gather.3.cloned.1.call-start = ((), (), s32[]{:S(2)}) async-start(), calls=%async_computation | async-start | bytes 14155776 | tf_op jit(solution)/shard_map/all_gather | solution.py:584
  9.7 50.3 %collective-permute-start.2 = (bf16[1024,1024]{1,0:T(8,128)(2,1)}, bf16[1024,1024]{1,0:T(8,128)(2,1)}, u32[]{:S(2)}, u32[]{:S(2)}) collective-permute-start(bf16[1024,1024]{1,0:T(8,128)(2,1)} %constant_dynamic-slice_fusion.1), channel_id=1, source_target_pairs={{1,0},{2,3},{5,4},{6,7},{9,8},{10,11},{13,12},{14,15},{17,16},{18,... | collective-permute-start | bytes 6291464 | tf_op jit(solution)/shard_map/ppermute | solution.py:68
  12.3 50.3 %collective-permute-start.1 = (bf16[1024,1024]{1,0:T(8,128)(2,1)}, bf16[1024,1024]{1,0:T(8,128)(2,1)S(1)}, u32[]{:S(2)}, u32[]{:S(2)}) collective-permute-start(bf16[1024,1024]{1,0:T(8,128)(2,1)} %constant_dynamic-slice_fusion.1), channel_id=1, source_target_pairs={{1,2},{2,1},{5,6},{6,5},{9,10},{10,9},{13,14},{14,13},{17,18},{18,... | collective-permute-start | bytes 6291464 | tf_op jit(solution)/shard_map/ppermute | solution.py:68
  17.4 26.0 %collective-permute-start.3 = (f32[1,8]{1,0:T(1,128)S(1)}, f32[1,8]{1,0:T(1,128)S(1)}, u32[]{:S(2)}, u32[]{:S(2)}) collective-permute-start(f32[1,8]{1,0:T(1,128)S(1)} %copy-done.26), channel_id=1, source_target_pairs={{0,1},{3,2},{4,5},{7,6},{8,9},{11,10},{12,13},{15,14},{16,17},{19,... | collective-permute-start | bytes 104 | tf_op jit(solution)/shard_map/ppermute | solution.py:68
  23.1 36.8 %collective-permute-start = (bf16[1024,768]{1,0:T(8,128)(2,1)}, bf16[1024,768]{1,0:T(8,128)(2,1)}, u32[]{:S(2)}, u32[]{:S(2)}) collective-permute-start(bf16[1024,768]{1,0:T(8,128)(2,1)} %pad_maximum_fusion.3), channel_id=1, source_target_pairs={{0,1},{3,2},{4,5},{7,6},{8,9},{11,10},{12,13},{15,14},{16,17},{19,... | collective-permute-start | bytes 4718600 | tf_op jit(solution)/shard_map/ppermute | solution.py:68
  62.6 199.6 %all-gather.5.cloned.1.call-start = ((), (), s32[]{:S(2)}) async-start(), calls=%async_computation.1 | async-start | bytes 14155776 | tf_op jit(solution)/shard_map/all_gather | solution.py:597
  62.7 104.4 %collective-permute-start.5 = (bf16[288,8192]{1,0:T(8,128)(2,1)}, bf16[288,8192]{1,0:T(8,128)(2,1)}, u32[]{:S(2)}, u32[]{:S(2)}) collective-permute-start(bf16[288,8192]{1,0:T(8,128)(2,1)} %pad_maximum_fusion.refs_0_), channel_id=1, source_target_pairs={{1,2},{2,1},{5,6},{6,5},{9,10},{10,9},{13,14},{14,13},{17,18},{18,... | collective-permute-start | bytes 14155784 | tf_op jit(solution)/shard_map/ppermute | solution.py:68
  66.0 86.5 %collective-permute-start.4 = (bf16[144,8192]{1,0:T(8,128)(2,1)}, bf16[144,8192]{1,0:T(8,128)(2,1)}, u32[]{:S(2)}, u32[]{:S(2)}) collective-permute-start(bf16[144,8192]{1,0:T(8,128)(2,1)} %get-tuple-element.180), channel_id=1, source_target_pairs={{0,1},{3,2},{4,5},{7,6},{8,9},{11,10},{12,13},{15,14},{16,17},{19,... | collective-permute-start | bytes 7077896 | tf_op jit(solution)/shard_map/ppermute | solution.py:68
  69.2 83.4 %collective-permute-start.7 = (bf16[1024,1024]{1,0:T(8,128)(2,1)S(1)}, bf16[1024,1024]{1,0:T(8,128)(2,1)}, u32[]{:S(2)}, u32[]{:S(2)}) collective-permute-start(bf16[1024,1024]{1,0:T(8,128)(2,1)S(1)} %broadcast_select_fusion.refs_0_), channel_id=1, source_target_pairs={{0,16},{4,20},{8,0},{12,4},{24,8},{28,12},{16,24},{20,28},{1,17},{... | collective-permute-start | bytes 6291464 | tf_op jit(solution)/shard_map/ppermute | solution.py:106
  70.4 82.1 %collective-permute-start.6 = (bf16[1024,1024]{1,0:T(8,128)(2,1)S(1)}, bf16[1024,1024]{1,0:T(8,128)(2,1)}, u32[]{:S(2)}, u32[]{:S(2)}) collective-permute-start(bf16[1024,1024]{1,0:T(8,128)(2,1)S(1)} %broadcast_select_fusion.refs_0_), channel_id=1, source_target_pairs={{0,8},{4,12},{8,24},{12,28},{24,16},{28,20},{16,0},{20,4},{1,9},{5... | collective-permute-start | bytes 6291464 | tf_op jit(solution)/shard_map/ppermute | solution.py:106
  91.4 61.1 %collective-permute-start.9 = (bf16[1024,768]{1,0:T(8,128)(2,1)}, bf16[1024,768]{1,0:T(8,128)(2,1)}, u32[]{:S(2)}, u32[]{:S(2)}) collective-permute-start(bf16[1024,768]{1,0:T(8,128)(2,1)} %pad_maximum_fusion.4), channel_id=1, source_target_pairs={{0,1},{3,2},{4,5},{7,6},{8,9},{11,10},{12,13},{15,14},{16,17},{19,... | collective-permute-start | bytes 4718600 | tf_op jit(solution)/shard_map/ppermute | solution.py:68
  167.1 56.7 %collective-permute-start.14 = (bf16[144,8192]{1,0:T(8,128)(2,1)}, bf16[144,8192]{1,0:T(8,128)(2,1)}, u32[]{:S(2)}, u32[]{:S(2)}) collective-permute-start(bf16[144,8192]{1,0:T(8,128)(2,1)} %get-tuple-element.198), channel_id=1, source_target_pairs={{0,1},{3,2},{4,5},{7,6},{8,9},{11,10},{12,13},{15,14},{16,17},{19,... | collective-permute-start | bytes 7077896 | tf_op jit(solution)/shard_map/ppermute | solution.py:68
  168.4 55.4 %collective-permute-start.10 = (bf16[144,8192]{1,0:T(8,128)(2,1)}, bf16[144,8192]{1,0:T(8,128)(2,1)}, u32[]{:S(2)}, u32[]{:S(2)}) collective-permute-start(bf16[144,8192]{1,0:T(8,128)(2,1)} %collective-permute-done.4.refs_0_.refs_1_), channel_id=1, source_target_pairs={{1,2},{2,1},{5,6},{6,5},{9,10},{10,9},{13,14},{14,13},{17,18},{18,... | collective-permute-start | bytes 7077896 | tf_op jit(solution)/shard_map/ppermute | solution.py:68
  171.0 52.8 %collective-permute-start.11 = (bf16[1024,1024]{1,0:T(8,128)(2,1)}, bf16[1024,1024]{1,0:T(8,128)(2,1)}, u32[]{:S(2)}, u32[]{:S(2)}) collective-permute-start(bf16[1024,1024]{1,0:T(8,128)(2,1)} %copy-done.16), channel_id=1, source_target_pairs={{1,0},{2,3},{5,4},{6,7},{9,8},{10,11},{13,12},{14,15},{17,16},{18,... | collective-permute-start | bytes 6291464 | tf_op jit(solution)/shard_map/ppermute | solution.py:68
  181.9 40.6 %collective-permute-start.13 = (bf16[512,1024]{1,0:T(8,128)(2,1)}, bf16[512,1024]{1,0:T(8,128)(2,1)}, u32[]{:S(2)}, u32[]{:S(2)}) collective-permute-start(bf16[512,1024]{1,0:T(8,128)(2,1)} %slice.71), channel_id=1, source_target_pairs={{0,16},{4,20},{8,0},{12,4},{24,8},{28,12},{16,24},{20,28},{1,17},{... | collective-permute-start | bytes 3145736 | tf_op jit(solution)/shard_map/ppermute | solution.py:106
  183.2 40.6 %collective-permute-start.12 = (bf16[512,1024]{1,0:T(8,128)(2,1)S(1)}, bf16[512,1024]{1,0:T(8,128)(2,1)}, u32[]{:S(2)}, u32[]{:S(2)}) collective-permute-start(bf16[512,1024]{1,0:T(8,128)(2,1)S(1)} %slice.70), channel_id=1, source_target_pairs={{0,8},{4,12},{8,24},{12,28},{24,16},{28,20},{16,0},{20,4},{1,9},{5... | collective-permute-start | bytes 3145736 | tf_op jit(solution)/shard_map/ppermute | solution.py:106
  223.8 55.5 %collective-permute-start.16 = (bf16[144,8192]{1,0:T(8,128)(2,1)}, bf16[144,8192]{1,0:T(8,128)(2,1)}, u32[]{:S(2)}, u32[]{:S(2)}) collective-permute-start(bf16[144,8192]{1,0:T(8,128)(2,1)} %collective-permute-done.14.refs_1_.refs_2_), channel_id=1, source_target_pairs={{1,2},{2,1},{5,6},{6,5},{9,10},{10,9},{13,14},{14,13},{17,18},{18,... | collective-permute-start | bytes 7077896 | tf_op jit(solution)/shard_map/ppermute | solution.py:68
  225.9 53.3 %collective-permute-start.17 = (bf16[512,1024]{1,0:T(8,128)(2,1)}, bf16[512,1024]{1,0:T(8,128)(2,1)}, u32[]{:S(2)}, u32[]{:S(2)}) collective-permute-start(bf16[512,1024]{1,0:T(8,128)(2,1)} %get-tuple-element.207), channel_id=1, source_target_pairs={{0,1},{3,2},{4,5},{7,6},{8,9},{11,10},{12,13},{15,14},{16,17},{19,... | collective-permute-start | bytes 3145736 | tf_op jit(solution)/shard_map/ppermute | solution.py:68
  227.2 52.1 %collective-permute-start.18 = (bf16[512,1024]{1,0:T(8,128)(2,1)}, bf16[512,1024]{1,0:T(8,128)(2,1)}, u32[]{:S(2)}, u32[]{:S(2)}) collective-permute-start(bf16[512,1024]{1,0:T(8,128)(2,1)} %get-tuple-element.208), channel_id=1, source_target_pairs={{0,1},{3,2},{4,5},{7,6},{8,9},{11,10},{12,13},{15,14},{16,17},{19,... | collective-permute-start | bytes 3145736 | tf_op jit(solution)/shard_map/ppermute | solution.py:68
  229.0 28.6 %collective-permute-start.19 = (f32[4,16]{1,0:T(4,128)S(1)}, f32[4,16]{1,0:T(4,128)S(1)}, u32[]{:S(2)}, u32[]{:S(2)}) collective-permute-start(f32[4,16]{1,0:T(4,128)S(1)} %pad_maximum_fusion.7), channel_id=1, source_target_pairs={{0,16},{4,20},{8,24},{12,28},{16,0},{20,4},{24,8},{28,12},{1,17},{... | collective-permute-start | bytes 776 | tf_op jit(solution)/shard_map/ppermute | solution.py:125
  283.6 56.2 %collective-permute-start.25 = (bf16[1024,1024]{1,0:T(8,128)(2,1)}, bf16[1024,1024]{1,0:T(8,128)(2,1)}, u32[]{:S(2)}, u32[]{:S(2)}) collective-permute-start(bf16[1024,1024]{1,0:T(8,128)(2,1)} %maximum_select_fusion.refs_1_), channel_id=1, source_target_pairs={{0,16},{4,20},{8,0},{12,4},{24,8},{28,12},{16,24},{20,28},{1,17},{... | collective-permute-start | bytes 6291464 | tf_op jit(solution)/shard_map/ppermute | solution.py:106
  284.3 55.5 %collective-permute-start.24 = (bf16[1024,1024]{1,0:T(8,128)(2,1)}, bf16[1024,1024]{1,0:T(8,128)(2,1)}, u32[]{:S(2)}, u32[]{:S(2)}) collective-permute-start(bf16[1024,1024]{1,0:T(8,128)(2,1)} %maximum_select_fusion.refs_1_), channel_id=1, source_target_pairs={{0,8},{4,12},{8,24},{12,28},{24,16},{28,20},{16,0},{20,4},{1,9},{5... | collective-permute-start | bytes 6291464 | tf_op jit(solution)/shard_map/ppermute | solution.py:106
  285.1 41.6 %collective-permute-start.20 = (bf16[512,1024]{1,0:T(8,128)(2,1)}, bf16[512,1024]{1,0:T(8,128)(2,1)}, u32[]{:S(2)}, u32[]{:S(2)}) collective-permute-start(bf16[512,1024]{1,0:T(8,128)(2,1)} %collective-permute-done.17), channel_id=1, source_target_pairs={{1,2},{2,1},{5,6},{6,5},{9,10},{10,9},{13,14},{14,13},{17,18},{18,... | collective-permute-start | bytes 3145736 | tf_op jit(solution)/shard_map/ppermute | solution.py:68
  311.3 11.8 %collective-permute-start.22 = (bf16[8,144,128]{2,1,0:T(8,128)(2,1)S(1)}, bf16[8,144,128]{2,1,0:T(8,128)(2,1)S(1)}, u32[]{:S(2)}, u32[]{:S(2)}) collective-permute-start(bf16[8,144,128]{2,1,0:T(8,128)(2,1)S(1)} %fusion.20), channel_id=1, source_target_pairs={{0,4},{4,0},{8,12},{12,8},{16,20},{20,16},{24,28},{28,24},{1,5},{5... | collective-permute-start | bytes 884744 | tf_op jit(solution)/shard_map/ppermute | solution.py:361
  323.3 15.4 %collective-permute-start.23 = (bf16[8,144,128]{2,1,0:T(8,128)(2,1)S(1)}, bf16[8,144,128]{2,1,0:T(8,128)(2,1)S(1)}, u32[]{:S(2)}, u32[]{:S(2)}) collective-permute-start(bf16[8,144,128]{2,1,0:T(8,128)(2,1)S(1)} %fusion.25), channel_id=1, source_target_pairs={{0,8},{4,12},{8,0},{12,4},{16,24},{20,28},{24,16},{28,20},{1,9},{5... | collective-permute-start | bytes 884744 | tf_op jit(solution)/shard_map/ppermute | solution.py:361
  324.5 27.3 %collective-permute-start.21 = (bf16[512,1024]{1,0:T(8,128)(2,1)}, bf16[512,1024]{1,0:T(8,128)(2,1)S(1)}, u32[]{:S(2)}, u32[]{:S(2)}) collective-permute-start(bf16[512,1024]{1,0:T(8,128)(2,1)} %collective-permute-done.18), channel_id=1, source_target_pairs={{1,2},{2,1},{5,6},{6,5},{9,10},{10,9},{13,14},{14,13},{17,18},{18,... | collective-permute-start | bytes 3145736 | tf_op jit(solution)/shard_map/ppermute | solution.py:68
  326.7 25.2 %collective-permute-start.27 = (bf16[512,1024]{1,0:T(8,128)(2,1)}, bf16[512,1024]{1,0:T(8,128)(2,1)S(1)}, u32[]{:S(2)}, u32[]{:S(2)}) collective-permute-start(bf16[512,1024]{1,0:T(8,128)(2,1)} %collective-permute-done.20), channel_id=1, source_target_pairs={{1,0},{2,3},{5,4},{6,7},{9,8},{10,11},{13,12},{14,15},{17,16},{18,... | collective-permute-start | bytes 3145736 | tf_op jit(solution)/shard_map/ppermute | solution.py:68
  339.1 12.3 %collective-permute-start.26 = (bf16[8,144,128]{2,1,0:T(8,128)(2,1)S(1)}, bf16[8,144,128]{2,1,0:T(8,128)(2,1)S(1)}, u32[]{:S(2)}, u32[]{:S(2)}) collective-permute-start(bf16[8,144,128]{2,1,0:T(8,128)(2,1)S(1)} %fusion.10), channel_id=1, source_target_pairs={{0,16},{4,20},{8,24},{12,28},{16,0},{20,4},{24,8},{28,12},{1,17},{... | collective-permute-start | bytes 884744 | tf_op jit(solution)/shard_map/ppermute | solution.py:361
  344.4 25.5 %collective-permute-start.30 = (bf16[512,1024]{1,0:T(8,128)(2,1)}, bf16[512,1024]{1,0:T(8,128)(2,1)S(1)}, u32[]{:S(2)}, u32[]{:S(2)}) collective-permute-start(bf16[512,1024]{1,0:T(8,128)(2,1)} %slice.74), channel_id=1, source_target_pairs={{0,8},{4,12},{8,24},{12,28},{24,16},{28,20},{16,0},{20,4},{1,9},{5... | collective-permute-start | bytes 3145736 | tf_op jit(solution)/shard_map/ppermute | solution.py:106
  345.7 24.1 %collective-permute-start.31 = (bf16[512,1024]{1,0:T(8,128)(2,1)}, bf16[512,1024]{1,0:T(8,128)(2,1)S(1)}, u32[]{:S(2)}, u32[]{:S(2)}) collective-permute-start(bf16[512,1024]{1,0:T(8,128)(2,1)} %slice.75), channel_id=1, source_target_pairs={{0,16},{4,20},{8,0},{12,4},{24,8},{28,12},{16,24},{20,28},{1,17},{... | collective-permute-start | bytes 3145736 | tf_op jit(solution)/shard_map/ppermute | solution.py:106
  360.8 16.1 %collective-permute-start.29 = (bf16[8,144,128]{2,1,0:T(8,128)(2,1)S(1)}, bf16[8,144,128]{2,1,0:T(8,128)(2,1)S(1)}, u32[]{:S(2)}, u32[]{:S(2)}) collective-permute-start(bf16[8,144,128]{2,1,0:T(8,128)(2,1)S(1)} %fusion.24), channel_id=1, source_target_pairs={{0,8},{4,12},{8,0},{12,4},{16,24},{20,28},{24,16},{28,20},{1,9},{5... | collective-permute-start | bytes 884744 | tf_op jit(solution)/shard_map/ppermute | solution.py:361
  362.2 35.4 %collective-permute-start.35 = (bf16[512,1024]{1,0:T(8,128)(2,1)S(1)}, bf16[512,1024]{1,0:T(8,128)(2,1)}, u32[]{:S(2)}, u32[]{:S(2)}) collective-permute-start(bf16[512,1024]{1,0:T(8,128)(2,1)S(1)} %collective-permute-done.21), channel_id=1, source_target_pairs={{1,0},{2,3},{5,4},{6,7},{9,8},{10,11},{13,12},{14,15},{17,16},{18,... | collective-permute-start | bytes 3145736 | tf_op jit(solution)/shard_map/ppermute | solution.py:68
  377.3 19.9 %collective-permute-start.32 = (bf16[8,144,128]{2,1,0:T(8,128)(2,1)S(1)}, bf16[8,144,128]{2,1,0:T(8,128)(2,1)S(1)}, u32[]{:S(2)}, u32[]{:S(2)}) collective-permute-start(bf16[8,144,128]{2,1,0:T(8,128)(2,1)S(1)} %fusion.16), channel_id=1, source_target_pairs={{0,16},{4,20},{8,24},{12,28},{16,0},{20,4},{24,8},{28,12},{1,17},{... | collective-permute-start | bytes 884744 | tf_op jit(solution)/shard_map/ppermute | solution.py:361
  377.4 12.7 %collective-permute-start.33 = (bf16[272,512]{1,0:T(8,128)(2,1)S(1)}, bf16[272,512]{1,0:T(8,128)(2,1)S(1)}, u32[]{:S(2)}, u32[]{:S(2)}) collective-permute-start(bf16[272,512]{1,0:T(8,128)(2,1)S(1)} %get-tuple-element.294), channel_id=1, source_target_pairs={{1,2},{2,1},{5,6},{6,5},{9,10},{10,9},{13,14},{14,13},{17,18},{18,... | collective-permute-start | bytes 835592 | tf_op jit(solution)/shard_map/ppermute | solution.py:68
  380.2 9.9 %collective-permute-start.34 = (bf16[272,512]{1,0:T(8,128)(2,1)S(1)}, bf16[272,512]{1,0:T(8,128)(2,1)S(1)}, u32[]{:S(2)}, u32[]{:S(2)}) collective-permute-start(bf16[272,512]{1,0:T(8,128)(2,1)S(1)} %get-tuple-element.295), channel_id=1, source_target_pairs={{1,3},{2,0},{5,7},{6,4},{9,11},{10,8},{13,15},{14,12},{17,19},{18,... | collective-permute-start | bytes 835592 | tf_op jit(solution)/shard_map/ppermute | solution.py:68
  381.5 16.5 %collective-permute-start.36 = (bf16[272,512]{1,0:T(8,128)(2,1)S(1)}, bf16[272,512]{1,0:T(8,128)(2,1)S(1)}, u32[]{:S(2)}, u32[]{:S(2)}) collective-permute-start(bf16[272,512]{1,0:T(8,128)(2,1)S(1)} %get-tuple-element.311), channel_id=1, source_target_pairs={{1,0},{2,3},{5,4},{6,7},{9,8},{10,11},{13,12},{14,15},{17,16},{18,... | collective-permute-start | bytes 835592 | tf_op jit(solution)/shard_map/ppermute | solution.py:68
  400.5 61.2 %collective-permute-start.47 = (bf16[1024,1024]{1,0:T(8,128)(2,1)S(1)}, bf16[1024,1024]{1,0:T(8,128)(2,1)S(1)}, u32[]{:S(2)}, u32[]{:S(2)}) collective-permute-start(bf16[1024,1024]{1,0:T(8,128)(2,1)S(1)} %pad_maximum_fusion.1.refs_0_), channel_id=1, source_target_pairs={{0,16},{4,20},{8,0},{12,4},{24,8},{28,12},{16,24},{20,28},{1,17},{... | collective-permute-start | bytes 6291464 | tf_op jit(solution)/shard_map/ppermute | solution.py:106
  401.9 59.9 %collective-permute-start.46 = (bf16[1024,1024]{1,0:T(8,128)(2,1)S(1)}, bf16[1024,1024]{1,0:T(8,128)(2,1)S(1)}, u32[]{:S(2)}, u32[]{:S(2)}) collective-permute-start(bf16[1024,1024]{1,0:T(8,128)(2,1)S(1)} %pad_maximum_fusion.1.refs_0_), channel_id=1, source_target_pairs={{0,8},{4,12},{8,24},{12,28},{24,16},{28,20},{16,0},{20,4},{1,9},{5... | collective-permute-start | bytes 6291464 | tf_op jit(solution)/shard_map/ppermute | solution.py:106
  402.1 23.2 %collective-permute-start.38 = (bf16[272,512]{1,0:T(8,128)(2,1)S(1)}, bf16[272,512]{1,0:T(8,128)(2,1)S(1)}, u32[]{:S(2)}, u32[]{:S(2)}) collective-permute-start(bf16[272,512]{1,0:T(8,128)(2,1)S(1)} %get-tuple-element.314), channel_id=1, source_target_pairs={{1,0},{2,3},{5,4},{6,7},{9,8},{10,11},{13,12},{14,15},{17,16},{18,... | collective-permute-start | bytes 835592 | tf_op jit(solution)/shard_map/ppermute | solution.py:68
  406.2 20.5 %collective-permute-start.39 = (bf16[272,512]{1,0:T(8,128)(2,1)S(1)}, bf16[272,512]{1,0:T(8,128)(2,1)}, u32[]{:S(2)}, u32[]{:S(2)}) collective-permute-start(bf16[272,512]{1,0:T(8,128)(2,1)S(1)} %get-tuple-element.315), channel_id=1, source_target_pairs={{1,2},{2,1},{5,6},{6,5},{9,10},{10,9},{13,14},{14,13},{17,18},{18,... | collective-permute-start | bytes 835592 | tf_op jit(solution)/shard_map/ppermute | solution.py:68
  409.9 18.3 %collective-permute-start.40 = (bf16[272,512]{1,0:T(8,128)(2,1)S(1)}, bf16[272,512]{1,0:T(8,128)(2,1)}, u32[]{:S(2)}, u32[]{:S(2)}) collective-permute-start(bf16[272,512]{1,0:T(8,128)(2,1)S(1)} %get-tuple-element.316), channel_id=1, source_target_pairs={{1,3},{2,0},{5,7},{6,4},{9,11},{10,8},{13,15},{14,12},{17,19},{18,... | collective-permute-start | bytes 835592 | tf_op jit(solution)/shard_map/ppermute | solution.py:68
  425.2 17.5 %collective-permute-start.37 = (bf16[272,512]{1,0:T(8,128)(2,1)S(1)}, bf16[272,512]{1,0:T(8,128)(2,1)S(1)}, u32[]{:S(2)}, u32[]{:S(2)}) collective-permute-start(bf16[272,512]{1,0:T(8,128)(2,1)S(1)} %get-tuple-element.313), channel_id=1, source_target_pairs={{1,0},{2,3},{5,4},{6,7},{9,8},{10,11},{13,12},{14,15},{17,16},{18,... | collective-permute-start | bytes 835592 | tf_op jit(solution)/shard_map/ppermute | solution.py:68
  426.7 18.0 %collective-permute-start.42 = (bf16[272,512]{1,0:T(8,128)(2,1)S(1)}, bf16[272,512]{1,0:T(8,128)(2,1)S(1)}, u32[]{:S(2)}, u32[]{:S(2)}) collective-permute-start(bf16[272,512]{1,0:T(8,128)(2,1)S(1)} %get-tuple-element.329), channel_id=1, source_target_pairs={{1,3},{2,0},{5,7},{6,4},{9,11},{10,8},{13,15},{14,12},{17,19},{18,... | collective-permute-start | bytes 835592 | tf_op jit(solution)/shard_map/ppermute | solution.py:68
  442.8 9.1 %collective-permute-start.44 = (bf16[272,512]{1,0:T(8,128)(2,1)S(1)}, bf16[272,512]{1,0:T(8,128)(2,1)S(1)}, u32[]{:S(2)}, u32[]{:S(2)}) collective-permute-start(bf16[272,512]{1,0:T(8,128)(2,1)S(1)} %get-tuple-element.331), channel_id=1, source_target_pairs={{1,2},{2,1},{5,6},{6,5},{9,10},{10,9},{13,14},{14,13},{17,18},{18,... | collective-permute-start | bytes 835592 | tf_op jit(solution)/shard_map/ppermute | solution.py:68
  446.2 15.2 %collective-permute-start.45 = (bf16[272,512]{1,0:T(8,128)(2,1)S(1)}, bf16[272,512]{1,0:T(8,128)(2,1)S(1)}, u32[]{:S(2)}, u32[]{:S(2)}) collective-permute-start(bf16[272,512]{1,0:T(8,128)(2,1)S(1)} %get-tuple-element.332), channel_id=1, source_target_pairs={{1,2},{2,1},{5,6},{6,5},{9,10},{10,9},{13,14},{14,13},{17,18},{18,... | collective-permute-start | bytes 835592 | tf_op jit(solution)/shard_map/ppermute | solution.py:68
  467.2 24.5 %collective-permute-start.50 = (bf16[512,1024]{1,0:T(8,128)(2,1)}, bf16[512,1024]{1,0:T(8,128)(2,1)S(1)}, u32[]{:S(2)}, u32[]{:S(2)}) collective-permute-start(bf16[512,1024]{1,0:T(8,128)(2,1)} %slice.81), channel_id=1, source_target_pairs={{0,16},{4,20},{8,0},{12,4},{24,8},{28,12},{16,24},{20,28},{1,17},{... | collective-permute-start | bytes 3145736 | tf_op jit(solution)/shard_map/ppermute | solution.py:106
  468.6 23.8 %collective-permute-start.49 = (bf16[512,1024]{1,0:T(8,128)(2,1)S(1)}, bf16[512,1024]{1,0:T(8,128)(2,1)S(1)}, u32[]{:S(2)}, u32[]{:S(2)}) collective-permute-start(bf16[512,1024]{1,0:T(8,128)(2,1)S(1)} %slice.80), channel_id=1, source_target_pairs={{0,8},{4,12},{8,24},{12,28},{24,16},{28,20},{16,0},{20,4},{1,9},{5... | collective-permute-start | bytes 3145736 | tf_op jit(solution)/shard_map/ppermute | solution.py:106
  468.7 23.7 %collective-permute-start.48 = (bf16[272,1024]{1,0:T(8,128)(2,1)S(1)}, bf16[272,1024]{1,0:T(8,128)(2,1)S(1)}, u32[]{:S(2)}, u32[]{:S(2)}) collective-permute-start(bf16[272,1024]{1,0:T(8,128)(2,1)S(1)} %maximum_select_fusion.4.mixed_ref), channel_id=1, source_target_pairs={{0,4},{4,0},{8,12},{12,8},{16,20},{20,16},{24,28},{28,24},{1,5},{5... | collective-permute-start | bytes 1671176 | tf_op jit(solution)/shard_map/ppermute | solution.py:77
  (37 other events, 321.4 us)
Sparse Core Ops, SparseCore 0:
  62.8 108.3 all-gather.2
  173.0 89.1 all-gather.4
